TPU v7x, 32 devices: a whole 2x2x4 slice. The times are simulated.
32 devices in a mesh: dp: 2 (over core), seq: 16 (over z, y, x).
Axes of the slice: x: 2, y: 2, z: 4, core: 2. Of those that a mesh axis runs over, the one named last changes fastest.
Arguments:
- tokens: bfloat16 [4, 8192, 768], P('dp', 'seq'), may hold values from -6 to 6
- segments: int32 [4, 8192], P('dp'), may hold values from 0 to 15, as said below
- cotangent: bfloat16 [4, 8192, 768], P('dp', 'seq'), may hold values from -6 to 6
- ln1_gain: bfloat16 [768], P(('dp', 'seq')), may hold values from 0.5 to 1.5
- ln1_bias: bfloat16 [768], P(('dp', 'seq')), may hold values from -3 to 3
- w_qkv: bfloat16 [768, 2304], P(('dp', 'seq')), may hold values from -0.21875 to 0.21875
- pool_taps: bfloat16 [5, 1536], P(None, ('dp', 'seq')), may hold values from -2.6875 to 2.6875
- w_out: bfloat16 [768, 768], P(('dp', 'seq')), may hold values from -1.75 to 1.75
- ln2_gain: bfloat16 [768], P(('dp', 'seq')), may hold values from 0.5 to 1.5
- ln2_bias: bfloat16 [768], P(('dp', 'seq')), may hold values from -3 to 3
- w_up: bfloat16 [768, 3072], P(('dp', 'seq')), may hold values from -0.21875 to 0.21875
- w_down: bfloat16 [3072, 768], P(None, ('dp', 'seq')), may hold values from -0.109375 to 0.109375
Outputs:
- output: bfloat16 [4, 8192, 768], P('dp', 'seq')
- input_grad: float32 [4, 8192, 768], P('dp', 'seq')
- grad_ln1_gain: float32 [768], P(('dp', 'seq'))
- grad_ln1_bias: float32 [768], P(('dp', 'seq'))
- grad_w_qkv: float32 [768, 2304], P(('dp', 'seq'))
- grad_pool_taps: float32 [5, 1536], P(None, ('dp', 'seq'))
- grad_w_out: float32 [768, 768], P(('dp', 'seq'))
- grad_ln2_gain: float32 [768], P(('dp', 'seq'))
- grad_ln2_bias: float32 [768], P(('dp', 'seq'))
- grad_w_up: float32 [768, 3072], P(('dp', 'seq'))
- grad_w_down: float32 [3072, 768], P(None, ('dp', 'seq'))
Inputs may be any that keep to these rules, and one draw needn't show every extreme that they name: `segments`: within a row the numbers start at 0 and rise by one at the start of each document; in each aligned group of 2 rows one row holds a single document and every other row holds exactly max(16, 2) documents.
All inputs are finite; a program needn't handle non-finite values.
Results may differ from a plain program's by a relative error of at most 0.013.
Values may be sent and summed in bfloat16 or wider, within the bound.
A program may use at most 256 MiB of HBM per device.

v0:
```python
import jax
import jax.numpy as jnp
from jax import lax
from jax.sharding import PartitionSpec as P

HEADS = 12
HEAD = 64
LOCAL_HALF = 64
POOL_REACH = 256


def with_halo(x, sides, width):
    for axis, dim in sides:
        size, length = (lax.axis_size(axis), x.shape[dim])
        up = [(i, (i + 1) % size) for i in range(size - 1)]
        down = [(j, i) for i, j in up]
        last = lax.slice_in_dim(x, length - width, length, axis=dim)
        first = lax.slice_in_dim(x, 0, width, axis=dim)
        before = lax.ppermute(last, axis, up)
        after = lax.ppermute(first, axis, down)
        x = jnp.concatenate([before, x, after], axis=dim)
    return x


def layer_norm(inputs, norm_gain, norm_bias):
    middle = jnp.mean(inputs, axis=-1, keepdims=True)
    centred = inputs - middle
    spread = jnp.mean(centred * centred, axis=-1, keepdims=True)
    return centred * lax.rsqrt(spread + 1e-05) * norm_gain + norm_bias


def pool_local(extended, taps_in, seg_window):
    block_rows = extended.shape[0] - 2 * LOCAL_HALF
    anchors = seg_window[POOL_REACH : POOL_REACH + block_rows : 4]
    pooled = jnp.zeros((block_rows // 4, extended.shape[1]), jnp.float32)
    for offset in range(5):
        start_row = LOCAL_HALF - 2 + offset
        picked = extended[start_row : start_row + block_rows : 4]
        seg_start = POOL_REACH - 2 + offset
        same_doc = (seg_window[seg_start : seg_start + block_rows : 4] == anchors).astype(
            jnp.float32
        )
        pooled = pooled + taps_in[offset] * picked * same_doc[:, None]
    return pooled


def window_masks(seg_window, block_rows):
    seg_query = seg_window[POOL_REACH : POOL_REACH + block_rows]
    seg_key = seg_window[POOL_REACH - LOCAL_HALF : POOL_REACH + block_rows + LOCAL_HALF]
    seg_pool = seg_window[0 : block_rows + 2 * POOL_REACH : 4]
    q_index = jnp.arange(block_rows, dtype=jnp.int32)
    k_index = jnp.arange(seg_key.shape[0], dtype=jnp.int32)
    p_index = jnp.arange(seg_pool.shape[0], dtype=jnp.int32)
    near_mask = (jnp.abs(q_index[:, None] - k_index[None, :] + LOCAL_HALF) <= LOCAL_HALF) & (
        seg_query[:, None] == seg_key[None, :]
    )
    far_mask = (jnp.abs(4 * p_index[None, :] - POOL_REACH - q_index[:, None]) <= POOL_REACH) & (
        seg_query[:, None] == seg_pool[None, :]
    )
    return (near_mask, far_mask)


def scores_of(queries, near_keys, far_keys, near_mask, far_mask):
    score_scale = HEAD ** (-0.5)
    near_scores = (
        jnp.einsum("qhd,khd->hqk", queries, near_keys, preferred_element_type=jnp.float32)
        * score_scale
    )
    far_scores = (
        jnp.einsum("qhd,khd->hqk", queries, far_keys, preferred_element_type=jnp.float32)
        * score_scale
    )
    return (
        jnp.where(near_mask[None], near_scores, -1e30),
        jnp.where(far_mask[None], far_scores, -1e30),
    )


def normalise(near_scores, far_scores, near_mask, far_mask, row_max, row_total):
    near_prob = jnp.where(near_mask[None], jnp.exp(near_scores - row_max), 0.0) / row_total
    far_prob = jnp.where(far_mask[None], jnp.exp(far_scores - row_max), 0.0) / row_total
    return (near_prob, far_prob)


def add_rims(middle_part, rim_values, rim_width):
    extra = middle_part.shape[0] - rim_width
    return (
        middle_part
        + jnp.pad(rim_values[:rim_width], ((0, extra), (0, 0)))
        + jnp.pad(rim_values[-rim_width:], ((extra, 0), (0, 0)))
    )


def shards(
    tokens,
    segments,
    cotangent,
    ln1_gain,
    ln1_bias,
    w_qkv,
    pool_taps,
    w_out,
    ln2_gain,
    ln2_bias,
    w_up,
    w_down,
):
    block_rows = tokens.shape[1]
    model_width = tokens.shape[2]
    pool_half = POOL_REACH // 4
    score_scale = HEAD ** (-0.5)
    offset_tokens = lax.axis_index("seq") * block_rows
    outputs = []
    input_grads = []
    summed = None
    for micro_step in range(tokens.shape[0]):
        gathered = (
            lax.all_gather(ln1_gain, ("dp", "seq"), axis=0, tiled=True),
            lax.all_gather(ln1_bias, ("dp", "seq"), axis=0, tiled=True),
            lax.all_gather(w_qkv, ("dp", "seq"), axis=0, tiled=True),
            lax.all_gather(pool_taps, ("dp", "seq"), axis=1, tiled=True),
            lax.all_gather(w_out, ("dp", "seq"), axis=0, tiled=True),
            lax.all_gather(ln2_gain, ("dp", "seq"), axis=0, tiled=True),
            lax.all_gather(ln2_bias, ("dp", "seq"), axis=0, tiled=True),
            lax.all_gather(w_up, ("dp", "seq"), axis=0, tiled=True),
            lax.all_gather(w_down, ("dp", "seq"), axis=1, tiled=True),
        )
        gain_one, bias_one, proj_qkv, taps, proj_out, gain_two, bias_two, proj_up, proj_down = (
            gathered
        )
        seg_row = segments[micro_step]
        seg_padded = jnp.pad(seg_row, (POOL_REACH, POOL_REACH), constant_values=-1)
        seg_window = lax.dynamic_slice_in_dim(
            seg_padded, offset_tokens, block_rows + 2 * POOL_REACH, 0
        )
        near_mask, far_mask = window_masks(seg_window, block_rows)
        inputs = tokens[micro_step].astype(jnp.float32)
        gain_float = gain_one.astype(jnp.float32)
        bias_float = bias_one.astype(jnp.float32)
        gain_second = gain_two.astype(jnp.float32)
        bias_second = bias_two.astype(jnp.float32)
        normed = layer_norm(inputs, gain_float, bias_float).astype(jnp.bfloat16)
        projected = jnp.dot(normed, proj_qkv, preferred_element_type=jnp.float32).astype(
            jnp.bfloat16
        )
        queries = projected[:, :model_width].reshape(block_rows, HEADS, HEAD)
        key_value = projected[:, model_width:]
        extended = with_halo(key_value, (("seq", 0),), LOCAL_HALF)
        ext_float = extended.astype(jnp.float32)
        taps_float = taps.astype(jnp.float32)
        pooled = pool_local(ext_float, taps_float, seg_window).astype(jnp.bfloat16)
        pool_ext = with_halo(pooled, (("seq", 0),), pool_half)
        near_keys = extended[:, :model_width].reshape(-1, HEADS, HEAD)
        near_values = extended[:, model_width:].reshape(-1, HEADS, HEAD)
        far_keys = pool_ext[:, :model_width].reshape(-1, HEADS, HEAD)
        far_values = pool_ext[:, model_width:].reshape(-1, HEADS, HEAD)
        near_scores, far_scores = scores_of(queries, near_keys, far_keys, near_mask, far_mask)
        row_max = jnp.maximum(
            jnp.max(near_scores, axis=2, keepdims=True), jnp.max(far_scores, axis=2, keepdims=True)
        )
        near_exp = jnp.where(near_mask[None], jnp.exp(near_scores - row_max), 0.0)
        far_exp = jnp.where(far_mask[None], jnp.exp(far_scores - row_max), 0.0)
        row_total = jnp.sum(near_exp, axis=2, keepdims=True) + jnp.sum(
            far_exp, axis=2, keepdims=True
        )
        near_low = (near_exp / row_total).astype(jnp.bfloat16)
        far_low = (far_exp / row_total).astype(jnp.bfloat16)
        mixed_sum = jnp.einsum(
            "hqk,khd->qhd", near_low, near_values, preferred_element_type=jnp.float32
        ) + jnp.einsum("hqk,khd->qhd", far_low, far_values, preferred_element_type=jnp.float32)
        attended = mixed_sum.reshape(block_rows, model_width).astype(jnp.bfloat16)
        branch = jnp.dot(attended, proj_out, preferred_element_type=jnp.float32)
        middle = inputs + branch
        normed_two = layer_norm(middle, gain_second, bias_second).astype(jnp.bfloat16)
        upward = jnp.dot(normed_two, proj_up, preferred_element_type=jnp.float32)
        activated = jax.nn.gelu(upward).astype(jnp.bfloat16)
        result = middle + jnp.dot(activated, proj_down, preferred_element_type=jnp.float32)
        outputs.append(result.astype(jnp.bfloat16))
        regathered = (
            lax.all_gather(ln1_gain, ("dp", "seq"), axis=0, tiled=True),
            lax.all_gather(ln1_bias, ("dp", "seq"), axis=0, tiled=True),
            lax.all_gather(w_qkv, ("dp", "seq"), axis=0, tiled=True),
            lax.all_gather(pool_taps, ("dp", "seq"), axis=1, tiled=True),
            lax.all_gather(w_out, ("dp", "seq"), axis=0, tiled=True),
            lax.all_gather(ln2_gain, ("dp", "seq"), axis=0, tiled=True),
            lax.all_gather(ln2_bias, ("dp", "seq"), axis=0, tiled=True),
            lax.all_gather(w_up, ("dp", "seq"), axis=0, tiled=True),
            lax.all_gather(w_down, ("dp", "seq"), axis=1, tiled=True),
        )
        back_qkv = regathered[2]
        back_out = regathered[4]
        back_up = regathered[7]
        back_down = regathered[8]
        grad_out = cotangent[micro_step]
        grad_act = jnp.dot(grad_out, back_down.T, preferred_element_type=jnp.float32)
        grad_down = jnp.dot(activated.T, grad_out, preferred_element_type=jnp.float32)
        gelu_value, gelu_back = jax.vjp(jax.nn.gelu, upward)
        grad_upin = gelu_back(grad_act)[0].astype(jnp.bfloat16)
        grad_upw = jnp.dot(normed_two.T, grad_upin, preferred_element_type=jnp.float32)
        grad_normed_two = jnp.dot(grad_upin, back_up.T, preferred_element_type=jnp.float32)
        norm_value_two, norm_back_two = jax.vjp(layer_norm, middle, gain_second, bias_second)
        grad_mid_part, grad_gain_two, grad_bias_two = norm_back_two(grad_normed_two)
        grad_middle = grad_out.astype(jnp.float32) + grad_mid_part
        grad_branch = grad_middle.astype(jnp.bfloat16)
        grad_outw = jnp.dot(attended.T, grad_branch, preferred_element_type=jnp.float32)
        grad_mixed = (
            jnp.dot(grad_branch, back_out.T, preferred_element_type=jnp.float32)
            .astype(jnp.bfloat16)
            .reshape(block_rows, HEADS, HEAD)
        )
        near_scores, far_scores = scores_of(queries, near_keys, far_keys, near_mask, far_mask)
        near_prob, far_prob = normalise(
            near_scores, far_scores, near_mask, far_mask, row_max, row_total
        )
        near_low = near_prob.astype(jnp.bfloat16)
        far_low = far_prob.astype(jnp.bfloat16)
        grad_near_values = jnp.einsum(
            "hqk,qhd->khd", near_low, grad_mixed, preferred_element_type=jnp.float32
        )
        grad_far_values = jnp.einsum(
            "hqk,qhd->khd", far_low, grad_mixed, preferred_element_type=jnp.float32
        )
        grad_near_prob = jnp.einsum(
            "qhd,khd->hqk", grad_mixed, near_values, preferred_element_type=jnp.float32
        )
        grad_far_prob = jnp.einsum(
            "qhd,khd->hqk", grad_mixed, far_values, preferred_element_type=jnp.float32
        )
        row_delta = jnp.sum(near_prob * grad_near_prob, axis=2, keepdims=True) + jnp.sum(
            far_prob * grad_far_prob, axis=2, keepdims=True
        )
        grad_near_scores = (near_prob * (grad_near_prob - row_delta)).astype(jnp.bfloat16)
        grad_far_scores = (far_prob * (grad_far_prob - row_delta)).astype(jnp.bfloat16)
        grad_queries = (
            jnp.einsum(
                "hqk,khd->qhd", grad_near_scores, near_keys, preferred_element_type=jnp.float32
            )
            + jnp.einsum(
                "hqk,khd->qhd", grad_far_scores, far_keys, preferred_element_type=jnp.float32
            )
        ) * score_scale
        grad_near_keys = (
            jnp.einsum(
                "hqk,qhd->khd", grad_near_scores, queries, preferred_element_type=jnp.float32
            )
            * score_scale
        )
        grad_far_keys = (
            jnp.einsum("hqk,qhd->khd", grad_far_scores, queries, preferred_element_type=jnp.float32)
            * score_scale
        )
        grad_extended = jnp.concatenate(
            [grad_near_keys.reshape(-1, model_width), grad_near_values.reshape(-1, model_width)],
            axis=1,
        )
        grad_pool_ext = jnp.concatenate(
            [grad_far_keys.reshape(-1, model_width), grad_far_values.reshape(-1, model_width)],
            axis=1,
        )
        pool_edges = jnp.concatenate(
            [grad_pool_ext[:pool_half], grad_pool_ext[-pool_half:]], axis=0
        )
        pool_returned = with_halo(pool_edges.astype(jnp.bfloat16), (("seq", 0),), pool_half).astype(
            pool_edges.dtype
        )
        grad_pooled = add_rims(grad_pool_ext[pool_half:-pool_half], pool_returned, pool_half)
        pool_value, pool_back = jax.vjp(
            lambda ext_in, taps_part: pool_local(ext_in, taps_part, seg_window),
            ext_float,
            taps_float,
        )
        grad_ext_pool, grad_taps = pool_back(grad_pooled)
        grad_extended = grad_extended + grad_ext_pool
        token_edges = jnp.concatenate(
            [grad_extended[:LOCAL_HALF], grad_extended[-LOCAL_HALF:]], axis=0
        )
        token_returned = with_halo(
            token_edges.astype(jnp.bfloat16), (("seq", 0),), LOCAL_HALF
        ).astype(token_edges.dtype)
        grad_kv = add_rims(grad_extended[LOCAL_HALF:-LOCAL_HALF], token_returned, LOCAL_HALF)
        grad_projected = jnp.concatenate(
            [grad_queries.reshape(block_rows, model_width), grad_kv], axis=1
        ).astype(jnp.bfloat16)
        grad_qkvw = jnp.dot(normed.T, grad_projected, preferred_element_type=jnp.float32)
        grad_normed = jnp.dot(grad_projected, back_qkv.T, preferred_element_type=jnp.float32)
        norm_value_one, norm_back_one = jax.vjp(layer_norm, inputs, gain_float, bias_float)
        grad_in_part, grad_gain_one, grad_bias_one = norm_back_one(grad_normed)
        input_grads.append(grad_middle + grad_in_part)
        shares = (
            lax.psum_scatter(grad_gain_one, ("dp", "seq"), scatter_dimension=0, tiled=True),
            lax.psum_scatter(grad_bias_one, ("dp", "seq"), scatter_dimension=0, tiled=True),
            lax.psum_scatter(grad_qkvw, ("dp", "seq"), scatter_dimension=0, tiled=True),
            lax.psum_scatter(grad_taps, ("dp", "seq"), scatter_dimension=1, tiled=True),
            lax.psum_scatter(grad_outw, ("dp", "seq"), scatter_dimension=0, tiled=True),
            lax.psum_scatter(grad_gain_two, ("dp", "seq"), scatter_dimension=0, tiled=True),
            lax.psum_scatter(grad_bias_two, ("dp", "seq"), scatter_dimension=0, tiled=True),
            lax.psum_scatter(grad_upw, ("dp", "seq"), scatter_dimension=0, tiled=True),
            lax.psum_scatter(grad_down, ("dp", "seq"), scatter_dimension=1, tiled=True),
        )
        if summed is None:
            summed = shares
        else:
            summed = jax.tree.map(jnp.add, summed, shares)
    return (
        jnp.stack(outputs),
        jnp.stack(input_grads),
        summed[0],
        summed[1],
        summed[2],
        summed[3],
        summed[4],
        summed[5],
        summed[6],
        summed[7],
        summed[8],
    )


def solution(mesh):
    placed = (
        P("dp", "seq", None),
        P("dp", None),
        P("dp", "seq", None),
        P(("dp", "seq")),
        P(("dp", "seq")),
        P(("dp", "seq"), None),
        P(None, ("dp", "seq")),
        P(("dp", "seq"), None),
        P(("dp", "seq")),
        P(("dp", "seq")),
        P(("dp", "seq"), None),
        P(None, ("dp", "seq")),
    )
    return jax.shard_map(
        shards,
        mesh=mesh,
        in_specs=placed,
        out_specs=(
            P("dp", "seq", None),
            P("dp", "seq", None),
            P(("dp", "seq")),
            P(("dp", "seq")),
            P(("dp", "seq"), None),
            P(None, ("dp", "seq")),
            P(("dp", "seq"), None),
            P(("dp", "seq")),
            P(("dp", "seq")),
            P(("dp", "seq"), None),
            P(None, ("dp", "seq")),
        ),
        check_vma=False,
    )
```

profile of v0, /device:TPU:0, one launch (start us, length us, event | category | flops | bytes accessed | tf_op | source)
XLA Modules:
  0.0 1165.4 jit_solution(12068151886575012651)
XLA Ops:
  17.3 42.2 %all-reduce.37 = (bf16[768]{0:T(1024)(128)(2,1)S(1)}, bf16[768]{0:T(1024)(128)(2,1)S(1)}, bf16[768]{0:T(1024)(128)(2,1)S(1)}, bf16[768]{0:T(1024)(128)(2,1)S(1)}) all-reduce(bf16[768]{0:T(1024)(128)(2,1)S(1)} %dynamic-update-slice.1, bf16[768]{0:T(1024)(128)(2,1)S(1)} %dynamic-update-slice, ...), channel_id=1, replica_groups=mesh['dp'=2,'seq'=16] {'dp','seq'}, use_global_device_ids=true, to_apply=%add.29 | all-reduce | flops 3072 | bytes 12288
  63.8 66.1 %all-gather = bf16[32,48,5]{1,2,0:T(8,128)(2,1)S(1)} all-gather(bf16[1,48,5]{1,2,0:T(8,128)(2,1)S(1)} %bitcast.285), channel_id=1, replica_groups=mesh['dp'=2,'seq'=16] {'dp','seq'}, dimensions={0}, use_global_device_ids=true | all-gather | bytes 15840 | tf_op jit(solution)/shard_map/all_gather | solution.py:121
  251.7 8.4 fusion.1
  260.2 8.0 fusion
  281.9 8.7 fusion.5
  300.2 13.2 %fusion.3 = f32[12,512]{1,0:T(8,128)S(1)} fusion(f32[12,512,640]{2,1,0:T(8,128)S(1)} %bitcast.227, f32[12,512]{1,0:T(8,128)S(1)} %max.16, pred[512,640]{1,0:T(8,128)(4,1)S(1)} %copy-done.48), kind=kLoop, calls=%fused_computation.11 | loop fusion | flops 19654656 | bytes 16105472 | tf_op jit(solution)/shard_map/reduce_sum | solution.py:163
  317.8 10.0 add_convert_fusion.2
  337.4 7.6 add_convert_fusion.5
  347.7 7.2 fusion.124
  354.9 9.4 fusion.19
  392.9 10.1 fusion.26
  412.2 10.2 fusion.30
  432.5 14.6 %multiply_reduce_fusion.1 = (f32[12,512]{1,0:T(8,128)}, f32[12,512,640]{2,1,0:T(8,128)}) fusion(f32[12,512]{1,0:T(8,128)S(1)} %copy-done.101, f32[12,512]{1,0:T(8,128)S(1)} %max.16, f32[12,512,640]{2,1,0:T(8,128)} %get-tuple-element.139, pred[512,640]{1,0:T(8,128)(4,1)} %compare_and_fusion.1, bf16[512,12,64]{0,2,1:T(8,128)(2,1)} %bitcast.274, ...), kind=kOutput, calls=%fused_computation.3 | convolution fusion | flops 530835456 | bytes 33628160 | tf_op jit(solution)/shard_map/qhd,khd->hqk/dot_general | solution.py:223
  457.6 11.1 multiply_reduce_fusion
  479.9 12.1 %multiply_convert_fusion.1 = bf16[12,512,640]{2,1,0:T(8,128)(2,1)S(1)} fusion(f32[12,512,640]{2,1,0:T(8,128)} %get-tuple-element.146, f32[12,512]{1,0:T(8,128)} %copy-done.104, f32[12,512]{1,0:T(8,128)S(1)} %copy-done.102, f32[12,512]{1,0:T(8,128)S(1)} %copy-done.83, f32[12,512,640]{2,1,0:T(8,128)} %get-tuple-element.139, pred[512,640]{1,0:T(8,128)(4,1)S(1)} %copy-done.51), kind=kLoop, calls=%fused_computation.2 | loop fusion | flops 31457280 | bytes 39723008 | tf_op jit(solution)/shard_map/convert_element_type | solution.py:232
  508.1 12.0 %multiply_convert_fusion = bf16[12,512,640]{2,1,0:T(8,128)(2,1)S(1)} fusion(f32[12,512,640]{2,1,0:T(8,128)} %get-tuple-element.150, f32[12,512]{1,0:T(8,128)} %copy-done.103, f32[12,512]{1,0:T(8,128)} %copy-done.96, f32[12,512]{1,0:T(8,128)} %copy-done.81, f32[12,512,640]{2,1,0:T(8,128)} %get-tuple-element.133, pred[512,640]{1,0:T(8,128)(4,1)} %copy-done.46), kind=kLoop, calls=%fused_computation | loop fusion | flops 31457280 | bytes 39723008 | tf_op jit(solution)/shard_map/convert_element_type | solution.py:232
  567.0 10.2 pad.100
  577.2 6.3 pad.103
  589.8 10.0 pad.101
  599.8 10.0 pad.99
  609.8 10.6 fusion.139
  627.6 10.2 pad.108
  650.3 6.3 pad.112
  656.6 6.4 pad.109
  663.0 8.8 fusion.137
  701.2 9.8 convolution_add_fusion.1
  723.8 8.1 fusion.82
  731.9 8.1 fusion.81
  751.7 47.0 %all-reduce.36 = (f32[768]{0:T(1024)S(1)}, f32[768]{0:T(1024)S(1)}, f32[768]{0:T(1024)S(1)}, f32[768]{0:T(1024)S(1)}) all-reduce(f32[768]{0:T(1024)S(1)} %add.417, f32[768]{0:T(1024)S(1)} %add.418, f32[768]{0:T(1024)S(1)} %add.422, f32[768]{0:T(1024)S(1)} %add.423), channel_id=11, replica_groups=mesh['dp'=2,'seq'=16] {'dp','seq'}, use_global_device_ids=true, to_apply=%region_29.30.clone | all-reduce | flops 3072 | bytes 24576
  806.5 68.5 %reduce-scatter.8.cloned.1.call-done = f32[24,2304]{1,0:T(8,128)} async-done(((f32[768,2304]{1,0:T(8,128)}), f32[24,2304]{1,0:T(8,128)}) %reduce-scatter.8.cloned.1.call-update) | async-done | bytes 221200 | tf_op jit(solution)/shard_map/reduce_scatter | solution.py:292
  875.1 141.3 %reduce-scatter.14.cloned.1.call-done = f32[3072,24]{0,1:T(8,128)} async-done(((f32[3072,768]{0,1:T(8,128)}), f32[3072,24]{0,1:T(8,128)}) %reduce-scatter.14.cloned.1.call-update) | async-done | bytes 294928 | tf_op jit(solution)/shard_map/reduce_scatter | solution.py:298
  1016.3 142.0 %reduce-scatter.12.cloned.1.call-done = f32[24,3072]{1,0:T(8,128)} async-done(((f32[768,3072]{1,0:T(8,128)}), f32[24,3072]{1,0:T(8,128)}) %reduce-scatter.12.cloned.1.call-update) | async-done | bytes 294928 | tf_op jit(solution)/shard_map/reduce_scatter | solution.py:297
  (663 shorter events, 393.8 us)
Async XLA Ops:
  7.2 126.1 %copy-start.3 = (bf16[2,512,768]{2,1,0:T(8,128)(2,1)S(1)}, bf16[2,512,768]{2,1,0:T(8,128)(2,1)}, u32[]{:S(2)}) copy-start(bf16[2,512,768]{2,1,0:T(8,128)(2,1)} %param.12) | copy-start | bytes 4718596
  7.2 126.1 %all-gather.6.cloned.1.call-start = ((), (), s32[]{:S(2)}) async-start(), calls=%async_computation.5 | async-start | bytes 3649536 | tf_op jit(solution)/shard_map/all_gather | solution.py:120
  7.9 319.9 %all-gather.8.cloned.1.call-start = ((), (), s32[]{:S(2)}) async-start(), calls=%async_computation.6 | async-start | bytes 1216512 | tf_op jit(solution)/shard_map/all_gather | solution.py:122
  8.7 339.1 %all-gather.10.cloned.1.call-start = ((), (), s32[]{:S(2)}) async-start(), calls=%async_computation.7 | async-start | bytes 4866048 | tf_op jit(solution)/shard_map/all_gather | solution.py:125
  9.4 345.5 %all-gather.12.cloned.1.call-start = ((), (), s32[]{:S(2)}) async-start(), calls=%async_computation.8 | async-start | bytes 4866048 | tf_op jit(solution)/shard_map/all_gather | solution.py:126
  10.0 731.3 %reduce-scatter.16.cloned.1.call-start = ((), (), s32[]{:S(2)}) async-start(), calls=%async_computation.13 | async-start | bytes 811008
  59.5 320.3 %copy-start.109 = (f32[768]{0:T(1024)}, f32[768]{0:T(1024)S(1)}, u32[]{:S(2)}) copy-start(f32[768]{0:T(1024)S(1)} %convert_element_type.232) | copy-start | bytes 9220
  59.5 307.5 %copy-start.122 = (f32[768]{0:T(1024)}, f32[768]{0:T(1024)S(1)}, u32[]{:S(2)}) copy-start(f32[768]{0:T(1024)S(1)} %convert_element_type.233) | copy-start | bytes 9220
  130.5 327.0 %copy-start.46 = (pred[512,640]{1,0:T(8,128)(4,1)}, pred[512,640]{1,0:T(8,128)(4,1)S(1)}, u32[]{:S(2)}) copy-start(pred[512,640]{1,0:T(8,128)(4,1)S(1)} %compare_and_fusion) | copy-start | bytes 983044
  138.4 19.2 %collective-permute-start = (bf16[64,1536]{1,0:T(8,128)(2,1)}, bf16[64,1536]{1,0:T(8,128)(2,1)}, u32[]{:S(2)}, u32[]{:S(2)}) collective-permute-start(bf16[64,1536]{1,0:T(8,128)(2,1)} %get-tuple-element.66), channel_id=1, source_target_pairs={{0,1},{1,2},{2,3},{3,4},{4,5},{5,6},{6,7},{7,8},{8,9},{9,10},{10,1... | collective-permute-start | bytes 589832 | tf_op jit(solution)/shard_map/ppermute | solution.py:19
  141.0 16.6 %collective-permute-start.1 = (bf16[64,1536]{1,0:T(8,128)(2,1)}, bf16[64,1536]{1,0:T(8,128)(2,1)}, u32[]{:S(2)}, u32[]{:S(2)}) collective-permute-start(bf16[64,1536]{1,0:T(8,128)(2,1)} %get-tuple-element.67), channel_id=1, source_target_pairs={{1,0},{2,1},{3,2},{4,3},{5,4},{6,5},{7,6},{8,7},{9,8},{10,9},{11,1... | collective-permute-start | bytes 589832 | tf_op jit(solution)/shard_map/ppermute | solution.py:20
  148.8 37.8 %collective-permute-start.4 = (bf16[64,1536]{1,0:T(8,128)(2,1)}, bf16[64,1536]{1,0:T(8,128)(2,1)}, u32[]{:S(2)}, u32[]{:S(2)}) collective-permute-start(bf16[64,1536]{1,0:T(8,128)(2,1)} %get-tuple-element.68), channel_id=1, source_target_pairs={{0,1},{1,2},{2,3},{3,4},{4,5},{5,6},{6,7},{7,8},{8,9},{9,10},{10,1... | collective-permute-start | bytes 589832 | tf_op jit(solution)/shard_map/ppermute | solution.py:19
  154.0 32.6 %collective-permute-start.5 = (bf16[64,1536]{1,0:T(8,128)(2,1)}, bf16[64,1536]{1,0:T(8,128)(2,1)}, u32[]{:S(2)}, u32[]{:S(2)}) collective-permute-start(bf16[64,1536]{1,0:T(8,128)(2,1)} %get-tuple-element.69), channel_id=1, source_target_pairs={{1,0},{2,1},{3,2},{4,3},{5,4},{6,5},{7,6},{8,7},{9,8},{10,9},{11,1... | collective-permute-start | bytes 589832 | tf_op jit(solution)/shard_map/ppermute | solution.py:20
  157.6 133.0 %copy-start.7 = (bf16[512,768]{0,1:T(8,128)(2,1)}, bf16[512,768]{0,1:T(8,128)(2,1)S(1)}, u32[]{:S(2)}) copy-start(bf16[512,768]{0,1:T(8,128)(2,1)S(1)} %copy.136) | copy-start | bytes 2359300
  224.7 43.5 %collective-permute-start.2 = (bf16[64,1536]{1,0:T(8,128)(2,1)}, bf16[64,1536]{1,0:T(8,128)(2,1)}, u32[]{:S(2)}, u32[]{:S(2)}) collective-permute-start(bf16[64,1536]{1,0:T(8,128)(2,1)} %get-tuple-element.106), channel_id=1, source_target_pairs={{0,1},{1,2},{2,3},{3,4},{4,5},{5,6},{6,7},{7,8},{8,9},{9,10},{10,1... | collective-permute-start | bytes 589832 | tf_op jit(solution)/shard_map/ppermute | solution.py:19
  230.1 38.1 %collective-permute-start.3 = (bf16[64,1536]{1,0:T(8,128)(2,1)}, bf16[64,1536]{1,0:T(8,128)(2,1)}, u32[]{:S(2)}, u32[]{:S(2)}) collective-permute-start(bf16[64,1536]{1,0:T(8,128)(2,1)} %get-tuple-element.107), channel_id=1, source_target_pairs={{1,0},{2,1},{3,2},{4,3},{5,4},{6,5},{7,6},{8,7},{9,8},{10,9},{11,1... | collective-permute-start | bytes 589832 | tf_op jit(solution)/shard_map/ppermute | solution.py:20
  242.9 29.2 %collective-permute-start.6 = (bf16[64,1536]{1,0:T(8,128)(2,1)}, bf16[64,1536]{1,0:T(8,128)(2,1)}, u32[]{:S(2)}, u32[]{:S(2)}) collective-permute-start(bf16[64,1536]{1,0:T(8,128)(2,1)} %get-tuple-element.108), channel_id=1, source_target_pairs={{0,1},{1,2},{2,3},{3,4},{4,5},{5,6},{6,7},{7,8},{8,9},{9,10},{10,1... | collective-permute-start | bytes 589832 | tf_op jit(solution)/shard_map/ppermute | solution.py:19
  248.1 24.0 %collective-permute-start.7 = (bf16[64,1536]{1,0:T(8,128)(2,1)}, bf16[64,1536]{1,0:T(8,128)(2,1)}, u32[]{:S(2)}, u32[]{:S(2)}) collective-permute-start(bf16[64,1536]{1,0:T(8,128)(2,1)} %get-tuple-element.109), channel_id=1, source_target_pairs={{1,0},{2,1},{3,2},{4,3},{5,4},{6,5},{7,6},{8,7},{9,8},{10,9},{11,1... | collective-permute-start | bytes 589832 | tf_op jit(solution)/shard_map/ppermute | solution.py:20
  280.4 188.3 %copy-start.81 = (f32[12,512]{1,0:T(8,128)}, f32[12,512]{1,0:T(8,128)S(1)}, u32[]{:S(2)}) copy-start(f32[12,512]{1,0:T(8,128)S(1)} %max.17) | copy-start | bytes 73732
  295.1 152.8 %copy-start.82 = (f32[12,512]{1,0:T(8,128)}, f32[12,512]{1,0:T(8,128)S(1)}, u32[]{:S(2)}) copy-start(f32[12,512]{1,0:T(8,128)S(1)} %max.16) | copy-start | bytes 73732
  501.6 36.1 %collective-permute-start.8 = (bf16[64,1536]{1,0:T(8,128)(2,1)}, bf16[64,1536]{1,0:T(8,128)(2,1)}, u32[]{:S(2)}, u32[]{:S(2)}) collective-permute-start(bf16[64,1536]{1,0:T(8,128)(2,1)} %get-tuple-element.100), channel_id=1, source_target_pairs={{0,1},{1,2},{2,3},{3,4},{4,5},{5,6},{6,7},{7,8},{8,9},{9,10},{10,1... | collective-permute-start | bytes 589832 | tf_op jit(solution)/shard_map/ppermute | solution.py:19
  506.8 30.9 %collective-permute-start.9 = (bf16[64,1536]{1,0:T(8,128)(2,1)}, bf16[64,1536]{1,0:T(8,128)(2,1)}, u32[]{:S(2)}, u32[]{:S(2)}) collective-permute-start(bf16[64,1536]{1,0:T(8,128)(2,1)} %get-tuple-element.101), channel_id=1, source_target_pairs={{1,0},{2,1},{3,2},{4,3},{5,4},{6,5},{7,6},{8,7},{9,8},{10,9},{11,1... | collective-permute-start | bytes 589832 | tf_op jit(solution)/shard_map/ppermute | solution.py:20
  528.0 13.8 %collective-permute-start.12 = (bf16[64,1536]{1,0:T(8,128)(2,1)S(1)}, bf16[64,1536]{1,0:T(8,128)(2,1)S(1)}, u32[]{:S(2)}, u32[]{:S(2)}) collective-permute-start(bf16[64,1536]{1,0:T(8,128)(2,1)S(1)} %get-tuple-element.91), channel_id=1, source_target_pairs={{0,1},{1,2},{2,3},{3,4},{4,5},{5,6},{6,7},{7,8},{8,9},{9,10},{10,1... | collective-permute-start | bytes 589832 | tf_op jit(solution)/shard_map/ppermute | solution.py:19
  532.8 9.1 collective-permute-start.13
  545.5 261.1 %reduce-scatter.10.cloned.1.call-start = ((), (), s32[]{:S(2)}) async-start(), calls=%async_computation.10 | async-start | bytes 2433024 | tf_op jit(solution)/shard_map/reduce_scatter | solution.py:294
  563.6 311.5 %reduce-scatter.8.cloned.1.call-start = ((), (), s32[]{:S(2)}) async-start(), calls=%async_computation.9 | async-start | bytes 7299072 | tf_op jit(solution)/shard_map/reduce_scatter | solution.py:292
  621.1 57.0 %collective-permute-start.10 = (bf16[64,1536]{1,0:T(8,128)(2,1)}, bf16[64,1536]{1,0:T(8,128)(2,1)}, u32[]{:S(2)}, u32[]{:S(2)}) collective-permute-start(bf16[64,1536]{1,0:T(8,128)(2,1)} %get-tuple-element.72), channel_id=1, source_target_pairs={{0,1},{1,2},{2,3},{3,4},{4,5},{5,6},{6,7},{7,8},{8,9},{9,10},{10,1... | collective-permute-start | bytes 589832 | tf_op jit(solution)/shard_map/ppermute | solution.py:19
  626.3 51.8 %collective-permute-start.11 = (bf16[64,1536]{1,0:T(8,128)(2,1)}, bf16[64,1536]{1,0:T(8,128)(2,1)}, u32[]{:S(2)}, u32[]{:S(2)}) collective-permute-start(bf16[64,1536]{1,0:T(8,128)(2,1)} %get-tuple-element.73), channel_id=1, source_target_pairs={{1,0},{2,1},{3,2},{4,3},{5,4},{6,5},{7,6},{8,7},{9,8},{10,9},{11,1... | collective-permute-start | bytes 589832 | tf_op jit(solution)/shard_map/ppermute | solution.py:20
  671.8 8.0 collective-permute-start.14
  676.7 8.7 collective-permute-start.15
  694.8 321.6 %reduce-scatter.14.cloned.1.call-start = ((), (), s32[]{:S(2)}) async-start(), calls=%async_computation.12 | async-start | bytes 9732096 | tf_op jit(solution)/shard_map/reduce_scatter | solution.py:298
  711.0 447.4 %reduce-scatter.12.cloned.1.call-start = ((), (), s32[]{:S(2)}) async-start(), calls=%async_computation.11 | async-start | bytes 9732096 | tf_op jit(solution)/shard_map/reduce_scatter | solution.py:297
  (194 other events, 3234.5 us)
Sparse Core Ops, SparseCore 0:
  10.9 62.8 all-gather.5
  76.7 52.9 all-gather.7
  132.6 65.0 all-gather.9
  200.5 68.5 all-gather.11
  545.6 100.3 reduce-scatter.15
  651.7 97.8 reduce-scatter.9
  756.8 118.2 reduce-scatter.7
  881.5 134.7 reduce-scatter.13
  1023.8 134.5 reduce-scatter.11
where the time goes:
time: 1180 us; the launch traced here: 1170 us
  waiting for transfers between devices  361 us (31%)
  matrix products  242 us (21%)
  local copies, waits for them, and re-layouts  210 us (18%)
  blocking collectives  155 us (13%)
  other arithmetic  131 us (11%)
  starting transfers between devices  49.5 us (4%)
  between operations  17.1 us (1%)
    reduce_scatter x1, waiting for transfers between devices, shards(): lax.psum_scatter(grad_upw, ('dp', 'seq'), scatter_dimension=0, tiled=True)  142 us
    reduce_scatter x1, waiting for transfers between devices, shards(): lax.psum_scatter(grad_down, ('dp', 'seq'), scatter_dimension=1, tiled=True)  141 us
    unnamed x2, blocking collectives  89.2 us
    pad x10, local copies, waits for them, and re-layouts, pool_local(): picked = extended[start_row:start_row + block_rows:4]  78.2 us
    reduce_scatter x1, waiting for transfers between devices, shards(): lax.psum_scatter(grad_qkvw, ('dp', 'seq'), scatter_dimension=0, tiled=True)  68.5 us
    all_gather x1, blocking collectives, shards(): lax.all_gather(pool_taps, ('dp', 'seq'), axis=1, tiled=True)  66.1 us
    slice x10, local copies, waits for them, and re-layouts, pool_local(): picked = extended[start_row:start_row + block_rows:4]  48 us
    ppermute x8, starting transfers between devices, with_halo(): before = lax.ppermute(last, axis, up)  38.5 us
  transfers between devices with their start and end apart: 25, of which 6 were waited for; matrix products, arithmetic and copies ran while one was open for 36% of the time, Pallas kernels for 0%

commit v1 on v0

--- a/solution.py
+++ b/solution.py
@@ -1,12 +1,1113 @@
+import functools
+
 import jax
 import jax.numpy as jnp
 from jax import lax
+from jax.experimental import pallas as pl
+from jax.experimental.pallas import tpu as pltpu
 from jax.sharding import PartitionSpec as P
 
 HEADS = 12
 HEAD = 64
-LOCAL_HALF = 64
-POOL_REACH = 256
+NEAR = 64
+REACH = 256
+F32, BF = jnp.float32, jnp.bfloat16
+NT = (((1,), (1,)), ((), ()))
+TN = (((0,), (0,)), ((), ()))
+NN = (((1,), (0,)), ((), ()))
+MESH = pl.DeviceIdType.MESH
+ANY = pl.BlockSpec(memory_space=pl.ANY)
+VM = pl.BlockSpec(memory_space=pltpu.VMEM)
+VMEM_LIMIT = 62 * 2**20
+UNIT = 384
+CLS = 3456
+WIDE = 3584
+PLACE = {"qkv": (0, 0, 2304), "out": (1, 0, 768), "up": (1, 3, 3072), "down": (1, 15, 3072)}
+
+
+def dg(a, b, dims):
+    return lax.dot_general(a, b, dims, preferred_element_type=F32)
+
+
+def spot(name, unit):
+    first, start, _ = PLACE[name]
+    at = start + unit
+    return first + at // 9, (at % 9) * UNIT
+
+
+def units(name):
+    return PLACE[name][2] // UNIT
+
+
+def where_am_i():
+    c = lax.axis_index("dp")
+    s = lax.axis_index("seq")
+    z, col = s // 4, s % 4
+    x, y = col % 2, col // 2
+    colx, coly, cold = y * 2 + (1 - x), (1 - y) * 2 + x, 3 - col
+    return dict(
+        c=c, s=s, z=z, col=col, colx=colx, coly=coly, cold=cold,
+        px=(c, z * 4 + colx), py=(c, z * 4 + coly), pd=(1 - c, s),
+    )
+
+
+def greet(me, halo):
+    bar = pltpu.get_barrier_semaphore()
+    who = [me["px"], me["py"], me["pd"]]
+    who += [(me["c"], lax.rem(me["z"] + j, 4) * 4 + me["col"]) for j in (1, 2, 3)]
+    for dev in who:
+        pl.semaphore_signal(bar, inc=1, device_id=dev, device_id_type=MESH)
+    count = 6
+    if halo:
+        last = lax.axis_size("seq") - 1
+
+        @pl.when(me["s"] > 0)
+        def _():
+            pl.semaphore_signal(bar, inc=1, device_id=(me["c"], me["s"] - 1), device_id_type=MESH)
+
+        @pl.when(me["s"] < last)
+        def _():
+            pl.semaphore_signal(bar, inc=1, device_id=(me["c"], me["s"] + 1), device_id_type=MESH)
+
+        count = 6 + (me["s"] > 0).astype(jnp.int32) + (me["s"] < last).astype(jnp.int32)
+    pl.semaphore_wait(bar, count)
+
+
+def lane_low():
+    return lax.broadcasted_iota(jnp.int32, (128, 128), 1) < HEAD
+
+
+def pair_rows(v):
+    low = lane_low()
+    zero = jnp.zeros_like(v)
+    return jnp.concatenate([jnp.where(low, v, zero), jnp.where(low, zero, v)], axis=0)
+
+
+def pair_out(t):
+    return jnp.concatenate([t[:HEAD, :128], t[HEAD:, 128:]], axis=0).T
+
+
+def softmax_block(q2, kn, kf, bias):
+    st = jnp.concatenate([dg(kn, q2, NT), dg(kf, q2, NT)], axis=0)
+    st = st + jnp.concatenate([bias, bias], axis=1)
+    top = jnp.max(st, axis=0, keepdims=True)
+    e = jnp.exp(st - top)
+    total = jnp.sum(e, axis=0, keepdims=True)
+    return e, 1.0 / total
+
+
+def mask_block(winc, win4, winr, r, b):
+    seg_q = winr[r : r + 1, 256 + 128 * b : 384 + 128 * b]
+    kk = lax.broadcasted_iota(jnp.int32, (256, 128), 0)
+    ii = lax.broadcasted_iota(jnp.int32, (256, 128), 1)
+    seg_k = winc[r, 192 + 128 * b : 448 + 128 * b, :]
+    near = (jnp.abs(kk - NEAR - ii) <= NEAR) & (seg_k == seg_q)
+    pp = lax.broadcasted_iota(jnp.int32, (160, 128), 0)
+    qi = lax.broadcasted_iota(jnp.int32, (160, 128), 1)
+    seg_p = win4[r, 32 * b : 32 * b + 160, 0:1]
+    far = (jnp.abs(4 * pp - REACH - qi) <= REACH) & (seg_p == seg_q)
+    return jnp.where(near, 0.0, -1e30), jnp.where(far, 0.0, -1e30)
+
+
+def fill_masks(winc, win4, winr, bias):
+    for r in range(2):
+        for b in range(4):
+            near, far = mask_block(winc, win4, winr, r, b)
+            bias[r * 4 + b, 0:256] = near
+            bias[r * 4 + b, 256:416] = far
+
+
+def head_lanes(h):
+    return (
+        pl.ds(pl.multiple_of(h * 128, 128), 128),
+        pl.ds(pl.multiple_of(768 + h * 128, 128), 128),
+    )
+
+
+def attend(q, kv, pe, bias, att, r, h):
+    kl, vl = head_lanes(h)
+    for b in range(4):
+        n, f, i = slice(b * 128, b * 128 + 256), slice(b * 32, b * 32 + 160), slice(b * 128, b * 128 + 128)
+        e, rt = softmax_block(pair_rows(q[r, i, kl]), kv[r, n, kl], pe[r, f, kl], bias[r * 4 + b])
+        low = (e * rt).astype(BF)
+        values = jnp.concatenate([kv[r, n, vl], pe[r, f, vl]], axis=0)
+        att[r, i, kl] = pair_out(dg(values, low, TN)).astype(BF)
+
+
+def attend_back(q, kv, pe, bias, g, gext, dkv, dpe, r, h):
+    kl, vl = head_lanes(h)
+    for part in (h, 6 + h):
+        dkv[r, part] = jnp.zeros((640, 128), F32)
+        dpe[r, part] = jnp.zeros((256, 128), F32)
+    for b in range(4):
+        n, f, i = slice(b * 128, b * 128 + 256), slice(b * 32, b * 32 + 160), slice(b * 128, b * 128 + 128)
+        q2, g2 = pair_rows(q[r, i, kl]), pair_rows(g[r, i, kl])
+        kn, vn, kf, vf = kv[r, n, kl], kv[r, n, vl], pe[r, f, kl], pe[r, f, vl]
+        e, rt = softmax_block(q2, kn, kf, bias[r * 4 + b])
+        p = e * rt
+        dp = jnp.concatenate([dg(vn, g2, NT), dg(vf, g2, NT)], axis=0)
+        delta = jnp.sum(p * dp, axis=0, keepdims=True)
+        ds = (p * (dp - delta)).astype(BF)
+        low = p.astype(BF)
+        dv, dk = dg(low, g2, NN), dg(ds, q2, NN)
+        dkv[r, h, n] += dk[:256]
+        dkv[r, 6 + h, n] += dv[:256]
+        dpe[r, h, f] += dk[256:]
+        dpe[r, 6 + h, f] += dv[256:]
+        dqt = dg(jnp.concatenate([kn, kf], axis=0), ds, TN)
+        gext[r, 64 + b * 128 : 192 + b * 128, kl] = (pair_out(dqt) * HEAD**-0.5).astype(BF)
+
+
+def norm_parts(v):
+    mean = jnp.mean(v, axis=-1, keepdims=True)
+    cen = v - mean
+    var = jnp.mean(cen * cen, axis=-1, keepdims=True)
+    rs = lax.rsqrt(var + 1e-05)
+    return cen * rs, rs
+
+
+def pack_own(grab, put):
+    for name in ("qkv", "out", "up", "down"):
+        half = units(name) // 2
+        for u in range(units(name)):
+            k, lo = spot(name, u)
+            put(k, lo, grab(name, 0, 16, u))
+        for u in range(half):
+            k, lo = spot(name, units(name) + u)
+            put(k, lo, jnp.concatenate([grab(name, 16, 24, u), grab(name, 16, 24, u + half)], axis=0))
+
+
+def unpack(name, got, dst):
+    half = units(name) // 2
+
+    def pair(i, carry):
+        rows = pl.ds(pl.multiple_of(48 * i, 16), 48)
+        for u in range(units(name)):
+            k, lo = spot(name, u)
+            kt, lt = spot(name, units(name) + u % half)
+            cut = slice(0, 8) if u < half else slice(8, 16)
+            parts = []
+            for j in (0, 1):
+                parts.append(got[k, 2 * i + j, :, lo : lo + UNIT])
+                parts.append(got[kt, 2 * i + j, :, lt : lt + UNIT][cut])
+            dst[rows, u * UNIT : (u + 1) * UNIT] = jnp.concatenate(parts, axis=0)
+        return carry
+
+    lax.fori_loop(0, 16, pair, 0)
+
+
+def spread_small(got, taps, gains):
+    lane = lax.broadcasted_iota(jnp.int32, (16, 128), 1)
+
+    def place(width, tiles):
+        acc = [jnp.zeros((16, 128), F32) for _ in range(tiles)]
+        for s in range(32):
+            at, off = divmod(width * s, 128)
+            v = jnp.where(lane < width, got[0, s, :, CLS:WIDE].astype(F32), 0.0)
+            v = pltpu.roll(v, off, 1) if off else v
+            acc[at] = acc[at] + jnp.where(lane >= off, v, 0.0)
+            if off + width > 128:
+                acc[at + 1] = acc[at + 1] + jnp.where(lane < off, v, 0.0)
+        return acc
+
+    for i, v in enumerate(place(48, 12)):
+        taps[:, i * 128 : (i + 1) * 128] = v
+    for i, v in enumerate(place(24, 6)):
+        gains[:, i * 128 : (i + 1) * 128] = v
+
+
+def front_kernel(
+    tok, winc, win4, winr, wq, wo, wu, wd, small,
+    o_wq, o_wo, o_wu, o_wd, o_taps, o_gains, o_h1, o_q, o_kv, o_pe, o_att, o_bias,
+    G, Wq, Wo, Wu, Wd, taps, gains, xe, h1, q, kv, pe, att, bias, chunk,
+    send_x, send_y, send_d, send_z, send_g, recv, hsend, hrecv, local,
+):
+    me = where_am_i()
+    c, s, z, col = me["c"], me["s"], me["z"], me["col"]
+    mine = c * 16 + s
+    last = lax.axis_size("seq") - 1
+    has_left, has_right = s > 0, s < last
+
+    def cols(k):
+        return WIDE if isinstance(k, int) and k == 0 else CLS
+
+    def hop(k, slot, to, sem):
+        part = G.at[k, slot, :, pl.ds(0, cols(k))]
+        return pltpu.make_async_remote_copy(
+            src_ref=part, dst_ref=part, send_sem=sem, recv_sem=recv.at[k, slot],
+            device_id=to, device_id_type=MESH,
+        )
+
+    def to_x(k, at):
+        return hop(k, c * 16 + at, me["px"], send_x.at[k, at])
+
+    def to_y(k, at):
+        return hop(k, c * 16 + at, me["py"], send_y.at[k, at])
+
+    def to_d(k, at):
+        return hop(k, c * 16 + at, me["pd"], send_d.at[k, at])
+
+    def to_z(k, j):
+        return hop(k, mine, (c, lax.rem(z + j, 4) * 4 + col), send_z.at[k, j - 1])
+
+    def to_g(k, zz):
+        even = lax.rem(zz, 2) == 0
+        at = zz * 4 + jnp.where(even, me["colx"], me["coly"])
+        to = (c, z * 4 + jnp.where(even, me["coly"], me["colx"]))
+        return hop(k, c * 16 + at, to, send_g.at[k, zz])
+
+    def got(k, slot):
+        hop(k, slot, me["px"], send_x.at[k, 0]).wait_recv()
+
+    def own(k):
+        for j in (1, 2, 3):
+            to_z(k, j).start()
+        to_x(k, s).start()
+        to_y(k, s).start()
+        to_d(k, s).start()
+
+    def column(k, j):
+        at = lax.rem(z + j, 4) * 4 + col
+        got(k, c * 16 + at)
+        to_x(k, at).start()
+        to_y(k, at).start()
+        to_d(k, at).start()
+
+    def plane(k, j):
+        zz = lax.rem(z + j, 4)
+        got(k, c * 16 + zz * 4 + me["colx"])
+        to_d(k, zz * 4 + me["colx"]).start()
+        got(k, c * 16 + zz * 4 + me["coly"])
+        to_d(k, zz * 4 + me["coly"]).start()
+        to_g(k, zz).start()
+
+    def diag(k, j):
+        at = lax.rem(z + j, 4) * 4 + me["cold"]
+        got(k, c * 16 + at)
+        to_d(k, at).start()
+
+    def event(e):
+        k, i = e // 11 + 1, lax.rem(e, 11)
+
+        @pl.when(i < 4)
+        def _():
+            plane(k, i)
+
+        @pl.when((i >= 4) & (i < 7) & (k < 3))
+        def _():
+            column(k + 1, i - 3)
+
+        @pl.when(i >= 7)
+        def _():
+            diag(k, i - 7)
+
+    def halo_tok(r, right):
+        src = tok.at[r, pl.ds(448 if right else 0, 64)]
+        dst = xe.at[r, pl.ds(0 if right else 576, 64)]
+        i = r * 2 + int(right)
+        return pltpu.make_async_remote_copy(
+            src_ref=src, dst_ref=dst, send_sem=hsend.at[i], recv_sem=hrecv.at[i],
+            device_id=(c, s + 1 if right else s - 1), device_id_type=MESH,
+        )
+
+    def halo_pool(r, right):
+        src = pe.at[r, pl.ds(128 if right else 64, 64)]
+        dst = pe.at[r, pl.ds(0 if right else 192, 64)]
+        i = 4 + r * 2 + int(right)
+        return pltpu.make_async_remote_copy(
+            src_ref=src, dst_ref=dst, send_sem=hsend.at[i], recv_sem=hrecv.at[i],
+            device_id=(c, s + 1 if right else s - 1), device_id_type=MESH,
+        )
+
+    def both(make, r, act):
+        @pl.when(has_right)
+        def _():
+            act(make(r, True), True)
+
+        @pl.when(has_left)
+        def _():
+            act(make(r, False), False)
+
+    def arrived(make, r):
+        @pl.when(has_left)
+        def _():
+            make(r, True).wait_recv()
+
+        @pl.when(has_right)
+        def _():
+            make(r, False).wait_recv()
+
+    load = [pltpu.make_async_copy(tok.at[r], xe.at[r, pl.ds(64, 512)], local.at[r]) for r in range(2)]
+    for copy in load:
+        copy.start()
+    shares = {"qkv": wq, "out": wo, "up": wu, "down": wd}
+
+    def grab(name, a, b, u):
+        return shares[name][a:b, u * UNIT : (u + 1) * UNIT]
+
+    def put(k, lo, v):
+        G[k, mine, :, lo : lo + UNIT] = v
+
+    pack_own(grab, put)
+    G[0, mine, :, CLS:WIDE] = small[...]
+
+    @pl.when(jnp.logical_not(has_left))
+    def _():
+        for r in range(2):
+            xe[r, 0:64] = jnp.zeros((64, 768), BF)
+            pe[r, 0:64] = jnp.zeros((64, 1536), BF)
+
+    @pl.when(jnp.logical_not(has_right))
+    def _():
+        for r in range(2):
+            xe[r, 576:640] = jnp.zeros((64, 768), BF)
+            pe[r, 192:256] = jnp.zeros((64, 1536), BF)
+
+    greet(me, True)
+    own(0)
+    for r in range(2):
+        both(halo_tok, r, lambda copy, right: copy.start())
+    own(1)
+    own(2)
+    fill_masks(winc, win4, winr, bias)
+    for j in (1, 2, 3):
+        column(0, j)
+    for j in range(4):
+        plane(0, j)
+    own(3)
+    for j in (1, 2, 3):
+        column(1, j)
+    for j in range(4):
+        diag(0, j)
+
+    def other(k):
+        def body(i, carry):
+            got(k, (1 - c) * 16 + i)
+            return carry
+
+        lax.fori_loop(0, 16, body, 0)
+
+    other(0)
+    unpack("qkv", G, Wq)
+    spread_small(G, taps, gains)
+    outs = [
+        pltpu.make_async_copy(a, b, local.at[2 + i])
+        for i, (a, b) in enumerate(
+            [(Wq, o_wq), (taps, o_taps), (gains, o_gains), (h1, o_h1), (q, o_q), (kv, o_kv), (pe, o_pe),
+             (att, o_att), (bias, o_bias), (Wo, o_wo), (Wu, o_wu), (Wd, o_wd)]
+        )
+    ]
+    for i in (0, 1, 2, 8):
+        outs[i].start()
+    for copy in load:
+        copy.wait()
+    for r in range(2):
+        arrived(halo_tok, r)
+
+    for r in range(2):
+        def norm_rows(i, carry):
+            rows = pl.ds(pl.multiple_of(i * 128, 128), 128)
+            n, _ = norm_parts(xe[r, rows].astype(F32))
+            h1[r, rows] = (n * gains[5:6] + gains[6:7]).astype(BF)
+            return carry
+
+        lax.fori_loop(0, 5, norm_rows, 0)
+    outs[3].start()
+
+    for r in range(2):
+        def queries(j, carry):
+            lanes = pl.ds(pl.multiple_of(j * 256, 256), 256)
+            v = dg(h1[r, 64:576], Wq[:, lanes], NN)
+            q[r, :, lanes] = v.astype(BF) * jnp.asarray(HEAD**-0.5, BF)
+            return carry
+
+        lax.fori_loop(0, 3, queries, 0)
+        anchor = win4[r, 64:192, 0:1]
+        same = [
+            (win4[r, a : a + 128, f : f + 1] == anchor).astype(F32)
+            for a, f in ((63, 2), (63, 3), (64, 0), (64, 1), (64, 2))
+        ]
+
+        def keys(j, carry):
+            event(r * 6 + j)
+            lanes = pl.ds(pl.multiple_of(j * 128, 128), 128)
+            from_lanes = pl.ds(pl.multiple_of(768 + j * 256, 256), 256)
+            to_lanes = pl.ds(pl.multiple_of(j * 256, 256), 256)
+            v = dg(h1[r], Wq[:, from_lanes], NN).astype(BF)
+            kv[r, :, to_lanes] = v
+            chunk[0] = v[:, :128].astype(F32)
+            chunk[1] = v[:, 128:].astype(F32)
+            for half in range(2):
+                hl = pl.ds(pl.multiple_of(j * 256 + half * 128, 128), 128)
+                acc = jnp.zeros((128, 128), F32)
+                for t in range(5):
+                    acc = acc + taps[t : t + 1, hl] * chunk[half, pl.ds(62 + t, 128, stride=4), :] * same[t]
+                pe[r, 64:192, hl] = acc.astype(BF)
+            return carry
+
+        lax.fori_loop(0, 6, keys, 0)
+        both(halo_pool, r, lambda copy, right: copy.start())
+    outs[4].start()
+    outs[5].start()
+    for r in range(2):
+        arrived(halo_pool, r)
+
+        def heads_event(h, carry):
+            attend(q, kv, pe, bias, att, r, h)
+            base = 12 + (r * 6 + h) * 2
+
+            @pl.when(base < 33)
+            def _():
+                event(base)
+
+            @pl.when(base + 1 < 33)
+            def _():
+                event(base + 1)
+
+            return carry
+
+        lax.fori_loop(0, 6, heads_event, 0)
+    outs[6].start()
+    outs[7].start()
+    for k in (1, 2, 3):
+        other(k)
+    for i, (name, dst) in enumerate((("out", Wo), ("up", Wu), ("down", Wd))):
+        unpack(name, G, dst)
+        outs[9 + i].start()
+    for r in range(2):
+        both(halo_tok, r, lambda copy, right: copy.wait_send())
+        both(halo_pool, r, lambda copy, right: copy.wait_send())
+    for k in range(4):
+        def done(i, carry):
+            to_x(k, i * 4 + col).wait_send()
+            to_y(k, i * 4 + col).wait_send()
+            to_g(k, i).wait_send()
+            for j in range(4):
+                to_d(k, i * 4 + j).wait_send()
+            return carry
+
+        lax.fori_loop(0, 4, done, 0)
+        for j in (1, 2, 3):
+            to_z(k, j).wait_send()
+    for copy in outs:
+        copy.wait()
+
+
+def front(tok, winc, win4, winr, wq, wo, wu, wd, small):
+    sds = jax.ShapeDtypeStruct
+    shapes = [
+        ((768, 2304), BF), ((768, 768), BF), ((768, 3072), BF), ((768, 3072), BF),
+        ((16, 1536), F32), ((16, 768), F32),
+        ((2, 640, 768), BF), ((2, 512, 768), BF), ((2, 640, 1536), BF), ((2, 256, 1536), BF),
+        ((2, 512, 768), BF), ((8, 416, 128), F32),
+    ]
+    scratch = [pltpu.VMEM((4, 32, 16, WIDE), BF)]
+    scratch += [pltpu.VMEM(sh, dt) for sh, dt in shapes[:6]]
+    scratch += [pltpu.VMEM((2, 640, 768), BF)]
+    scratch += [pltpu.VMEM(sh, dt) for sh, dt in shapes[6:]]
+    scratch += [pltpu.VMEM((2, 640, 128), F32)]
+    dma = pltpu.SemaphoreType.DMA
+    scratch += [dma((4, 16)), dma((4, 16)), dma((4, 16)), dma((4, 3)), dma((4, 4)), dma((4, 32)), dma((8,)), dma((8,)), dma((14,))]
+    return pl.pallas_call(
+        front_kernel,
+        out_shape=[sds(sh, dt) for sh, dt in shapes],
+        in_specs=[ANY] + [VM] * 8,
+        out_specs=[ANY] * len(shapes),
+        scratch_shapes=scratch,
+        compiler_params=pltpu.CompilerParams(collective_id=0, has_side_effects=True, vmem_limit_bytes=VMEM_LIMIT),
+    )(tok, winc, win4, winr, wq, wo, wu, wd, small)
+
+
+def windows(segments):
+    block = 512
+    padded = jnp.pad(segments, ((0, 0), (REACH, REACH)), constant_values=-1)
+    win = lax.dynamic_slice_in_dim(padded, lax.axis_index("seq") * block, block + 2 * REACH, 1)
+    return win[:, :, None], win.reshape(2, 256, 4), win
+
+
+def small_share(pool_taps, ln1_gain, ln1_bias, ln2_gain, ln2_bias):
+    rows = jnp.stack([ln1_gain, ln1_bias, ln2_gain, ln2_bias])
+    return jnp.concatenate(
+        [jnp.pad(pool_taps, ((0, 0), (0, 80))), jnp.pad(rows, ((0, 7), (0, 104)))], axis=0
+    )
+
+
+def gelu_both(u):
+    a, b = 0.7978845608028654, 0.044715
+    sq = u * u
+    t = jnp.tanh(a * u * (1.0 + b * sq))
+    half = 0.5 + 0.5 * t
+    grad = half + 0.5 * u * (1.0 - t * t) * (a + (3.0 * a * b) * sq)
+    return u * half, grad
+
+
+def pack_pair(lo, hi):
+    return jnp.concatenate([lo, hi], axis=0).astype(BF)
+
+
+def middle_kernel(
+    tok, att, dy, wo, wu, wd, gains,
+    o_out, o_gmid, o_gatt, o_ffn, o_sout, o_sums,
+    Tok, Att, Dy, Wo, Wu, Wd, mid, h2, DyT, H2T, y, gh2, act, gu, dw, gb, S, Sout, outv, sems,
+):
+    def copy(i, a, b):
+        return pltpu.make_async_copy(a, b, sems.at[i])
+
+    loads = [
+        copy(i, a, b)
+        for i, (a, b) in enumerate([(tok, Tok), (att, Att), (wo, Wo), (dy, Dy), (wu, Wu), (wd, Wd)])
+    ]
+    for ld in loads:
+        ld.start()
+    for ld in loads[:3]:
+        ld.wait()
+
+    def first(i, carry):
+        rows = pl.ds(pl.multiple_of(i * 128, 128), 128)
+        v = Tok[rows].astype(F32) + dg(Att[rows], Wo[...], NN)
+        mid[rows] = v
+        n, _ = norm_parts(v)
+        h2[rows] = (n * gains[7:8] + gains[8:9]).astype(BF)
+        return carry
+
+    lax.fori_loop(0, 8, first, 0)
+    loads[3].wait()
+
+    def flip(i, carry):
+        rows = pl.ds(pl.multiple_of(i * 128, 128), 128)
+        for j in range(3):
+            DyT[j * 256 : j * 256 + 256, rows] = Dy[rows, j * 256 : j * 256 + 256].T
+            H2T[j * 256 : j * 256 + 256, rows] = h2[rows, j * 256 : j * 256 + 256].T
+        return carry
+
+    lax.fori_loop(0, 8, flip, 0)
+    loads[4].wait()
+    loads[5].wait()
+
+    def chunk(j, carry):
+        lanes = [pl.ds(pl.multiple_of(j * 256 + h * 1536, 256), 256) for h in range(2)]
+
+        def elementwise(m, c):
+            rows = pl.ds(pl.multiple_of(m * 256, 256), 256)
+            for h in range(2):
+                u = dg(h2[rows], Wu[:, lanes[h]], NN)
+                ga = dg(Dy[rows], Wd[:, lanes[h]], NN)
+                a, da = gelu_both(u)
+                act[rows, h * 256 : h * 256 + 256] = a.astype(BF)
+                gu[rows, h * 256 : h * 256 + 256] = (ga * da).astype(BF)
+            return c
+
+        lax.fori_loop(0, 4, elementwise, 0)
+
+        def sums(m, c):
+            rows = pl.ds(pl.multiple_of(m * 256, 256), 256)
+            yy = dg(act[rows, 0:256], Wd[:, lanes[0]], NT) + dg(act[rows, 256:512], Wd[:, lanes[1]], NT)
+            gg = dg(gu[rows, 0:256], Wu[:, lanes[0]], NT) + dg(gu[rows, 256:512], Wu[:, lanes[1]], NT)
+
+            @pl.when(j == 0)
+            def _():
+                y[rows] = yy
+                gh2[rows] = gg
+
+            @pl.when(j > 0)
+            def _():
+                y[rows] += yy
+                gh2[rows] += gg
+
+            return c
+
+        lax.fori_loop(0, 4, sums, 0)
+        for which, (left, right) in enumerate(((H2T, gu), (DyT, act))):
+            def grads(m, c):
+                rows = pl.ds(pl.multiple_of(m * 256, 256), 256)
+                dw[rows, 0:512] = dg(left[rows], right[...], NN)
+                return c
+
+            lax.fori_loop(0, 3, grads, 0)
+            base = lax.rem(j, 2) * 1536 + which * 768
+
+            def share(s, c):
+                r0 = pl.multiple_of(s * 24, 8)
+                at = lambda q: pl.ds(pl.multiple_of(base + q * 256, 256), 256)
+                S[j // 2, s, :, at(0)] = dw[pl.ds(r0, 16), 0:256].astype(BF)
+                S[j // 2, s, :, at(1)] = dw[pl.ds(r0, 16), 256:512].astype(BF)
+                tail = pl.ds(pl.multiple_of(r0 + 16, 8), 8)
+                S[j // 2, s, :, at(2)] = pack_pair(dw[tail, 0:256], dw[tail, 256:512])
+                return c
+
+            lax.fori_loop(0, 32, share, 0)
+        return carry
+
+    lax.fori_loop(0, 6, chunk, 0)
+    store = [copy(6, S, o_ffn)]
+    store[0].start()
+
+    def last(i, carry):
+        rows = pl.ds(pl.multiple_of(i * 128, 128), 128)
+        v = mid[rows]
+        outv[rows] = (v + y[rows]).astype(BF)
+        n, rs = norm_parts(v)
+        g = gh2[rows]
+        e = g * gains[7:8]
+        gm = Dy[rows].astype(F32) + rs * (
+            e - jnp.mean(e, axis=-1, keepdims=True) - n * jnp.mean(e * n, axis=-1, keepdims=True)
+        )
+        y[rows] = gm
+        gb[rows] = gm.astype(BF)
+        a, b = carry
+        return a + jnp.sum((g * n).reshape(16, 8, 768), axis=0), b + jnp.sum(g.reshape(16, 8, 768), axis=0)
+
+    zero = jnp.zeros((8, 768), F32)
+    a, b = lax.fori_loop(0, 8, last, (zero, zero))
+    o_sums[0:1] = jnp.sum(a, axis=0, keepdims=True)
+    o_sums[1:2] = jnp.sum(b, axis=0, keepdims=True)
+    o_sums[2:8] = jnp.zeros((6, 768), F32)
+    store += [copy(7, outv, o_out), copy(8, y, o_gmid)]
+    for st in store[1:]:
+        st.start()
+
+    def flip_att(i, carry):
+        rows = pl.ds(pl.multiple_of(i * 128, 128), 128)
+        for j in range(3):
+            DyT[j * 256 : j * 256 + 256, rows] = Att[rows, j * 256 : j * 256 + 256].T
+        return carry
+
+    lax.fori_loop(0, 8, flip_att, 0)
+
+    def back(m, c):
+        rows = pl.ds(pl.multiple_of(m * 256, 256), 256)
+        h2[rows] = dg(gb[rows], Wo[...], NT).astype(BF)
+        return c
+
+    lax.fori_loop(0, 4, back, 0)
+    store.append(copy(9, h2, o_gatt))
+    store[-1].start()
+
+    def grads_out(m, c):
+        rows = pl.ds(pl.multiple_of(m * 256, 256), 256)
+        dw[rows] = dg(DyT[rows], gb[...], NN)
+        return c
+
+    lax.fori_loop(0, 3, grads_out, 0)
+
+    def share_out(s, c):
+        r0 = pl.multiple_of(s * 24, 8)
+        Sout[s, :, 0:768] = dw[pl.ds(r0, 16)].astype(BF)
+        tail = pl.ds(pl.multiple_of(r0 + 16, 8), 8)
+        Sout[s, :, 768:1152] = pack_pair(dw[tail, 0:384], dw[tail, 384:768])
+        return c
+
+    lax.fori_loop(0, 32, share_out, 0)
+    store.append(copy(10, Sout, o_sout))
+    store[-1].start()
+    for st in store:
+        st.wait()
+
+
+def middle_part(tok, att, dy, wo, wu, wd, gains):
+    sds = jax.ShapeDtypeStruct
+    n = 1024
+    vm = pltpu.VMEM
+    big = lambda dt: vm((n, 768), dt)
+    return pl.pallas_call(
+        middle_kernel,
+        out_shape=[
+            sds((n, 768), BF), sds((n, 768), F32), sds((n, 768), BF), sds((3, 32, 16, 3072), BF),
+            sds((32, 16, 1152), BF), sds((8, 768), F32),
+        ],
+        in_specs=[ANY] * 6 + [VM],
+        out_specs=[ANY] * 5 + [VM],
+        scratch_shapes=[
+            big(BF), big(BF), big(BF), vm((768, 768), BF), vm((768, 3072), BF), vm((768, 3072), BF),
+            big(F32), big(BF), vm((768, n), BF), vm((768, n), BF), big(F32), big(F32),
+            vm((n, 512), BF), vm((n, 512), BF), vm((768, 768), F32), big(BF),
+            vm((3, 32, 16, 3072), BF), vm((32, 16, 1152), BF), big(BF),
+            pltpu.SemaphoreType.DMA((11,)),
+        ],
+        compiler_params=pltpu.CompilerParams(vmem_limit_bytes=VMEM_LIMIT),
+    )(tok, att, dy, wo, wu, wd, gains)
+
+
+def pick_small(tg, lg, put):
+    lane = lax.broadcasted_iota(jnp.int32, (16, 128), 1)
+
+    def part(src, width, s):
+        at, off = divmod(width * s, 128)
+        v = src[:, at * 128 : at * 128 + 128]
+        v = pltpu.roll(v, 128 - off, 1) if off else v
+        if off + width > 128:
+            w = pltpu.roll(src[:, at * 128 + 128 : at * 128 + 256], 128 - off, 1)
+            v = jnp.where(lane < 128 - off, v, w)
+        return jnp.where(lane < width, v, 0.0)
+
+    for s in range(32):
+        put(s, (part(tg, 48, s) + part(lg, 24, s)).astype(BF))
+
+
+def back_kernel(
+    sffn, sout, q_in, kv_in, pe_in, bias_in, gatt_in, gmid_in, h1_in, tok_in, wq_in,
+    taps, gains, win4, sums2,
+    o_in, o_wq, o_wo, o_wu, o_wd, o_small,
+    Sf, So, Sq, Ss, Rf, Ro, Rq, Rs, gext, pstage, precv, hstage, hrecv, tg, lg,
+    send, recv, psend, prsem, local,
+):
+    me = where_am_i()
+    c, s, z, col = me["c"], me["s"], me["z"], me["col"]
+    has_left, has_right = s > 0, s < lax.axis_size("seq") - 1
+
+    def copy(i, a, b):
+        return pltpu.make_async_copy(a, b, local.at[i])
+
+    def cls(k):
+        if k < 3:
+            return Sf.at[k], Rf.at[k]
+        if k == 3:
+            return So, Ro
+        if k == 4:
+            return Sq.at[pl.ds(c * 16, 16)], Rq
+        return Ss.at[pl.ds(c * 16, 16)], Rs
+
+    def other(k):
+        start = (1 - c) * 16
+        if k < 3:
+            return sffn.at[k, pl.ds(start, 16)]
+        if k == 3:
+            return sout.at[pl.ds(start, 16)]
+        return (Sq if k == 4 else Ss).at[pl.ds(start, 16)]
+
+    def remote(k, src, slot, i, to):
+        return pltpu.make_async_remote_copy(
+            src_ref=src, dst_ref=slot, send_sem=send.at[k, i], recv_sem=recv.at[k, i],
+            device_id=to, device_id_type=MESH,
+        )
+
+    def swap(k):
+        return remote(k, other(k), cls(k)[1].at[pl.ds(0, 16)], 0, me["pd"])
+
+    def step_g(k, zz):
+        S, R = cls(k)
+        to = me["px"] if zz % 2 == 0 else me["py"]
+        return remote(k, S.at[zz * 4 + me["cold"]], R.at[16 + zz], 1 + zz, to)
+
+    def step_x(k, zz):
+        S, R = cls(k)
+        return remote(k, S.at[zz * 4 + me["colx"]], R.at[20 + zz], 5 + zz, me["px"])
+
+    def step_y(k, zz):
+        S, R = cls(k)
+        return remote(k, S.at[zz * 4 + me["coly"]], R.at[24 + zz], 9 + zz, me["py"])
+
+    def step_z(k, j):
+        S, R = cls(k)
+        zz = lax.rem(z + j, 4)
+        return remote(k, S.at[zz * 4 + col], R.at[27 + j], 12 + j, (c, zz * 4 + col))
+
+    def add(k, at, slots):
+        S, R = cls(k)
+        v = S[at].astype(F32) + R[at].astype(F32)
+        for slot in slots:
+            v = v + R[slot].astype(F32)
+        return v
+
+    def begin(k):
+        swap(k).start()
+
+    def do_g(k, zz):
+        if zz == 0:
+            swap(k).wait_recv()
+        at = zz * 4 + me["cold"]
+        cls(k)[0][at] = add(k, at, []).astype(BF)
+        step_g(k, zz).start()
+
+    def do_p(k, zz):
+        step_g(k, zz).wait_recv()
+        even = zz % 2 == 0
+        for at, step, has in ((zz * 4 + me["colx"], step_x, not even), (zz * 4 + me["coly"], step_y, even)):
+            cls(k)[0][at] = add(k, at, [16 + zz] if has else []).astype(BF)
+            step(k, zz).start()
+
+    def arrive(k, zz):
+        S, R = cls(k)
+        remote(k, S.at[0], R.at[20 + zz], 5 + zz, me["px"]).wait_recv()
+        remote(k, S.at[0], R.at[24 + zz], 9 + zz, me["py"]).wait_recv()
+
+    def do_c(k, j):
+        zz = lax.rem(z + j, 4)
+        arrive(k, zz)
+        at = zz * 4 + col
+        cls(k)[0][at] = add(k, at, [20 + zz, 24 + zz]).astype(BF)
+        step_z(k, j).start()
+
+    def total(k):
+        arrive(k, z)
+        for j in (1, 2, 3):
+            step_z(k, j).wait_recv()
+        return add(k, z * 4 + col, [20 + z, 24 + z, 28, 29, 30])
+
+    def drain(k):
+        swap(k).wait_send()
+        for zz in range(4):
+            step_g(k, zz).wait_send()
+            step_x(k, zz).wait_send()
+            step_y(k, zz).wait_send()
+        for j in (1, 2, 3):
+            step_z(k, j).wait_send()
+
+    def finish(k):
+        v = total(k)
+        if k < 3:
+            for i in range(2):
+                for ref, base in ((o_wu, i * 1536), (o_wd, i * 1536 + 768)):
+                    lo, hi = (2 * k + i) * 256, 1536 + (2 * k + i) * 256
+                    ref[0:16, lo : lo + 256] = v[:, base : base + 256]
+                    ref[0:16, hi : hi + 256] = v[:, base + 256 : base + 512]
+                    ref[16:24, lo : lo + 256] = v[0:8, base + 512 : base + 768]
+                    ref[16:24, hi : hi + 256] = v[8:16, base + 512 : base + 768]
+        elif k < 5:
+            ref = o_wo if k == 3 else o_wq
+            n = 768 if k == 3 else 2304
+            ref[0:16] = v[:, :n]
+            ref[16:24, : n // 2] = v[0:8, n:]
+            ref[16:24, n // 2 :] = v[8:16, n:]
+        else:
+            o_small[...] = v
+        drain(k)
+
+    def halo(src, dst, r, right, base):
+        i = base + r * 2 + int(right)
+        return pltpu.make_async_remote_copy(
+            src_ref=src.at[r, int(right)], dst_ref=dst.at[r, int(right)],
+            send_sem=psend.at[i], recv_sem=prsem.at[i],
+            device_id=(c, s + 1 if right else s - 1), device_id_type=MESH,
+        )
+
+    def both(src, dst, r, base, act):
+        @pl.when(has_right)
+        def _():
+            act(halo(src, dst, r, True, base))
+
+        @pl.when(has_left)
+        def _():
+            act(halo(src, dst, r, False, base))
+
+    def arrived(src, dst, r, base):
+        @pl.when(has_left)
+        def _():
+            halo(src, dst, r, True, base).wait_recv()
+
+        @pl.when(has_right)
+        def _():
+            halo(src, dst, r, False, base).wait_recv()
+
+    mine = [copy(k, sffn.at[k, pl.ds(c * 16, 16)], Sf.at[k]) for k in range(3)]
+    mine.append(copy(3, sout.at[pl.ds(c * 16, 16)], So))
+
+    def attention(q, kv, pe, bias, gatt, dkv, dpe, chunk):
+        loads = [
+            copy(4 + i, a, b)
+            for i, (a, b) in enumerate(
+                [(q_in, q), (kv_in, kv), (pe_in, pe), (bias_in, bias), (gatt_in, gatt)]
+            )
+        ]
+        for ld in loads + mine:
+            ld.start()
+        for r in range(2):
+            gext[r, 0:64, 0:768] = jnp.zeros((64, 768), BF)
+            gext[r, 576:640, 0:768] = jnp.zeros((64, 768), BF)
+
+        @pl.when(jnp.logical_not(has_left))
+        def _():
+            precv[:, 1] = jnp.zeros((2, 64, 1536), BF)
+            hrecv[:, 1] = jnp.zeros((2, 64, 768), BF)
+
+        @pl.when(jnp.logical_not(has_right))
+        def _():
+            precv[:, 0] = jnp.zeros((2, 64, 1536), BF)
+            hrecv[:, 0] = jnp.zeros((2, 64, 768), BF)
+
+        tg[...] = jnp.zeros((16, 1536), F32)
+        lg[...] = jnp.zeros((16, 768), F32)
+        greet(me, True)
+        for k in range(4):
+            begin(k)
+        for ld in loads + mine:
+            ld.wait()
+        blocks = [
+            (do_g, 0), (do_g, 1), (do_p, 0), (do_g, 2), (do_p, 1), (do_c, 0),
+            (do_g, 3), (do_p, 2), (do_c, 1), (do_p, 3), (do_c, 2), (do_c, 3),
+        ]
+        for r in range(2):
+            def heads(h, carry):
+                attend_back(q, kv, pe, bias, gatt, gext, dkv, dpe, r, h)
+                for i, (fn, k) in enumerate(blocks):
+                    @pl.when(r * 6 + h == i)
+                    def _():
+                        for j in (1, 2, 3) if fn is do_c else (0, 1, 2, 3):
+                            fn(k, j)
+
+                return carry
+
+            lax.fori_loop(0, 6, heads, 0)
+            for t in range(12):
+                lanes = slice(t * 128, t * 128 + 128)
+                pstage[r, 0, :, lanes] = dpe[r, t, 0:64].astype(BF)
+                pstage[r, 1, :, lanes] = dpe[r, t, 192:256].astype(BF)
+            both(pstage, precv, r, 0, lambda cp: cp.start())
+
+        for r in range(2):
+            anchor = win4[r, 64:192, 0:1]
+            same = [
+                (win4[r, a : a + 128, f : f + 1] == anchor).astype(F32)
+                for a, f in ((63, 2), (63, 3), (64, 0), (64, 1), (64, 2))
+            ]
+            arrived(pstage, precv, r, 0)
+
+            def pool_back(t, carry):
+                lanes = pl.ds(pl.multiple_of(t * 128, 128), 128)
+                low = dpe[r, t, 64:128] + precv[r, 1, :, lanes].astype(F32)
+                high = dpe[r, t, 128:192] + precv[r, 0, :, lanes].astype(F32)
+                gp = jnp.concatenate([low, high], axis=0)
+                chunk[...] = kv[r, :, lanes].astype(F32)
+                for i in range(5):
+                    at = pl.ds(62 + i, 128, stride=4)
+                    gm = gp * same[i]
+                    tg[i : i + 1, lanes] += jnp.sum(gm * chunk[at, :], axis=0, keepdims=True)
+                    dkv[r, t, at, :] += gm * taps[i : i + 1, lanes]
+                out_lanes = pl.ds(pl.multiple_of(768 + t * 128, 128), 128)
+                gext[r, :, out_lanes] = dkv[r, t].astype(BF)
+                return carry
+
+            lax.fori_loop(0, 12, pool_back, 0)
+
+    vm = pltpu.VMEM
+    pl.run_scoped(
+        attention,
+        vm((2, 512, 768), BF), vm((2, 640, 1536), BF), vm((2, 256, 1536), BF), vm((8, 416, 128), F32),
+        vm((2, 512, 768), BF), vm((2, 12, 640, 128), F32), vm((2, 12, 256, 128), F32), vm((640, 128), F32),
+    )
+
+    def projection(h1, h1t, wq, tok, gmid, gh, dw):
+        loads = [
+            copy(9 + i, a, b)
+            for i, (a, b) in enumerate([(h1_in, h1), (wq_in, wq), (tok_in, tok), (gmid_in, gmid)])
+        ]
+        for ld in loads:
+            ld.start()
+        loads[0].wait()
+        for r in range(2):
+            def flip(i, carry):
+                rows = pl.ds(pl.multiple_of(i * 128, 128), 128)
+                for j in range(3):
+                    h1t[r, j * 256 : j * 256 + 256, rows] = h1[r, rows, j * 256 : j * 256 + 256].T
+                return carry
+
+            lax.fori_loop(0, 5, flip, 0)
+
+        def grads(j, carry):
+            lanes = pl.ds(pl.multiple_of(j * 256, 256), 256)
+            dw[:, lanes] = dg(h1t[0], gext[0, :, lanes], NN) + dg(h1t[1], gext[1, :, lanes], NN)
+            return carry
+
+        lax.fori_loop(0, 9, grads, 0)
+
+        def share(i, carry):
+            r0 = pl.multiple_of(i * 24, 8)
+            Sq[i, :, 0:2304] = dw[pl.ds(r0, 16)].astype(BF)
+            tail = pl.ds(pl.multiple_of(r0 + 16, 8), 8)
+            Sq[i, :, 2304:3456] = pack_pair(dw[tail, 0:1152], dw[tail, 1152:2304])
+            return carry
+
+        lax.fori_loop(0, 32, share, 0)
+        begin(4)
+        for k in range(4):
+            finish(k)
+        for ld in loads[1:]:
+            ld.wait()
+        for r in range(2):
+            def rows_back(i, carry):
+                rows = pl.ds(pl.multiple_of(i * 128, 128), 128)
+                gh[r, rows] = dg(gext[r, rows], wq[...], NT)
+                return carry
+
+            lax.fori_loop(0, 5, rows_back, 0)
+            hstage[r, 0] = gh[r, 0:64].astype(BF)
+            hstage[r, 1] = gh[r, 576:640].astype(BF)
+            both(hstage, hrecv, r, 4, lambda cp: cp.start())
+            for zz in range(4):
+                (do_g if r == 0 else do_p)(4, zz)
+        for r in range(2):
+            arrived(hstage, hrecv, r, 4)
+            gh[r, 64:128] += hrecv[r, 1].astype(F32)
+            gh[r, 512:576] += hrecv[r, 0].astype(F32)
+        zero = jnp.zeros((8, 768), F32)
+        acc = (zero, zero)
+        for r in range(2):
+            def rows_norm(i, carry):
+                rows = pl.ds(pl.multiple_of(i * 128, 128), 128)
+                n, rs = norm_parts(tok[r, rows].astype(F32))
+                g = gh[r, pl.ds(pl.multiple_of(i * 128 + 64, 64), 128)]
+                e = g * gains[5:6]
+                gmid[r, rows] += rs * (
+                    e - jnp.mean(e, axis=-1, keepdims=True) - n * jnp.mean(e * n, axis=-1, keepdims=True)
+                )
+                a, b = carry
+                return a + jnp.sum((g * n).reshape(16, 8, 768), axis=0), b + jnp.sum(g.reshape(16, 8, 768), axis=0)
+
+            acc = lax.fori_loop(0, 4, rows_norm, acc)
+        out = copy(13, gmid, o_in)
+        out.start()
+        lg[5:6] = jnp.sum(acc[0], axis=0, keepdims=True)
+        lg[6:7] = jnp.sum(acc[1], axis=0, keepdims=True)
+        lg[7:9] = sums2[0:2]
+
+        def put(i, v):
+            Ss[i] = v
+
+        pick_small(tg, lg, put)
+        begin(5)
+        for j in (1, 2, 3):
+            do_c(4, j)
+        for zz in range(4):
+            do_g(5, zz)
+        for zz in range(4):
+            do_p(5, zz)
+        for j in (1, 2, 3):
+            do_c(5, j)
+        finish(4)
+        finish(5)
+        out.wait()
+
+    pl.run_scoped(
+        projection,
+        vm((2, 640, 768), BF), vm((2, 768, 640), BF), vm((768, 2304), BF), vm((2, 512, 768), BF),
+        vm((2, 512, 768), F32), vm((2, 640, 768), F32), vm((768, 2304), F32),
+    )
+    for r in range(2):
+        both(pstage, precv, r, 0, lambda cp: cp.wait_send())
+        both(hstage, hrecv, r, 4, lambda cp: cp.wait_send())
+
+
+def back_part(sffn, sout, q, kv, pe, bias, gatt, gmid, h1, tok, wq, taps, gains, win4, sums2):
+    sds = jax.ShapeDtypeStruct
+    vm, dma = pltpu.VMEM, pltpu.SemaphoreType.DMA
+    return pl.pallas_call(
+        back_kernel,
+        out_shape=[
+            sds((2, 512, 768), F32), sds((24, 2304), F32), sds((24, 768), F32), sds((24, 3072), F32),
+            sds((24, 3072), F32), sds((16, 128), F32),
+        ],
+        in_specs=[ANY] * 11 + [VM] * 4,
+        out_specs=[ANY] + [VM] * 5,
+        scratch_shapes=[
+            vm((3, 16, 16, 3072), BF), vm((16, 16, 1152), BF), vm((32, 16, 3456), BF), vm((32, 16, 128), BF),
+            vm((3, 31, 16, 3072), BF), vm((31, 16, 1152), BF), vm((31, 16, 3456), BF), vm((31, 16, 128), BF),
+            vm((2, 640, 2304), BF),
+            vm((2, 2, 64, 1536), BF), vm((2, 2, 64, 1536), BF), vm((2, 2, 64, 768), BF), vm((2, 2, 64, 768), BF),
+            vm((16, 1536), F32), vm((16, 768), F32),
+            dma((6, 16)), dma((6, 16)), dma((8,)), dma((8,)), dma((14,)),
+        ],
+        compiler_params=pltpu.CompilerParams(collective_id=1, has_side_effects=True, vmem_limit_bytes=VMEM_LIMIT),
+    )(sffn, sout, q, kv, pe, bias, gatt, gmid, h1, tok, wq, taps, gains, win4, sums2)
 
 
 def with_halo(x, sides, width):
@@ -30,13 +1131,13 @@
 
 
 def pool_local(extended, taps_in, seg_window):
-    block_rows = extended.shape[0] - 2 * LOCAL_HALF
-    anchors = seg_window[POOL_REACH : POOL_REACH + block_rows : 4]
+    block_rows = extended.shape[0] - 2 * NEAR
+    anchors = seg_window[REACH : REACH + block_rows : 4]
     pooled = jnp.zeros((block_rows // 4, extended.shape[1]), jnp.float32)
     for offset in range(5):
-        start_row = LOCAL_HALF - 2 + offset
+        start_row = NEAR - 2 + offset
         picked = extended[start_row : start_row + block_rows : 4]
-        seg_start = POOL_REACH - 2 + offset
+        seg_start = REACH - 2 + offset
         same_doc = (seg_window[seg_start : seg_start + block_rows : 4] == anchors).astype(
             jnp.float32
         )
@@ -45,16 +1146,16 @@
 
 
 def window_masks(seg_window, block_rows):
-    seg_query = seg_window[POOL_REACH : POOL_REACH + block_rows]
-    seg_key = seg_window[POOL_REACH - LOCAL_HALF : POOL_REACH + block_rows + LOCAL_HALF]
-    seg_pool = seg_window[0 : block_rows + 2 * POOL_REACH : 4]
+    seg_query = seg_window[REACH : REACH + block_rows]
+    seg_key = seg_window[REACH - NEAR : REACH + block_rows + NEAR]
+    seg_pool = seg_window[0 : block_rows + 2 * REACH : 4]
     q_index = jnp.arange(block_rows, dtype=jnp.int32)
     k_index = jnp.arange(seg_key.shape[0], dtype=jnp.int32)
     p_index = jnp.arange(seg_pool.shape[0], dtype=jnp.int32)
-    near_mask = (jnp.abs(q_index[:, None] - k_index[None, :] + LOCAL_HALF) <= LOCAL_HALF) & (
+    near_mask = (jnp.abs(q_index[:, None] - k_index[None, :] + NEAR) <= NEAR) & (
         seg_query[:, None] == seg_key[None, :]
     )
-    far_mask = (jnp.abs(4 * p_index[None, :] - POOL_REACH - q_index[:, None]) <= POOL_REACH) & (
+    far_mask = (jnp.abs(4 * p_index[None, :] - REACH - q_index[:, None]) <= REACH) & (
         seg_query[:, None] == seg_pool[None, :]
     )
     return (near_mask, far_mask)
@@ -107,7 +1208,7 @@
 ):
     block_rows = tokens.shape[1]
     model_width = tokens.shape[2]
-    pool_half = POOL_REACH // 4
+    pool_half = REACH // 4
     score_scale = HEAD ** (-0.5)
     offset_tokens = lax.axis_index("seq") * block_rows
     outputs = []
@@ -129,9 +1230,9 @@
             gathered
         )
         seg_row = segments[micro_step]
-        seg_padded = jnp.pad(seg_row, (POOL_REACH, POOL_REACH), constant_values=-1)
+        seg_padded = jnp.pad(seg_row, (REACH, REACH), constant_values=-1)
         seg_window = lax.dynamic_slice_in_dim(
-            seg_padded, offset_tokens, block_rows + 2 * POOL_REACH, 0
+            seg_padded, offset_tokens, block_rows + 2 * REACH, 0
         )
         near_mask, far_mask = window_masks(seg_window, block_rows)
         inputs = tokens[micro_step].astype(jnp.float32)
@@ -145,7 +1246,7 @@
         )
         queries = projected[:, :model_width].reshape(block_rows, HEADS, HEAD)
         key_value = projected[:, model_width:]
-        extended = with_halo(key_value, (("seq", 0),), LOCAL_HALF)
+        extended = with_halo(key_value, (("seq", 0),), NEAR)
         ext_float = extended.astype(jnp.float32)
         taps_float = taps.astype(jnp.float32)
         pooled = pool_local(ext_float, taps_float, seg_window).astype(jnp.bfloat16)
@@ -272,12 +1373,12 @@
         grad_ext_pool, grad_taps = pool_back(grad_pooled)
         grad_extended = grad_extended + grad_ext_pool
         token_edges = jnp.concatenate(
-            [grad_extended[:LOCAL_HALF], grad_extended[-LOCAL_HALF:]], axis=0
+            [grad_extended[:NEAR], grad_extended[-NEAR:]], axis=0
         )
         token_returned = with_halo(
-            token_edges.astype(jnp.bfloat16), (("seq", 0),), LOCAL_HALF
+            token_edges.astype(jnp.bfloat16), (("seq", 0),), NEAR
         ).astype(token_edges.dtype)
-        grad_kv = add_rims(grad_extended[LOCAL_HALF:-LOCAL_HALF], token_returned, LOCAL_HALF)
+        grad_kv = add_rims(grad_extended[NEAR:-NEAR], token_returned, NEAR)
         grad_projected = jnp.concatenate(
             [grad_queries.reshape(block_rows, model_width), grad_kv], axis=1
         ).astype(jnp.bfloat16)
@@ -316,37 +1417,36 @@
     )
 
 
+def chained(
+    tokens, segments, cotangent, ln1_gain, ln1_bias, w_qkv, pool_taps, w_out, ln2_gain, ln2_bias, w_up, w_down,
+):
+    winc, win4, winr = windows(segments)
+    small = small_share(pool_taps, ln1_gain, ln1_bias, ln2_gain, ln2_bias)
+    wq, wo, wu, wd, taps, gains, h1, q, kv, pe, att, bias = front(
+        tokens, winc, win4, winr, w_qkv, w_out, w_up, w_down.T, small
+    )
+    flat = (1024, 768)
+    out, gmid, gatt, sffn, sout, sums2 = middle_part(
+        tokens.reshape(flat), att.reshape(flat), cotangent.reshape(flat), wo, wu, wd, gains
+    )
+    split = (2, 512, 768)
+    g_in, g_wq, g_wo, g_wu, g_wd, g_small = back_part(
+        sffn, sout, q, kv, pe, bias, gatt.reshape(split), gmid.reshape(split), h1, tokens, wq, taps, gains, win4, sums2
+    )
+    return (
+        out.reshape(split), g_in, g_small[5, :24], g_small[6, :24], g_wq, g_small[0:5, :48], g_wo,
+        g_small[7, :24], g_small[8, :24], g_wu, g_wd.T,
+    )
+
+
 def solution(mesh):
-    placed = (
-        P("dp", "seq", None),
-        P("dp", None),
-        P("dp", "seq", None),
-        P(("dp", "seq")),
-        P(("dp", "seq")),
-        P(("dp", "seq"), None),
-        P(None, ("dp", "seq")),
-        P(("dp", "seq"), None),
-        P(("dp", "seq")),
-        P(("dp", "seq")),
-        P(("dp", "seq"), None),
-        P(None, ("dp", "seq")),
-    )
+    both = ("dp", "seq")
+    row, tok, first, second = P(both), P("dp", "seq", None), P(both, None), P(None, both)
+    small_mesh = mesh.shape["dp"] == 2 and mesh.shape["seq"] == 16
     return jax.shard_map(
-        shards,
+        chained if small_mesh else shards,
         mesh=mesh,
-        in_specs=placed,
-        out_specs=(
-            P("dp", "seq", None),
-            P("dp", "seq", None),
-            P(("dp", "seq")),
-            P(("dp", "seq")),
-            P(("dp", "seq"), None),
-            P(None, ("dp", "seq")),
-            P(("dp", "seq"), None),
-            P(("dp", "seq")),
-            P(("dp", "seq")),
-            P(("dp", "seq"), None),
-            P(None, ("dp", "seq")),
-        ),
+        in_specs=(tok, P("dp", None), tok, row, row, first, second, first, row, row, first, second),
+        out_specs=(tok, tok, row, row, first, second, first, row, row, first, second),
         check_vma=False,
     )

time: 1180 us -> 327 us (0.28); the launches traced: 1170 us -> 326 us
  waiting for transfers between devices: 361 us -> 0 us
  Pallas kernels: 0 us -> 311 us
  matrix products: 242 us -> 0 us
  local copies, waits for them, and re-layouts: 210 us -> 12.9 us
  blocking collectives: 155 us -> 0 us
  other arithmetic: 131 us -> 2 us
  starting transfers between devices: 49.5 us -> 0 us
  between operations: 17.1 us -> 0.69 us
    reduce_scatter x4 -> x0, waiting for transfers between devices: 352 us -> none  [the longest x1 142 us: shards(): lax.psum_scatter(grad_upw, ('dp', 'seq'), scatter_dimension=0, tiled=True)]
    pallas_call x0 -> x3, Pallas kernels: none -> 311 us  [the longest x1 130 us: back_part(): pl.pallas_call(back_kernel, out_shape=[sds((2, 512, 768), F32), sds((24,...]
    dot_general x48 -> x0, matrix products: 242 us -> none  [the longest x2 25.7 us: shards(): jnp.einsum('qhd,khd->hqk', grad_mixed, near_values, preferred_element_typ...]
    unnamed x2 -> x0, blocking collectives: 89.2 us -> none
    slice x54 -> x1, local copies, waits for them, and re-layouts: 85.5 us -> 1.27 us  [chained(): g_small[0:5, :48]]
    pad x10 -> x0, local copies, waits for them, and re-layouts: 78.2 us -> none  [pool_local(): picked = extended[start_row:start_row + block_rows:4]]
    all_gather x1 -> x0, blocking collectives: 66.1 us -> none  [shards(): lax.all_gather(pool_taps, ('dp', 'seq'), axis=1, tiled=True)]
    ppermute x16 -> x0, starting transfers between devices: 49.2 us -> none  [the longest x8 38.5 us: with_halo(): before = lax.ppermute(last, axis, up)]
  transfers between devices with their start and end apart: 25 -> 0, of which waited for: 6 -> 0; matrix products, arithmetic and copies ran while one was open for 36% -> 0% of each run, Pallas kernels for 0% -> 0%
where the time goes in v1:
time: 327 us; the launch traced here: 326 us
  Pallas kernels  311 us (95%)
  local copies, waits for them, and re-layouts  12.9 us (4%)
    pallas_call x1, Pallas kernels, back_part(): pl.pallas_call(back_kernel, out_shape=[sds((2, 512, 768), F32), sds((24,...  130 us
    pallas_call x1, Pallas kernels, front(): pl.pallas_call(front_kernel, out_shape=[sds(sh, dt) for sh, dt in shapes]...  105 us
    pallas_call x1, Pallas kernels, middle_part(): pl.pallas_call(middle_kernel, out_shape=[sds((n, 768), BF), sds((n, 768),...  76.3 us
    unnamed x15, local copies, waits for them, and re-layouts  6.6 us

profile of v1, /device:TPU:0, one launch (start us, length us, event | category | flops | bytes accessed | tf_op | source)
XLA Modules:
  0.0 326.4 jit_solution(15685366661415716096)
XLA Ops:
  0.6 0.7 fusion.10
  1.4 1.3 fusion.6.small
  2.6 0.7 pad_dynamic-slice_fusion.winr
  3.3 0.0 copy-start.3
  3.4 0.7 fusion.14
  4.1 1.0 reshape.44.win4
  5.0 1.3 copy.23.winc
  6.4 0.0 copy-done.3
  6.4 104.7 %shard_map.203 = (bf16[768,2304]{1,0:T(8,128)(2,1)}, bf16[768,768]{1,0:T(8,128)(2,1)}, bf16[768,3072]{1,0:T(8,128)(2,1)}, bf16[768,3072]{1,0:T(8,128)(2,1)}, f32...) custom-call(bf16[2,512,768]{2,1,0:T(8,128)(2,1)} %tok_in.1, ...), custom_call_target="tpu_custom_call" | custom-call | tf_op jit(solution)/shard_map/pallas_call | solution.py:511
  111.1 76.3 %shard_map.204 = (bf16[1024,768]{1,0:T(8,128)(2,1)}, f32[1024,768]{1,0:T(8,128)}, bf16[1024,768]{1,0:T(8,128)(2,1)}, bf16[3,32,16,3072]{3,2,1,0:T(8,128)(2,1)}, ...) custom-call(bf16[1024,768]{1,0:T(8,128)(2,1)} %bitcast.22, bf16[1024,768]{1,0:T(8,128)(2,1)} %bitcast.26, ...), custom_call_target="tpu_custom_call" | custom-call | tf_op jit(solution)/shard_map/pallas_call | solution.py:712
  187.4 129.8 %shard_map.205 = (f32[2,512,768]{2,1,0:T(8,128)}, f32[24,2304]{1,0:T(8,128)}, f32[24,768]{1,0:T(8,128)}, f32[24,3072]{1,0:T(8,128)}, f32[24,3072]{1,0:T(8,128)}, /*index=5*/f32[16,128]{1,0:T(8,128)}) custom-call(bf16[3,32,16,3072]{3,2,1,0:T(8,128)(2,1)} %get-tuple-element.41.sffn, bf16[32,16,1152]{2,1,0:T(8,128)(2,1)} %get-tuple-element.42.sout, ...), custom_call_target="tpu_custom_call" | custom-call | tf_op jit(solution)/shard_map/pallas_call | solution.py:1093
  317.2 1.3 slice_bitcast_fusion
  318.5 1.3 slice.17
  319.8 0.0 copy-start.2
  319.8 0.0 copy-start.4
  319.8 0.0 copy-start.1
  319.8 0.0 copy-start
  319.8 3.8 %copy.29 = f32[2,512,768]{2,1,0:T(8,128)} copy(f32[2,512,768]{2,1,0:T(8,128)} %get-tuple-element.75) | data formatting | bytes 6291456
  323.7 0.0 copy-done.2
  323.7 0.7 copy.30
  324.4 0.0 copy-done.4
  324.4 0.6 copy.31
  325.0 0.0 copy-done.1
  325.0 0.7 copy.32
  325.7 0.0 copy-done
  325.7 0.7 copy.33
Async XLA Ops:
  3.3 3.0 copy-start.3
  319.8 3.8 %copy-start.2 = (f32[24,2304]{1,0:T(8,128)S(1)}, f32[24,2304]{1,0:T(8,128)}, u32[]{:S(2)}) copy-start(f32[24,2304]{1,0:T(8,128)} %get-tuple-element.78) | copy-start | bytes 663556
  319.8 4.5 %copy-start.4 = (f32[24,768]{1,0:T(8,128)S(1)}, f32[24,768]{1,0:T(8,128)}, u32[]{:S(2)}) copy-start(f32[24,768]{1,0:T(8,128)} %get-tuple-element.80) | copy-start | bytes 221188
  319.8 5.2 %copy-start.1 = (f32[24,3072]{1,0:T(8,128)S(1)}, f32[24,3072]{1,0:T(8,128)}, u32[]{:S(2)}) copy-start(f32[24,3072]{1,0:T(8,128)} %get-tuple-element.83) | copy-start | bytes 884740
  319.8 5.9 %copy-start = (f32[24,3072]{1,0:T(8,128)S(1)}, f32[24,3072]{1,0:T(8,128)}, u32[]{:S(2)}) copy-start(f32[24,3072]{1,0:T(8,128)} %get-tuple-element.58) | copy-start | bytes 884740

commit v2 on v1

--- a/solution.py
+++ b/solution.py
@@ -141,7 +141,7 @@
         dpe[r, part] = jnp.zeros((256, 128), F32)
     for b in range(4):
         n, f, i = slice(b * 128, b * 128 + 256), slice(b * 32, b * 32 + 160), slice(b * 128, b * 128 + 128)
-        q2, g2 = pair_rows(q[r, i, kl]), pair_rows(g[r, i, kl])
+        q2, g2 = pair_rows(q[r, i, kl]), pair_rows(g[r * 512 + b * 128 : r * 512 + b * 128 + 128, kl])
         kn, vn, kf, vf = kv[r, n, kl], kv[r, n, vl], pe[r, f, kl], pe[r, f, vl]
         e, rt = softmax_block(q2, kn, kf, bias[r * 4 + b])
         p = e * rt
@@ -155,7 +155,7 @@
         dpe[r, h, f] += dk[256:]
         dpe[r, 6 + h, f] += dv[256:]
         dqt = dg(jnp.concatenate([kn, kf], axis=0), ds, TN)
-        gext[r, 64 + b * 128 : 192 + b * 128, kl] = (pair_out(dqt) * HEAD**-0.5).astype(BF)
+        gext[r * 640 + 64 + b * 128 : r * 640 + 192 + b * 128, kl] = (pair_out(dqt) * HEAD**-0.5).astype(BF)
 
 
 def norm_parts(v):
@@ -177,20 +177,29 @@
             put(k, lo, jnp.concatenate([grab(name, 16, 24, u), grab(name, 16, 24, u + half)], axis=0))
 
 
+def hidden_place(n):
+    half, r = divmod(n, 1536)
+    return (r // 256) * 512 + half * 256 + r % 256
+
+
 def unpack(name, got, dst):
     half = units(name) // 2
 
-    def pair(i, carry):
-        rows = pl.ds(pl.multiple_of(48 * i, 16), 48)
+    def pair(p, carry):
+        rows = pl.ds(pl.multiple_of(48 * p, 16), 48)
         for u in range(units(name)):
             k, lo = spot(name, u)
             kt, lt = spot(name, units(name) + u % half)
             cut = slice(0, 8) if u < half else slice(8, 16)
-            parts = []
-            for j in (0, 1):
-                parts.append(got[k, 2 * i + j, :, lo : lo + UNIT])
-                parts.append(got[kt, 2 * i + j, :, lt : lt + UNIT][cut])
-            dst[rows, u * UNIT : (u + 1) * UNIT] = jnp.concatenate(parts, axis=0)
+            hidden = name in ("up", "down")
+            for i in range(0, UNIT, 128) if hidden else (0,):
+                n = 128 if hidden else UNIT
+                to = hidden_place(u * UNIT + i) if hidden else u * UNIT
+                parts = []
+                for j in (0, 1):
+                    parts.append(got[k, 2 * p + j, :, lo + i : lo + i + n])
+                    parts.append(got[kt, 2 * p + j, :, lt + i : lt + i + n][cut])
+                dst[rows, to : to + n] = jnp.concatenate(parts, axis=0)
         return carry
 
     lax.fori_loop(0, 16, pair, 0)
@@ -545,189 +554,6 @@
     return jnp.concatenate([lo, hi], axis=0).astype(BF)
 
 
-def middle_kernel(
-    tok, att, dy, wo, wu, wd, gains,
-    o_out, o_gmid, o_gatt, o_ffn, o_sout, o_sums,
-    Tok, Att, Dy, Wo, Wu, Wd, mid, h2, DyT, H2T, y, gh2, act, gu, dw, gb, S, Sout, outv, sems,
-):
-    def copy(i, a, b):
-        return pltpu.make_async_copy(a, b, sems.at[i])
-
-    loads = [
-        copy(i, a, b)
-        for i, (a, b) in enumerate([(tok, Tok), (att, Att), (wo, Wo), (dy, Dy), (wu, Wu), (wd, Wd)])
-    ]
-    for ld in loads:
-        ld.start()
-    for ld in loads[:3]:
-        ld.wait()
-
-    def first(i, carry):
-        rows = pl.ds(pl.multiple_of(i * 128, 128), 128)
-        v = Tok[rows].astype(F32) + dg(Att[rows], Wo[...], NN)
-        mid[rows] = v
-        n, _ = norm_parts(v)
-        h2[rows] = (n * gains[7:8] + gains[8:9]).astype(BF)
-        return carry
-
-    lax.fori_loop(0, 8, first, 0)
-    loads[3].wait()
-
-    def flip(i, carry):
-        rows = pl.ds(pl.multiple_of(i * 128, 128), 128)
-        for j in range(3):
-            DyT[j * 256 : j * 256 + 256, rows] = Dy[rows, j * 256 : j * 256 + 256].T
-            H2T[j * 256 : j * 256 + 256, rows] = h2[rows, j * 256 : j * 256 + 256].T
-        return carry
-
-    lax.fori_loop(0, 8, flip, 0)
-    loads[4].wait()
-    loads[5].wait()
-
-    def chunk(j, carry):
-        lanes = [pl.ds(pl.multiple_of(j * 256 + h * 1536, 256), 256) for h in range(2)]
-
-        def elementwise(m, c):
-            rows = pl.ds(pl.multiple_of(m * 256, 256), 256)
-            for h in range(2):
-                u = dg(h2[rows], Wu[:, lanes[h]], NN)
-                ga = dg(Dy[rows], Wd[:, lanes[h]], NN)
-                a, da = gelu_both(u)
-                act[rows, h * 256 : h * 256 + 256] = a.astype(BF)
-                gu[rows, h * 256 : h * 256 + 256] = (ga * da).astype(BF)
-            return c
-
-        lax.fori_loop(0, 4, elementwise, 0)
-
-        def sums(m, c):
-            rows = pl.ds(pl.multiple_of(m * 256, 256), 256)
-            yy = dg(act[rows, 0:256], Wd[:, lanes[0]], NT) + dg(act[rows, 256:512], Wd[:, lanes[1]], NT)
-            gg = dg(gu[rows, 0:256], Wu[:, lanes[0]], NT) + dg(gu[rows, 256:512], Wu[:, lanes[1]], NT)
-
-            @pl.when(j == 0)
-            def _():
-                y[rows] = yy
-                gh2[rows] = gg
-
-            @pl.when(j > 0)
-            def _():
-                y[rows] += yy
-                gh2[rows] += gg
-
-            return c
-
-        lax.fori_loop(0, 4, sums, 0)
-        for which, (left, right) in enumerate(((H2T, gu), (DyT, act))):
-            def grads(m, c):
-                rows = pl.ds(pl.multiple_of(m * 256, 256), 256)
-                dw[rows, 0:512] = dg(left[rows], right[...], NN)
-                return c
-
-            lax.fori_loop(0, 3, grads, 0)
-            base = lax.rem(j, 2) * 1536 + which * 768
-
-            def share(s, c):
-                r0 = pl.multiple_of(s * 24, 8)
-                at = lambda q: pl.ds(pl.multiple_of(base + q * 256, 256), 256)
-                S[j // 2, s, :, at(0)] = dw[pl.ds(r0, 16), 0:256].astype(BF)
-                S[j // 2, s, :, at(1)] = dw[pl.ds(r0, 16), 256:512].astype(BF)
-                tail = pl.ds(pl.multiple_of(r0 + 16, 8), 8)
-                S[j // 2, s, :, at(2)] = pack_pair(dw[tail, 0:256], dw[tail, 256:512])
-                return c
-
-            lax.fori_loop(0, 32, share, 0)
-        return carry
-
-    lax.fori_loop(0, 6, chunk, 0)
-    store = [copy(6, S, o_ffn)]
-    store[0].start()
-
-    def last(i, carry):
-        rows = pl.ds(pl.multiple_of(i * 128, 128), 128)
-        v = mid[rows]
-        outv[rows] = (v + y[rows]).astype(BF)
-        n, rs = norm_parts(v)
-        g = gh2[rows]
-        e = g * gains[7:8]
-        gm = Dy[rows].astype(F32) + rs * (
-            e - jnp.mean(e, axis=-1, keepdims=True) - n * jnp.mean(e * n, axis=-1, keepdims=True)
-        )
-        y[rows] = gm
-        gb[rows] = gm.astype(BF)
-        a, b = carry
-        return a + jnp.sum((g * n).reshape(16, 8, 768), axis=0), b + jnp.sum(g.reshape(16, 8, 768), axis=0)
-
-    zero = jnp.zeros((8, 768), F32)
-    a, b = lax.fori_loop(0, 8, last, (zero, zero))
-    o_sums[0:1] = jnp.sum(a, axis=0, keepdims=True)
-    o_sums[1:2] = jnp.sum(b, axis=0, keepdims=True)
-    o_sums[2:8] = jnp.zeros((6, 768), F32)
-    store += [copy(7, outv, o_out), copy(8, y, o_gmid)]
-    for st in store[1:]:
-        st.start()
-
-    def flip_att(i, carry):
-        rows = pl.ds(pl.multiple_of(i * 128, 128), 128)
-        for j in range(3):
-            DyT[j * 256 : j * 256 + 256, rows] = Att[rows, j * 256 : j * 256 + 256].T
-        return carry
-
-    lax.fori_loop(0, 8, flip_att, 0)
-
-    def back(m, c):
-        rows = pl.ds(pl.multiple_of(m * 256, 256), 256)
-        h2[rows] = dg(gb[rows], Wo[...], NT).astype(BF)
-        return c
-
-    lax.fori_loop(0, 4, back, 0)
-    store.append(copy(9, h2, o_gatt))
-    store[-1].start()
-
-    def grads_out(m, c):
-        rows = pl.ds(pl.multiple_of(m * 256, 256), 256)
-        dw[rows] = dg(DyT[rows], gb[...], NN)
-        return c
-
-    lax.fori_loop(0, 3, grads_out, 0)
-
-    def share_out(s, c):
-        r0 = pl.multiple_of(s * 24, 8)
-        Sout[s, :, 0:768] = dw[pl.ds(r0, 16)].astype(BF)
-        tail = pl.ds(pl.multiple_of(r0 + 16, 8), 8)
-        Sout[s, :, 768:1152] = pack_pair(dw[tail, 0:384], dw[tail, 384:768])
-        return c
-
-    lax.fori_loop(0, 32, share_out, 0)
-    store.append(copy(10, Sout, o_sout))
-    store[-1].start()
-    for st in store:
-        st.wait()
-
-
-def middle_part(tok, att, dy, wo, wu, wd, gains):
-    sds = jax.ShapeDtypeStruct
-    n = 1024
-    vm = pltpu.VMEM
-    big = lambda dt: vm((n, 768), dt)
-    return pl.pallas_call(
-        middle_kernel,
-        out_shape=[
-            sds((n, 768), BF), sds((n, 768), F32), sds((n, 768), BF), sds((3, 32, 16, 3072), BF),
-            sds((32, 16, 1152), BF), sds((8, 768), F32),
-        ],
-        in_specs=[ANY] * 6 + [VM],
-        out_specs=[ANY] * 5 + [VM],
-        scratch_shapes=[
-            big(BF), big(BF), big(BF), vm((768, 768), BF), vm((768, 3072), BF), vm((768, 3072), BF),
-            big(F32), big(BF), vm((768, n), BF), vm((768, n), BF), big(F32), big(F32),
-            vm((n, 512), BF), vm((n, 512), BF), vm((768, 768), F32), big(BF),
-            vm((3, 32, 16, 3072), BF), vm((32, 16, 1152), BF), big(BF),
-            pltpu.SemaphoreType.DMA((11,)),
-        ],
-        compiler_params=pltpu.CompilerParams(vmem_limit_bytes=VMEM_LIMIT),
-    )(tok, att, dy, wo, wu, wd, gains)
-
-
 def pick_small(tg, lg, put):
     lane = lax.broadcasted_iota(jnp.int32, (16, 128), 1)
 
@@ -745,10 +571,10 @@
 
 
 def back_kernel(
-    sffn, sout, q_in, kv_in, pe_in, bias_in, gatt_in, gmid_in, h1_in, tok_in, wq_in,
-    taps, gains, win4, sums2,
-    o_in, o_wq, o_wo, o_wu, o_wd, o_small,
-    Sf, So, Sq, Ss, Rf, Ro, Rq, Rs, gext, pstage, precv, hstage, hrecv, tg, lg,
+    tok_in, att_in, dy_in, wo_in, wu_in, wd_in,
+    q_in, kv_in, pe_in, bias_in, h1_in, wq_in, taps, gains, win4,
+    o_out, o_gmid, o_in, o_wq, o_wo, o_wu, o_wd, o_small,
+    Sf, So, Ss, Rf, Ro, Rq, Rs, gatt, pstage, precv, hstage, hrecv, tg, lg,
     send, recv, psend, prsem, local,
 ):
     me = where_am_i()
@@ -758,22 +584,22 @@
     def copy(i, a, b):
         return pltpu.make_async_copy(a, b, local.at[i])
 
+    late = []
+
     def cls(k):
         if k < 3:
-            return Sf.at[k], Rf.at[k]
+            return Sf.at[k, pl.ds(c * 16, 16)], Rf.at[k]
         if k == 3:
-            return So, Ro
+            return So.at[pl.ds(c * 16, 16)], Ro
         if k == 4:
-            return Sq.at[pl.ds(c * 16, 16)], Rq
+            return late[0].at[pl.ds(c * 16, 16)], Rq
         return Ss.at[pl.ds(c * 16, 16)], Rs
 
     def other(k):
         start = (1 - c) * 16
         if k < 3:
-            return sffn.at[k, pl.ds(start, 16)]
-        if k == 3:
-            return sout.at[pl.ds(start, 16)]
-        return (Sq if k == 4 else Ss).at[pl.ds(start, 16)]
+            return Sf.at[k, pl.ds(start, 16)]
+        return (So, late[0] if late else None, Ss)[k - 3].at[pl.ds(start, 16)]
 
     def remote(k, src, slot, i, to):
         return pltpu.make_async_remote_copy(
@@ -865,10 +691,11 @@
                     ref[16:24, hi : hi + 256] = v[8:16, base + 512 : base + 768]
         elif k < 5:
             ref = o_wo if k == 3 else o_wq
-            n = 768 if k == 3 else 2304
-            ref[0:16] = v[:, :n]
-            ref[16:24, : n // 2] = v[0:8, n:]
-            ref[16:24, n // 2 :] = v[8:16, n:]
+            for i in range(1 if k == 3 else 3):
+                at, frm = i * 768, i * 1152
+                ref[0:16, at : at + 768] = v[:, frm : frm + 768]
+                ref[16:24, at : at + 384] = v[0:8, frm + 768 : frm + 1152]
+                ref[16:24, at + 384 : at + 768] = v[8:16, frm + 768 : frm + 1152]
         else:
             o_small[...] = v
         drain(k)
@@ -899,52 +726,162 @@
         def _():
             halo(src, dst, r, False, base).wait_recv()
 
-    mine = [copy(k, sffn.at[k, pl.ds(c * 16, 16)], Sf.at[k]) for k in range(3)]
-    mine.append(copy(3, sout.at[pl.ds(c * 16, 16)], So))
-
-    def attention(q, kv, pe, bias, gatt, dkv, dpe, chunk):
+    @pl.when(jnp.logical_not(has_left))
+    def _():
+        precv[:, 1] = jnp.zeros((2, 64, 1536), BF)
+        hrecv[:, 1] = jnp.zeros((2, 64, 768), BF)
+
+    @pl.when(jnp.logical_not(has_right))
+    def _():
+        precv[:, 0] = jnp.zeros((2, 64, 1536), BF)
+        hrecv[:, 0] = jnp.zeros((2, 64, 768), BF)
+
+    tg[...] = jnp.zeros((16, 1536), F32)
+    lg[...] = jnp.zeros((16, 768), F32)
+    greet(me, True)
+
+    def run(plan, at):
+        for i, todo in plan.items():
+            @pl.when(at == i)
+            def _():
+                for fn, k in todo:
+                    if fn is begin:
+                        begin(k)
+                    else:
+                        for j in (1, 2, 3) if fn is do_c else (0, 1, 2, 3):
+                            fn(k, j)
+
+    def feed_forward(Tok, Att, Dy, Wo, Wu, Wd, mid, h2, DyT, H2T, y, gh2, act, gu):
+        loads = [
+            copy(i, a, b)
+            for i, (a, b) in enumerate(
+                [(tok_in, Tok), (att_in, Att), (wo_in, Wo), (dy_in, Dy), (wu_in, Wu), (wd_in, Wd)]
+            )
+        ]
+        for ld in loads:
+            ld.start()
+        y[...] = jnp.zeros((1024, 768), F32)
+        gh2[...] = jnp.zeros((1024, 768), F32)
+        for ld in loads[:3]:
+            ld.wait()
+        mid[...] = dg(Att[...], Wo[...], NN)
+
+        def first(i, carry):
+            rows = pl.ds(pl.multiple_of(i * 128, 128), 128)
+            v = Tok[rows].astype(F32) + mid[rows]
+            mid[rows] = v
+            n, _ = norm_parts(v)
+            h2[rows] = (n * gains[7:8] + gains[8:9]).astype(BF)
+            return carry
+
+        lax.fori_loop(0, 8, first, 0)
+        loads[3].wait()
+
+        def flip(i, carry):
+            rows = pl.ds(pl.multiple_of(i * 128, 128), 128)
+            for j in range(3):
+                cols = slice(j * 256, j * 256 + 256)
+                DyT[cols, rows] = Dy[rows, cols].T
+                H2T[cols, rows] = h2[rows, cols].T
+            return carry
+
+        lax.fori_loop(0, 8, flip, 0)
+        loads[4].wait()
+        loads[5].wait()
+        plan = {
+            5: [(begin, 0)], 6: [(do_g, 0)], 8: [(do_p, 0)], 9: [(do_c, 0)],
+            11: [(begin, 1)], 12: [(do_g, 1)], 14: [(do_p, 1)], 15: [(do_c, 1)], 17: [(begin, 2)],
+        }
+
+        def chunk(j, carry):
+            lanes = [pl.ds(pl.multiple_of(j * 512 + h * 256, 256), 256) for h in range(2)]
+            whole = pl.ds(pl.multiple_of(j * 512, 512), 512)
+            for m in range(2):
+                rows = slice(m * 512, m * 512 + 512)
+                for h in range(2):
+                    u = dg(h2[rows], Wu[:, lanes[h]], NN)
+                    ga = dg(Dy[rows], Wd[:, lanes[h]], NN)
+                    a, da = gelu_both(u)
+                    act[rows, h * 256 : h * 256 + 256] = a.astype(BF)
+                    gu[rows, h * 256 : h * 256 + 256] = (ga * da).astype(BF)
+            run(plan, j * 3)
+            y[...] += dg(act[...], Wd[:, whole], NT)
+            gh2[...] += dg(gu[...], Wu[:, whole], NT)
+            run(plan, j * 3 + 1)
+            for which, (left, right) in enumerate(((H2T, gu), (DyT, act))):
+                base = lax.rem(j, 2) * 1536 + which * 768
+                at = [pl.ds(pl.multiple_of(base + i * 256, 256), 256) for i in range(3)]
+                dws = dg(left[...], right[...], NN)
+                for i in range(32):
+                    head, tail = dws[i * 24 : i * 24 + 16].astype(BF), dws[i * 24 + 16 : i * 24 + 24]
+                    Sf[j // 2, i, :, at[0]] = head[:, 0:256]
+                    Sf[j // 2, i, :, at[1]] = head[:, 256:512]
+                    Sf[j // 2, i, :, at[2]] = pack_pair(tail[:, 0:256], tail[:, 256:512])
+            run(plan, j * 3 + 2)
+            return carry
+
+        lax.fori_loop(0, 6, chunk, 0)
+
+        def last(i, carry):
+            rows = pl.ds(pl.multiple_of(i * 128, 128), 128)
+            v = mid[rows]
+            Tok[rows] = (v + y[rows]).astype(BF)
+            n, rs = norm_parts(v)
+            g = gh2[rows]
+            e = g * gains[7:8]
+            gm = Dy[rows].astype(F32) + rs * (
+                e - jnp.mean(e, axis=-1, keepdims=True) - n * jnp.mean(e * n, axis=-1, keepdims=True)
+            )
+            y[rows] = gm
+            h2[rows] = gm.astype(BF)
+            a, b = carry
+            return a + jnp.sum((g * n).reshape(16, 8, 768), axis=0), b + jnp.sum(g.reshape(16, 8, 768), axis=0)
+
+        zero = jnp.zeros((8, 768), F32)
+        a, b = lax.fori_loop(0, 8, last, (zero, zero))
+        lg[7:8] = jnp.sum(a, axis=0, keepdims=True)
+        lg[8:9] = jnp.sum(b, axis=0, keepdims=True)
+        store = [copy(6, Tok, o_out), copy(7, y, o_gmid)]
+        for st in store:
+            st.start()
+
+        def flip_att(i, carry):
+            rows = pl.ds(pl.multiple_of(i * 128, 128), 128)
+            for j in range(3):
+                DyT[j * 256 : j * 256 + 256, rows] = Att[rows, j * 256 : j * 256 + 256].T
+            return carry
+
+        lax.fori_loop(0, 8, flip_att, 0)
+        gatt[...] = dg(h2[...], Wo[...], NT).astype(BF)
+        dws = dg(DyT[...], h2[...], NN)
+        for i in range(32):
+            tail = dws[i * 24 + 16 : i * 24 + 24]
+            So[i, :, 0:768] = dws[i * 24 : i * 24 + 16].astype(BF)
+            So[i, :, 768:1152] = pack_pair(tail[:, 0:384], tail[:, 384:768])
+        begin(3)
+        for st in store:
+            st.wait()
+
+    def attention(gext, q, kv, pe, bias, dkv, dpe, chunk):
         loads = [
             copy(4 + i, a, b)
-            for i, (a, b) in enumerate(
-                [(q_in, q), (kv_in, kv), (pe_in, pe), (bias_in, bias), (gatt_in, gatt)]
-            )
+            for i, (a, b) in enumerate([(q_in, q), (kv_in, kv), (pe_in, pe), (bias_in, bias)])
         ]
-        for ld in loads + mine:
+        for ld in loads:
             ld.start()
         for r in range(2):
-            gext[r, 0:64, 0:768] = jnp.zeros((64, 768), BF)
-            gext[r, 576:640, 0:768] = jnp.zeros((64, 768), BF)
-
-        @pl.when(jnp.logical_not(has_left))
-        def _():
-            precv[:, 1] = jnp.zeros((2, 64, 1536), BF)
-            hrecv[:, 1] = jnp.zeros((2, 64, 768), BF)
-
-        @pl.when(jnp.logical_not(has_right))
-        def _():
-            precv[:, 0] = jnp.zeros((2, 64, 1536), BF)
-            hrecv[:, 0] = jnp.zeros((2, 64, 768), BF)
-
-        tg[...] = jnp.zeros((16, 1536), F32)
-        lg[...] = jnp.zeros((16, 768), F32)
-        greet(me, True)
-        for k in range(4):
-            begin(k)
-        for ld in loads + mine:
+            gext[r * 640 : r * 640 + 64, 0:768] = jnp.zeros((64, 768), BF)
+            gext[r * 640 + 576 : r * 640 + 640, 0:768] = jnp.zeros((64, 768), BF)
+        for ld in loads:
             ld.wait()
-        blocks = [
-            (do_g, 0), (do_g, 1), (do_p, 0), (do_g, 2), (do_p, 1), (do_c, 0),
-            (do_g, 3), (do_p, 2), (do_c, 1), (do_p, 3), (do_c, 2), (do_c, 3),
-        ]
+        plan = {
+            0: [(do_g, 2)], 1: [(do_g, 3)], 2: [(do_p, 2)], 3: [(do_p, 3)], 4: [(do_c, 2)], 5: [(do_c, 3)],
+        }
         for r in range(2):
             def heads(h, carry):
                 attend_back(q, kv, pe, bias, gatt, gext, dkv, dpe, r, h)
-                for i, (fn, k) in enumerate(blocks):
-                    @pl.when(r * 6 + h == i)
-                    def _():
-                        for j in (1, 2, 3) if fn is do_c else (0, 1, 2, 3):
-                            fn(k, j)
-
+                if r == 0:
+                    run(plan, h)
                 return carry
 
             lax.fori_loop(0, 6, heads, 0)
@@ -974,22 +911,16 @@
                     tg[i : i + 1, lanes] += jnp.sum(gm * chunk[at, :], axis=0, keepdims=True)
                     dkv[r, t, at, :] += gm * taps[i : i + 1, lanes]
                 out_lanes = pl.ds(pl.multiple_of(768 + t * 128, 128), 128)
-                gext[r, :, out_lanes] = dkv[r, t].astype(BF)
+                gext[r * 640 : r * 640 + 640, out_lanes] = dkv[r, t].astype(BF)
                 return carry
 
             lax.fori_loop(0, 12, pool_back, 0)
 
-    vm = pltpu.VMEM
-    pl.run_scoped(
-        attention,
-        vm((2, 512, 768), BF), vm((2, 640, 1536), BF), vm((2, 256, 1536), BF), vm((8, 416, 128), F32),
-        vm((2, 512, 768), BF), vm((2, 12, 640, 128), F32), vm((2, 12, 256, 128), F32), vm((640, 128), F32),
-    )
-
-    def projection(h1, h1t, wq, tok, gmid, gh, dw):
+    def projection(gext, h1, h1t, wq, tok, gmid, gh, Sq):
+        late.append(Sq)
         loads = [
             copy(9 + i, a, b)
-            for i, (a, b) in enumerate([(h1_in, h1), (wq_in, wq), (tok_in, tok), (gmid_in, gmid)])
+            for i, (a, b) in enumerate([(h1_in, h1), (wq_in, wq), (tok_in, tok), (o_gmid, gmid)])
         ]
         for ld in loads:
             ld.start()
@@ -998,38 +929,25 @@
             def flip(i, carry):
                 rows = pl.ds(pl.multiple_of(i * 128, 128), 128)
                 for j in range(3):
-                    h1t[r, j * 256 : j * 256 + 256, rows] = h1[r, rows, j * 256 : j * 256 + 256].T
+                    to = pl.ds(pl.multiple_of(r * 640 + i * 128, 128), 128)
+                    h1t[j * 256 : j * 256 + 256, to] = h1[r, rows, j * 256 : j * 256 + 256].T
                 return carry
 
             lax.fori_loop(0, 5, flip, 0)
 
-        def grads(j, carry):
-            lanes = pl.ds(pl.multiple_of(j * 256, 256), 256)
-            dw[:, lanes] = dg(h1t[0], gext[0, :, lanes], NN) + dg(h1t[1], gext[1, :, lanes], NN)
-            return carry
-
-        lax.fori_loop(0, 9, grads, 0)
-
-        def share(i, carry):
-            r0 = pl.multiple_of(i * 24, 8)
-            Sq[i, :, 0:2304] = dw[pl.ds(r0, 16)].astype(BF)
-            tail = pl.ds(pl.multiple_of(r0 + 16, 8), 8)
-            Sq[i, :, 2304:3456] = pack_pair(dw[tail, 0:1152], dw[tail, 1152:2304])
-            return carry
-
-        lax.fori_loop(0, 32, share, 0)
+        for j in range(3):
+            dws = dg(h1t[...], gext[:, j * 768 : j * 768 + 768], NN)
+            for i in range(32):
+                tail = dws[i * 24 + 16 : i * 24 + 24]
+                Sq[i, :, j * 1152 : j * 1152 + 768] = dws[i * 24 : i * 24 + 16].astype(BF)
+                Sq[i, :, j * 1152 + 768 : j * 1152 + 1152] = pack_pair(tail[:, 0:384], tail[:, 384:768])
         begin(4)
         for k in range(4):
             finish(k)
         for ld in loads[1:]:
             ld.wait()
         for r in range(2):
-            def rows_back(i, carry):
-                rows = pl.ds(pl.multiple_of(i * 128, 128), 128)
-                gh[r, rows] = dg(gext[r, rows], wq[...], NT)
-                return carry
-
-            lax.fori_loop(0, 5, rows_back, 0)
+            gh[r] = dg(gext[r * 640 : r * 640 + 640], wq[...], NT)
             hstage[r, 0] = gh[r, 0:64].astype(BF)
             hstage[r, 1] = gh[r, 576:640].astype(BF)
             both(hstage, hrecv, r, 4, lambda cp: cp.start())
@@ -1043,11 +961,11 @@
         acc = (zero, zero)
         for r in range(2):
             def rows_norm(i, carry):
-                rows = pl.ds(pl.multiple_of(i * 128, 128), 128)
-                n, rs = norm_parts(tok[r, rows].astype(F32))
+                flat = pl.ds(pl.multiple_of(r * 512 + i * 128, 128), 128)
+                n, rs = norm_parts(tok[flat].astype(F32))
                 g = gh[r, pl.ds(pl.multiple_of(i * 128 + 64, 64), 128)]
                 e = g * gains[5:6]
-                gmid[r, rows] += rs * (
+                gmid[flat] += rs * (
                     e - jnp.mean(e, axis=-1, keepdims=True) - n * jnp.mean(e * n, axis=-1, keepdims=True)
                 )
                 a, b = carry
@@ -1058,7 +976,6 @@
         out.start()
         lg[5:6] = jnp.sum(acc[0], axis=0, keepdims=True)
         lg[6:7] = jnp.sum(acc[1], axis=0, keepdims=True)
-        lg[7:9] = sums2[0:2]
 
         def put(i, v):
             Ss[i] = v
@@ -1077,37 +994,53 @@
         finish(5)
         out.wait()
 
+    vm = pltpu.VMEM
+    tall, wide = (lambda dt: vm((1024, 768), dt)), (lambda dt: vm((768, 1024), dt))
     pl.run_scoped(
-        projection,
-        vm((2, 640, 768), BF), vm((2, 768, 640), BF), vm((768, 2304), BF), vm((2, 512, 768), BF),
-        vm((2, 512, 768), F32), vm((2, 640, 768), F32), vm((768, 2304), F32),
-    )
+        feed_forward,
+        tall(BF), tall(BF), tall(BF), vm((768, 768), BF), vm((768, 3072), BF), vm((768, 3072), BF),
+        tall(F32), tall(BF), wide(BF), wide(BF), tall(F32), tall(F32), vm((1024, 512), BF), vm((1024, 512), BF),
+    )
+
+    def rest(gext):
+        pl.run_scoped(
+            functools.partial(attention, gext),
+            vm((2, 512, 768), BF), vm((2, 640, 1536), BF), vm((2, 256, 1536), BF), vm((8, 416, 128), F32),
+            vm((2, 12, 640, 128), F32), vm((2, 12, 256, 128), F32), vm((640, 128), F32),
+        )
+        pl.run_scoped(
+            functools.partial(projection, gext),
+            vm((2, 640, 768), BF), vm((768, 1280), BF), vm((768, 2304), BF), tall(BF),
+            tall(F32), vm((2, 640, 768), F32), vm((32, 16, 3456), BF),
+        )
+
+    pl.run_scoped(rest, vm((1280, 2304), BF))
     for r in range(2):
         both(pstage, precv, r, 0, lambda cp: cp.wait_send())
         both(hstage, hrecv, r, 4, lambda cp: cp.wait_send())
 
 
-def back_part(sffn, sout, q, kv, pe, bias, gatt, gmid, h1, tok, wq, taps, gains, win4, sums2):
+def back_part(*args):
     sds = jax.ShapeDtypeStruct
     vm, dma = pltpu.VMEM, pltpu.SemaphoreType.DMA
     return pl.pallas_call(
         back_kernel,
         out_shape=[
-            sds((2, 512, 768), F32), sds((24, 2304), F32), sds((24, 768), F32), sds((24, 3072), F32),
-            sds((24, 3072), F32), sds((16, 128), F32),
+            sds((1024, 768), BF), sds((1024, 768), F32), sds((1024, 768), F32),
+            sds((24, 2304), F32), sds((24, 768), F32), sds((24, 3072), F32), sds((24, 3072), F32), sds((16, 128), F32),
         ],
-        in_specs=[ANY] * 11 + [VM] * 4,
-        out_specs=[ANY] + [VM] * 5,
+        in_specs=[ANY] * 12 + [VM] * 3,
+        out_specs=[ANY] * 3 + [VM] * 5,
         scratch_shapes=[
-            vm((3, 16, 16, 3072), BF), vm((16, 16, 1152), BF), vm((32, 16, 3456), BF), vm((32, 16, 128), BF),
+            vm((3, 32, 16, 3072), BF), vm((32, 16, 1152), BF), vm((32, 16, 128), BF),
             vm((3, 31, 16, 3072), BF), vm((31, 16, 1152), BF), vm((31, 16, 3456), BF), vm((31, 16, 128), BF),
-            vm((2, 640, 2304), BF),
+            vm((1024, 768), BF),
             vm((2, 2, 64, 1536), BF), vm((2, 2, 64, 1536), BF), vm((2, 2, 64, 768), BF), vm((2, 2, 64, 768), BF),
             vm((16, 1536), F32), vm((16, 768), F32),
             dma((6, 16)), dma((6, 16)), dma((8,)), dma((8,)), dma((14,)),
         ],
         compiler_params=pltpu.CompilerParams(collective_id=1, has_side_effects=True, vmem_limit_bytes=VMEM_LIMIT),
-    )(sffn, sout, q, kv, pe, bias, gatt, gmid, h1, tok, wq, taps, gains, win4, sums2)
+    )(*args)
 
 
 def with_halo(x, sides, width):
@@ -1425,16 +1358,13 @@
     wq, wo, wu, wd, taps, gains, h1, q, kv, pe, att, bias = front(
         tokens, winc, win4, winr, w_qkv, w_out, w_up, w_down.T, small
     )
-    flat = (1024, 768)
-    out, gmid, gatt, sffn, sout, sums2 = middle_part(
-        tokens.reshape(flat), att.reshape(flat), cotangent.reshape(flat), wo, wu, wd, gains
-    )
-    split = (2, 512, 768)
-    g_in, g_wq, g_wo, g_wu, g_wd, g_small = back_part(
-        sffn, sout, q, kv, pe, bias, gatt.reshape(split), gmid.reshape(split), h1, tokens, wq, taps, gains, win4, sums2
+    flat, split = (1024, 768), (2, 512, 768)
+    out, _, g_in, g_wq, g_wo, g_wu, g_wd, g_small = back_part(
+        tokens.reshape(flat), att.reshape(flat), cotangent.reshape(flat), wo, wu, wd,
+        q, kv, pe, bias, h1, wq, taps, gains, win4,
     )
     return (
-        out.reshape(split), g_in, g_small[5, :24], g_small[6, :24], g_wq, g_small[0:5, :48], g_wo,
+        out.reshape(split), g_in.reshape(split), g_small[5, :24], g_small[6, :24], g_wq, g_small[0:5, :48], g_wo,
         g_small[7, :24], g_small[8, :24], g_wu, g_wd.T,
     )
 

time: 327 us -> 294 us (0.90)
  Pallas kernels: 311 us -> 277 us
    pallas_call x2 -> x1, Pallas kernels: 206 us -> 172 us  [back_part(): pl.pallas_call(back_kernel, out_shape=[sds((1024, 768), BF), sds((1024, 7...]
    unnamed x15 -> x18, local copies, waits for them, and re-layouts: 6.6 us -> 7.09 us
where the time goes in v2:
time: 294 us; the launch traced here: 293 us
  Pallas kernels  277 us (94%)
  local copies, waits for them, and re-layouts  13.4 us (5%)
    pallas_call x1, Pallas kernels, back_part(): pl.pallas_call(back_kernel, out_shape=[sds((1024, 768), BF), sds((1024, 7...  172 us
    pallas_call x1, Pallas kernels, front(): pl.pallas_call(front_kernel, out_shape=[sds(sh, dt) for sh, dt in shapes]...  105 us
    unnamed x18, local copies, waits for them, and re-layouts  7.09 us

profile of v2, /device:TPU:0, one launch (start us, length us, event | category | flops | bytes accessed | tf_op | source)
XLA Modules:
  0.0 293.5 jit_solution(4560002179908413246)
XLA Ops:
  0.6 0.7 fusion.10
  1.4 1.3 fusion.6.small
  2.6 0.7 pad_dynamic-slice_fusion.winr
  3.3 0.0 copy-start.4
  3.4 0.7 fusion.14
  4.1 1.0 reshape.41.win4
  5.0 1.3 copy.23.winc
  6.4 0.0 copy-done.4
  6.4 104.9 %shard_map.203 = (bf16[768,2304]{1,0:T(8,128)(2,1)}, bf16[768,768]{1,0:T(8,128)(2,1)}, bf16[768,3072]{1,0:T(8,128)(2,1)}, bf16[768,3072]{1,0:T(8,128)(2,1)}, f32...) custom-call(bf16[2,512,768]{2,1,0:T(8,128)(2,1)} %tok.1, ...), custom_call_target="tpu_custom_call" | custom-call | tf_op jit(solution)/shard_map/pallas_call | solution.py:520
  111.3 172.4 %shard_map.204 = (bf16[1024,768]{1,0:T(8,128)(2,1)}, f32[1024,768]{1,0:T(8,128)}, f32[1024,768]{1,0:T(8,128)}, f32[24,2304]{1,0:T(8,128)}, f32[24,768]{1,0:T(8,1...) custom-call(bf16[1024,768]{1,0:T(8,128)(2,1)} %bitcast.21, bf16[1024,768]{1,0:T(8,128)(2,1)} %bitcast.24, ...), custom_call_target="tpu_custom_call" | custom-call | tf_op jit(solution)/shard_map/pallas_call | solution.py:1026
  283.7 0.0 copy-start
  283.7 1.4 slice_bitcast_fusion
  285.1 1.3 slice.17
  286.4 2.7 copy.30
  289.0 0.0 copy-done
  289.0 0.0 copy-start.3
  289.0 0.0 copy-start.5
  289.0 0.0 copy-start.2
  289.0 0.0 copy-start.1
  289.1 1.7 copy.31
  290.7 0.0 copy-done.3
  290.7 0.7 copy.32
  291.4 0.0 copy-done.5
  291.4 0.6 copy.33
  292.0 0.0 copy-done.2
  292.0 0.7 copy.34
  292.8 0.0 copy-done.1
  292.8 0.7 copy.35
Async XLA Ops:
  3.3 3.0 %copy-start.4 = (s32[2,1024]{1,0:T(2,128)}, s32[2,1024]{1,0:T(2,128)S(1)}, u32[]{:S(2)}) copy-start(s32[2,1024]{1,0:T(2,128)S(1)} %pad_dynamic-slice_fusion.winr) | copy-start | bytes 24580
  283.7 5.3 %copy-start = (f32[1024,768]{1,0:T(8,128)S(1)}, f32[1024,768]{1,0:T(8,128)}, u32[]{:S(2)}) copy-start(f32[1024,768]{1,0:T(8,128)} %get-tuple-element.43) | copy-start | bytes 9437188
  289.0 1.7 copy-start.3
  289.0 2.4 copy-start.5
  289.0 3.0 %copy-start.2 = (f32[24,3072]{1,0:T(8,128)S(1)}, f32[24,3072]{1,0:T(8,128)}, u32[]{:S(2)}) copy-start(f32[24,3072]{1,0:T(8,128)} %get-tuple-element.73) | copy-start | bytes 884740
  289.0 3.7 %copy-start.1 = (f32[24,3072]{1,0:T(8,128)S(1)}, f32[24,3072]{1,0:T(8,128)}, u32[]{:S(2)}) copy-start(f32[24,3072]{1,0:T(8,128)} %get-tuple-element.48) | copy-start | bytes 884740

commit v3 on v2

--- a/solution.py
+++ b/solution.py
@@ -73,6 +73,14 @@
     pl.semaphore_wait(bar, count)
 
 
+def greet_all(me):
+    bar = pltpu.get_barrier_semaphore()
+    pl.semaphore_signal(bar, inc=1, device_id=me["pd"], device_id_type=MESH)
+    for d in range(1, 16):
+        pl.semaphore_signal(bar, inc=1, device_id=(me["c"], lax.rem(me["s"] + d, 16)), device_id_type=MESH)
+    pl.semaphore_wait(bar, 16)
+
+
 def lane_low():
     return lax.broadcasted_iota(jnp.int32, (128, 128), 1) < HEAD
 
@@ -93,7 +101,7 @@
     top = jnp.max(st, axis=0, keepdims=True)
     e = jnp.exp(st - top)
     total = jnp.sum(e, axis=0, keepdims=True)
-    return e, 1.0 / total
+    return e, 1.0 / total, top + jnp.log(total)
 
 
 def mask_block(winc, win4, winr, r, b):
@@ -124,17 +132,19 @@
     )
 
 
-def attend(q, kv, pe, bias, att, r, h):
+def attend(q, kv, pe, bias, att, lse, r, h):
     kl, vl = head_lanes(h)
     for b in range(4):
         n, f, i = slice(b * 128, b * 128 + 256), slice(b * 32, b * 32 + 160), slice(b * 128, b * 128 + 128)
-        e, rt = softmax_block(pair_rows(q[r, i, kl]), kv[r, n, kl], pe[r, f, kl], bias[r * 4 + b])
+        e, rt, lse[r * 6 + h, b : b + 1] = softmax_block(
+            pair_rows(q[r, i, kl]), kv[r, n, kl], pe[r, f, kl], bias[r * 4 + b]
+        )
         low = (e * rt).astype(BF)
         values = jnp.concatenate([kv[r, n, vl], pe[r, f, vl]], axis=0)
         att[r, i, kl] = pair_out(dg(values, low, TN)).astype(BF)
 
 
-def attend_back(q, kv, pe, bias, g, gext, dkv, dpe, r, h):
+def attend_back(q, kv, pe, bias, lse, g, gext, dkv, dpe, r, h):
     kl, vl = head_lanes(h)
     for part in (h, 6 + h):
         dkv[r, part] = jnp.zeros((640, 128), F32)
@@ -143,8 +153,8 @@
         n, f, i = slice(b * 128, b * 128 + 256), slice(b * 32, b * 32 + 160), slice(b * 128, b * 128 + 128)
         q2, g2 = pair_rows(q[r, i, kl]), pair_rows(g[r * 512 + b * 128 : r * 512 + b * 128 + 128, kl])
         kn, vn, kf, vf = kv[r, n, kl], kv[r, n, vl], pe[r, f, kl], pe[r, f, vl]
-        e, rt = softmax_block(q2, kn, kf, bias[r * 4 + b])
-        p = e * rt
+        st = jnp.concatenate([dg(kn, q2, NT), dg(kf, q2, NT)], axis=0) - lse[r * 6 + h, b : b + 1]
+        p = jnp.exp(st + jnp.concatenate([bias[r * 4 + b], bias[r * 4 + b]], axis=1))
         dp = jnp.concatenate([dg(vn, g2, NT), dg(vf, g2, NT)], axis=0)
         delta = jnp.sum(p * dp, axis=0, keepdims=True)
         ds = (p * (dp - delta)).astype(BF)
@@ -227,8 +237,8 @@
 
 def front_kernel(
     tok, winc, win4, winr, wq, wo, wu, wd, small,
-    o_wq, o_wo, o_wu, o_wd, o_taps, o_gains, o_h1, o_q, o_kv, o_pe, o_att, o_bias,
-    G, Wq, Wo, Wu, Wd, taps, gains, xe, h1, q, kv, pe, att, bias, chunk,
+    o_wq, o_wo, o_wu, o_wd, o_taps, o_gains, o_h1, o_q, o_kv, o_pe, o_att, o_bias, o_lse,
+    G, Wq, Wo, Wu, Wd, taps, gains, xe, h1, q, kv, pe, att, bias, lse, chunk,
     send_x, send_y, send_d, send_z, send_g, recv, hsend, hrecv, local,
 ):
     me = where_am_i()
@@ -259,10 +269,13 @@
     def to_z(k, j):
         return hop(k, mine, (c, lax.rem(z + j, 4) * 4 + col), send_z.at[k, j - 1])
 
+    def by_y(k, zz):
+        return zz != 3
+
     def to_g(k, zz):
-        even = lax.rem(zz, 2) == 0
-        at = zz * 4 + jnp.where(even, me["colx"], me["coly"])
-        to = (c, z * 4 + jnp.where(even, me["coly"], me["colx"]))
+        over_y = by_y(k, zz)
+        at = zz * 4 + jnp.where(over_y, me["colx"], me["coly"])
+        to = (c, z * 4 + jnp.where(over_y, me["coly"], me["colx"]))
         return hop(k, c * 16 + at, to, send_g.at[k, zz])
 
     def got(k, slot):
@@ -372,6 +385,7 @@
             xe[r, 576:640] = jnp.zeros((64, 768), BF)
             pe[r, 192:256] = jnp.zeros((64, 1536), BF)
 
+    lse[...] = jnp.zeros((12, 8, 256), F32)
     greet(me, True)
     own(0)
     for r in range(2):
@@ -403,7 +417,7 @@
         pltpu.make_async_copy(a, b, local.at[2 + i])
         for i, (a, b) in enumerate(
             [(Wq, o_wq), (taps, o_taps), (gains, o_gains), (h1, o_h1), (q, o_q), (kv, o_kv), (pe, o_pe),
-             (att, o_att), (bias, o_bias), (Wo, o_wo), (Wu, o_wu), (Wd, o_wd)]
+             (att, o_att), (bias, o_bias), (Wo, o_wo), (Wu, o_wu), (Wd, o_wd), (lse, o_lse)]
         )
     ]
     for i in (0, 1, 2, 8):
@@ -462,7 +476,7 @@
         arrived(halo_pool, r)
 
         def heads_event(h, carry):
-            attend(q, kv, pe, bias, att, r, h)
+            attend(q, kv, pe, bias, att, lse, r, h)
             base = 12 + (r * 6 + h) * 2
 
             @pl.when(base < 33)
@@ -478,6 +492,7 @@
         lax.fori_loop(0, 6, heads_event, 0)
     outs[6].start()
     outs[7].start()
+    outs[12].start()
     for k in (1, 2, 3):
         other(k)
     for i, (name, dst) in enumerate((("out", Wo), ("up", Wu), ("down", Wd))):
@@ -508,7 +523,7 @@
         ((768, 2304), BF), ((768, 768), BF), ((768, 3072), BF), ((768, 3072), BF),
         ((16, 1536), F32), ((16, 768), F32),
         ((2, 640, 768), BF), ((2, 512, 768), BF), ((2, 640, 1536), BF), ((2, 256, 1536), BF),
-        ((2, 512, 768), BF), ((8, 416, 128), F32),
+        ((2, 512, 768), BF), ((8, 416, 128), F32), ((12, 8, 256), F32),
     ]
     scratch = [pltpu.VMEM((4, 32, 16, WIDE), BF)]
     scratch += [pltpu.VMEM(sh, dt) for sh, dt in shapes[:6]]
@@ -516,7 +531,7 @@
     scratch += [pltpu.VMEM(sh, dt) for sh, dt in shapes[6:]]
     scratch += [pltpu.VMEM((2, 640, 128), F32)]
     dma = pltpu.SemaphoreType.DMA
-    scratch += [dma((4, 16)), dma((4, 16)), dma((4, 16)), dma((4, 3)), dma((4, 4)), dma((4, 32)), dma((8,)), dma((8,)), dma((14,))]
+    scratch += [dma((4, 16)), dma((4, 16)), dma((4, 16)), dma((4, 3)), dma((4, 4)), dma((4, 32)), dma((8,)), dma((8,)), dma((15,))]
     return pl.pallas_call(
         front_kernel,
         out_shape=[sds(sh, dt) for sh, dt in shapes],
@@ -572,7 +587,7 @@
 
 def back_kernel(
     tok_in, att_in, dy_in, wo_in, wu_in, wd_in,
-    q_in, kv_in, pe_in, bias_in, h1_in, wq_in, taps, gains, win4,
+    q_in, kv_in, pe_in, bias_in, h1_in, wq_in, taps, gains, win4, lse,
     o_out, o_gmid, o_in, o_wq, o_wo, o_wu, o_wd, o_small,
     Sf, So, Ss, Rf, Ro, Rq, Rs, gatt, pstage, precv, hstage, hrecv, tg, lg,
     send, recv, psend, prsem, local,
@@ -591,15 +606,17 @@
             return Sf.at[k, pl.ds(c * 16, 16)], Rf.at[k]
         if k == 3:
             return So.at[pl.ds(c * 16, 16)], Ro
-        if k == 4:
-            return late[0].at[pl.ds(c * 16, 16)], Rq
+        if k < 7:
+            return late[0].at[k - 4, pl.ds(c * 16, 16)], Rq.at[k - 4]
         return Ss.at[pl.ds(c * 16, 16)], Rs
 
     def other(k):
         start = (1 - c) * 16
         if k < 3:
             return Sf.at[k, pl.ds(start, 16)]
-        return (So, late[0] if late else None, Ss)[k - 3].at[pl.ds(start, 16)]
+        if k == 3 or k == 7:
+            return (So if k == 3 else Ss).at[pl.ds(start, 16)]
+        return late[0].at[k - 4, pl.ds(start, 16)]
 
     def remote(k, src, slot, i, to):
         return pltpu.make_async_remote_copy(
@@ -689,67 +706,92 @@
                     ref[0:16, hi : hi + 256] = v[:, base + 256 : base + 512]
                     ref[16:24, lo : lo + 256] = v[0:8, base + 512 : base + 768]
                     ref[16:24, hi : hi + 256] = v[8:16, base + 512 : base + 768]
-        elif k < 5:
-            ref = o_wo if k == 3 else o_wq
-            for i in range(1 if k == 3 else 3):
-                at, frm = i * 768, i * 1152
-                ref[0:16, at : at + 768] = v[:, frm : frm + 768]
-                ref[16:24, at : at + 384] = v[0:8, frm + 768 : frm + 1152]
-                ref[16:24, at + 384 : at + 768] = v[8:16, frm + 768 : frm + 1152]
         else:
-            o_small[...] = v
+            ref, at = (o_wo, 0) if k == 3 else (o_wq, (k - 4) * 768)
+            ref[0:16, at : at + 768] = v[:, 0:768]
+            ref[16:24, at : at + 384] = v[0:8, 768:1152]
+            ref[16:24, at + 384 : at + 768] = v[8:16, 768:1152]
         drain(k)
 
-    def halo(src, dst, r, right, base):
-        i = base + r * 2 + int(right)
+    def to_owner(d):
+        owner = lax.rem(s + d, 16)
+        return remote(7, Ss.at[c * 16 + owner], Rs.at[16 + s], d, (c, owner))
+
+    def from_peer(d):
+        slot = 16 + lax.rem(s + 16 - d, 16)
+        return remote(7, Ss.at[0], Rs.at[slot], d, me["px"])
+
+    def small_out():
+        swap(7).wait_recv()
+        for i in range(16):
+            Ss[c * 16 + i] = (Ss[c * 16 + i].astype(F32) + Rs[i].astype(F32)).astype(BF)
+        for d in range(1, 16):
+            to_owner(d).start()
+
+    def small_in():
+        v = Ss[c * 16 + s].astype(F32)
+        for d in range(1, 16):
+            from_peer(d).wait_recv()
+            v = v + Rs[16 + lax.rem(s + 16 - d, 16)].astype(F32)
+        o_small[...] = v
+        swap(7).wait_send()
+        for d in range(1, 16):
+            to_owner(d).wait_send()
+
+    def halo(src, dst, r, right, h):
+        side = int(right)
+        i = 24 + r * 2 + side if h is None else (r * 2 + side) * 6 + h
+        at = (r, side) if h is None else (r, side, h)
         return pltpu.make_async_remote_copy(
-            src_ref=src.at[r, int(right)], dst_ref=dst.at[r, int(right)],
-            send_sem=psend.at[i], recv_sem=prsem.at[i],
+            src_ref=src.at[at], dst_ref=dst.at[at], send_sem=psend.at[i], recv_sem=prsem.at[i],
             device_id=(c, s + 1 if right else s - 1), device_id_type=MESH,
         )
 
-    def both(src, dst, r, base, act):
+    def both(src, dst, r, h, act):
         @pl.when(has_right)
         def _():
-            act(halo(src, dst, r, True, base))
+            act(halo(src, dst, r, True, h))
 
         @pl.when(has_left)
         def _():
-            act(halo(src, dst, r, False, base))
-
-    def arrived(src, dst, r, base):
+            act(halo(src, dst, r, False, h))
+
+    def arrived(src, dst, r, h):
         @pl.when(has_left)
         def _():
-            halo(src, dst, r, True, base).wait_recv()
+            halo(src, dst, r, True, h).wait_recv()
 
         @pl.when(has_right)
         def _():
-            halo(src, dst, r, False, base).wait_recv()
+            halo(src, dst, r, False, h).wait_recv()
 
     @pl.when(jnp.logical_not(has_left))
     def _():
-        precv[:, 1] = jnp.zeros((2, 64, 1536), BF)
+        precv[:, 1] = jnp.zeros((2, 6, 2, 64, 128), BF)
         hrecv[:, 1] = jnp.zeros((2, 64, 768), BF)
 
     @pl.when(jnp.logical_not(has_right))
     def _():
-        precv[:, 0] = jnp.zeros((2, 64, 1536), BF)
+        precv[:, 0] = jnp.zeros((2, 6, 2, 64, 128), BF)
         hrecv[:, 0] = jnp.zeros((2, 64, 768), BF)
 
     tg[...] = jnp.zeros((16, 1536), F32)
     lg[...] = jnp.zeros((16, 768), F32)
-    greet(me, True)
+    greet_all(me)
+
+    def perform(todo):
+        for fn, k in todo:
+            if fn is begin or fn is finish:
+                fn(k)
+            else:
+                for j in (1, 2, 3) if fn is do_c else (0, 1, 2, 3):
+                    fn(k, j)
 
     def run(plan, at):
         for i, todo in plan.items():
             @pl.when(at == i)
             def _():
-                for fn, k in todo:
-                    if fn is begin:
-                        begin(k)
-                    else:
-                        for j in (1, 2, 3) if fn is do_c else (0, 1, 2, 3):
-                            fn(k, j)
+                perform(todo)
 
     def feed_forward(Tok, Att, Dy, Wo, Wu, Wd, mid, h2, DyT, H2T, y, gh2, act, gu):
         loads = [
@@ -789,8 +831,8 @@
         loads[4].wait()
         loads[5].wait()
         plan = {
-            5: [(begin, 0)], 6: [(do_g, 0)], 8: [(do_p, 0)], 9: [(do_c, 0)],
-            11: [(begin, 1)], 12: [(do_g, 1)], 14: [(do_p, 1)], 15: [(do_c, 1)], 17: [(begin, 2)],
+            5: [(begin, 0)], 7: [(do_g, 0)], 11: [(do_p, 0), (begin, 1)], 13: [(do_g, 1)],
+            17: [(do_c, 0), (begin, 2)],
         }
 
         def chunk(j, carry):
@@ -839,6 +881,7 @@
 
         zero = jnp.zeros((8, 768), F32)
         a, b = lax.fori_loop(0, 8, last, (zero, zero))
+        perform([(do_p, 1)])
         lg[7:8] = jnp.sum(a, axis=0, keepdims=True)
         lg[8:9] = jnp.sum(b, axis=0, keepdims=True)
         store = [copy(6, Tok, o_out), copy(7, y, o_gmid)]
@@ -859,50 +902,74 @@
             So[i, :, 0:768] = dws[i * 24 : i * 24 + 16].astype(BF)
             So[i, :, 768:1152] = pack_pair(tail[:, 0:384], tail[:, 384:768])
         begin(3)
+        perform([(do_g, 2)])
         for st in store:
             st.wait()
 
-    def attention(gext, q, kv, pe, bias, dkv, dpe, chunk):
+    def weight_grad(gext, h1t, Sq, j):
+        dws = dg(h1t[...], gext[:, j * 768 : j * 768 + 768], NN)
+        for i in range(32):
+            tail = dws[i * 24 + 16 : i * 24 + 24]
+            Sq[j, i, :, 0:768] = dws[i * 24 : i * 24 + 16].astype(BF)
+            Sq[j, i, :, 768:1152] = pack_pair(tail[:, 0:384], tail[:, 384:768])
+        begin(4 + j)
+
+    def attention(gext, h1, h1t, Sq, q, kv, pe, bias, dkv, dpe, chunk):
         loads = [
             copy(4 + i, a, b)
-            for i, (a, b) in enumerate([(q_in, q), (kv_in, kv), (pe_in, pe), (bias_in, bias)])
+            for i, (a, b) in enumerate([(q_in, q), (kv_in, kv), (pe_in, pe), (bias_in, bias), (h1_in, h1)])
         ]
         for ld in loads:
             ld.start()
         for r in range(2):
             gext[r * 640 : r * 640 + 64, 0:768] = jnp.zeros((64, 768), BF)
             gext[r * 640 + 576 : r * 640 + 640, 0:768] = jnp.zeros((64, 768), BF)
-        for ld in loads:
+        for ld in loads[:4]:
             ld.wait()
-        plan = {
-            0: [(do_g, 2)], 1: [(do_g, 3)], 2: [(do_p, 2)], 3: [(do_p, 3)], 4: [(do_c, 2)], 5: [(do_c, 3)],
-        }
+        plans = (
+            {0: [(do_c, 1)], 2: [(do_p, 2)], 3: [(do_g, 3)], 5: [(do_p, 3)]},
+            {2: [(do_c, 2)], 3: [(do_c, 3)]},
+        )
         for r in range(2):
             def heads(h, carry):
-                attend_back(q, kv, pe, bias, gatt, gext, dkv, dpe, r, h)
-                if r == 0:
-                    run(plan, h)
+                attend_back(q, kv, pe, bias, lse, gatt, gext, dkv, dpe, r, h)
+                for part in range(2):
+                    pstage[r, 0, h, part] = dpe[r, part * 6 + h, 0:64].astype(BF)
+                    pstage[r, 1, h, part] = dpe[r, part * 6 + h, 192:256].astype(BF)
+                both(pstage, precv, r, h, lambda cp: cp.start())
+                run(plans[r], h)
                 return carry
 
             lax.fori_loop(0, 6, heads, 0)
-            for t in range(12):
-                lanes = slice(t * 128, t * 128 + 128)
-                pstage[r, 0, :, lanes] = dpe[r, t, 0:64].astype(BF)
-                pstage[r, 1, :, lanes] = dpe[r, t, 192:256].astype(BF)
-            both(pstage, precv, r, 0, lambda cp: cp.start())
-
+
+        loads[4].wait()
+        for r in range(2):
+            def flip(i, carry):
+                rows = pl.ds(pl.multiple_of(i * 128, 128), 128)
+                for j in range(3):
+                    to = pl.ds(pl.multiple_of(r * 640 + i * 128, 128), 128)
+                    h1t[j * 256 : j * 256 + 256, to] = h1[r, rows, j * 256 : j * 256 + 256].T
+                return carry
+
+            lax.fori_loop(0, 5, flip, 0)
+        weight_grad(gext, h1t, Sq, 0)
         for r in range(2):
             anchor = win4[r, 64:192, 0:1]
             same = [
                 (win4[r, a : a + 128, f : f + 1] == anchor).astype(F32)
                 for a, f in ((63, 2), (63, 3), (64, 0), (64, 1), (64, 2))
             ]
-            arrived(pstage, precv, r, 0)
 
             def pool_back(t, carry):
                 lanes = pl.ds(pl.multiple_of(t * 128, 128), 128)
-                low = dpe[r, t, 64:128] + precv[r, 1, :, lanes].astype(F32)
-                high = dpe[r, t, 128:192] + precv[r, 0, :, lanes].astype(F32)
+                h, part = lax.rem(t, 6), t // 6
+
+                @pl.when(t < 6)
+                def _():
+                    arrived(pstage, precv, r, h)
+
+                low = dpe[r, t, 64:128] + precv[r, 1, h, part].astype(F32)
+                high = dpe[r, t, 128:192] + precv[r, 0, h, part].astype(F32)
                 gp = jnp.concatenate([low, high], axis=0)
                 chunk[...] = kv[r, :, lanes].astype(F32)
                 for i in range(5):
@@ -915,63 +982,48 @@
                 return carry
 
             lax.fori_loop(0, 12, pool_back, 0)
-
-    def projection(gext, h1, h1t, wq, tok, gmid, gh, Sq):
-        late.append(Sq)
+        perform([(do_g, 4)])
+
+    def projection(gext, h1t, Sq, wq, tok, gmid, gh):
         loads = [
-            copy(9 + i, a, b)
-            for i, (a, b) in enumerate([(h1_in, h1), (wq_in, wq), (tok_in, tok), (o_gmid, gmid)])
+            copy(9 + i, a, b) for i, (a, b) in enumerate([(wq_in, wq), (tok_in, tok), (o_gmid, gmid)])
         ]
         for ld in loads:
             ld.start()
-        loads[0].wait()
-        for r in range(2):
-            def flip(i, carry):
-                rows = pl.ds(pl.multiple_of(i * 128, 128), 128)
-                for j in range(3):
-                    to = pl.ds(pl.multiple_of(r * 640 + i * 128, 128), 128)
-                    h1t[j * 256 : j * 256 + 256, to] = h1[r, rows, j * 256 : j * 256 + 256].T
-                return carry
-
-            lax.fori_loop(0, 5, flip, 0)
-
-        for j in range(3):
-            dws = dg(h1t[...], gext[:, j * 768 : j * 768 + 768], NN)
-            for i in range(32):
-                tail = dws[i * 24 + 16 : i * 24 + 24]
-                Sq[i, :, j * 1152 : j * 1152 + 768] = dws[i * 24 : i * 24 + 16].astype(BF)
-                Sq[i, :, j * 1152 + 768 : j * 1152 + 1152] = pack_pair(tail[:, 0:384], tail[:, 384:768])
-        begin(4)
-        for k in range(4):
-            finish(k)
-        for ld in loads[1:]:
+        weight_grad(gext, h1t, Sq, 1)
+        weight_grad(gext, h1t, Sq, 2)
+        perform([(do_p, 4), (do_g, 5)])
+        for ld in loads:
             ld.wait()
         for r in range(2):
             gh[r] = dg(gext[r * 640 : r * 640 + 640], wq[...], NT)
             hstage[r, 0] = gh[r, 0:64].astype(BF)
             hstage[r, 1] = gh[r, 576:640].astype(BF)
-            both(hstage, hrecv, r, 4, lambda cp: cp.start())
-            for zz in range(4):
-                (do_g if r == 0 else do_p)(4, zz)
-        for r in range(2):
-            arrived(hstage, hrecv, r, 4)
+            both(hstage, hrecv, r, None, lambda cp: cp.start())
+            perform(([(do_g, 6), (do_p, 5)], [(do_p, 6), (do_c, 4)])[r])
+
+        def rows_norm(r, i, carry):
+            rows = pl.ds(pl.multiple_of(r * 512 + i * 128, 128), 128)
+            n, rs = norm_parts(tok[rows].astype(F32))
+            g = gh[r, pl.ds(pl.multiple_of(i * 128 + 64, 64), 128)]
+            e = g * gains[5:6]
+            gmid[rows] += rs * (
+                e - jnp.mean(e, axis=-1, keepdims=True) - n * jnp.mean(e * n, axis=-1, keepdims=True)
+            )
+            a, b = carry
+            return a + jnp.sum((g * n).reshape(16, 8, 768), axis=0), b + jnp.sum(g.reshape(16, 8, 768), axis=0)
+
+        def add_halo(r):
+            arrived(hstage, hrecv, r, None)
             gh[r, 64:128] += hrecv[r, 1].astype(F32)
             gh[r, 512:576] += hrecv[r, 0].astype(F32)
+
         zero = jnp.zeros((8, 768), F32)
-        acc = (zero, zero)
-        for r in range(2):
-            def rows_norm(i, carry):
-                flat = pl.ds(pl.multiple_of(r * 512 + i * 128, 128), 128)
-                n, rs = norm_parts(tok[flat].astype(F32))
-                g = gh[r, pl.ds(pl.multiple_of(i * 128 + 64, 64), 128)]
-                e = g * gains[5:6]
-                gmid[flat] += rs * (
-                    e - jnp.mean(e, axis=-1, keepdims=True) - n * jnp.mean(e * n, axis=-1, keepdims=True)
-                )
-                a, b = carry
-                return a + jnp.sum((g * n).reshape(16, 8, 768), axis=0), b + jnp.sum(g.reshape(16, 8, 768), axis=0)
-
-            acc = lax.fori_loop(0, 4, rows_norm, acc)
+        add_halo(0)
+        acc = lax.fori_loop(0, 4, lambda i, cr: rows_norm(0, i, cr), (zero, zero))
+        acc = lax.fori_loop(1, 3, lambda i, cr: rows_norm(1, i, cr), acc)
+        add_halo(1)
+        acc = lax.fori_loop(0, 2, lambda i, cr: rows_norm(1, 3 * i, cr), acc)
         out = copy(13, gmid, o_in)
         out.start()
         lg[5:6] = jnp.sum(acc[0], axis=0, keepdims=True)
@@ -981,17 +1033,12 @@
             Ss[i] = v
 
         pick_small(tg, lg, put)
-        begin(5)
-        for j in (1, 2, 3):
-            do_c(4, j)
-        for zz in range(4):
-            do_g(5, zz)
-        for zz in range(4):
-            do_p(5, zz)
-        for j in (1, 2, 3):
-            do_c(5, j)
-        finish(4)
-        finish(5)
+        begin(7)
+        perform([(do_c, 5), (finish, 0)])
+        small_out()
+        perform([(finish, 1), (finish, 2), (finish, 3), (do_c, 6), (finish, 4), (finish, 5)])
+        small_in()
+        perform([(finish, 6)])
         out.wait()
 
     vm = pltpu.VMEM
@@ -1002,22 +1049,25 @@
         tall(F32), tall(BF), wide(BF), wide(BF), tall(F32), tall(F32), vm((1024, 512), BF), vm((1024, 512), BF),
     )
 
-    def rest(gext):
+    def rest(gext, h1, h1t, Sq):
+        late.append(Sq)
         pl.run_scoped(
-            functools.partial(attention, gext),
+            functools.partial(attention, gext, h1, h1t, Sq),
             vm((2, 512, 768), BF), vm((2, 640, 1536), BF), vm((2, 256, 1536), BF), vm((8, 416, 128), F32),
             vm((2, 12, 640, 128), F32), vm((2, 12, 256, 128), F32), vm((640, 128), F32),
         )
         pl.run_scoped(
-            functools.partial(projection, gext),
-            vm((2, 640, 768), BF), vm((768, 1280), BF), vm((768, 2304), BF), tall(BF),
-            tall(F32), vm((2, 640, 768), F32), vm((32, 16, 3456), BF),
-        )
-
-    pl.run_scoped(rest, vm((1280, 2304), BF))
+            functools.partial(projection, gext, h1t, Sq),
+            vm((768, 2304), BF), tall(BF), tall(F32), vm((2, 640, 768), F32),
+        )
+
+    pl.run_scoped(
+        rest, vm((1280, 2304), BF), vm((2, 640, 768), BF), vm((768, 1280), BF), vm((3, 32, 16, 1152), BF)
+    )
     for r in range(2):
-        both(pstage, precv, r, 0, lambda cp: cp.wait_send())
-        both(hstage, hrecv, r, 4, lambda cp: cp.wait_send())
+        for h in range(6):
+            both(pstage, precv, r, h, lambda cp: cp.wait_send())
+        both(hstage, hrecv, r, None, lambda cp: cp.wait_send())
 
 
 def back_part(*args):
@@ -1029,15 +1079,15 @@
             sds((1024, 768), BF), sds((1024, 768), F32), sds((1024, 768), F32),
             sds((24, 2304), F32), sds((24, 768), F32), sds((24, 3072), F32), sds((24, 3072), F32), sds((16, 128), F32),
         ],
-        in_specs=[ANY] * 12 + [VM] * 3,
+        in_specs=[ANY] * 12 + [VM] * 4,
         out_specs=[ANY] * 3 + [VM] * 5,
         scratch_shapes=[
             vm((3, 32, 16, 3072), BF), vm((32, 16, 1152), BF), vm((32, 16, 128), BF),
-            vm((3, 31, 16, 3072), BF), vm((31, 16, 1152), BF), vm((31, 16, 3456), BF), vm((31, 16, 128), BF),
+            vm((3, 31, 16, 3072), BF), vm((31, 16, 1152), BF), vm((3, 31, 16, 1152), BF), vm((32, 16, 128), BF),
             vm((1024, 768), BF),
-            vm((2, 2, 64, 1536), BF), vm((2, 2, 64, 1536), BF), vm((2, 2, 64, 768), BF), vm((2, 2, 64, 768), BF),
+            vm((2, 2, 6, 2, 64, 128), BF), vm((2, 2, 6, 2, 64, 128), BF), vm((2, 2, 64, 768), BF), vm((2, 2, 64, 768), BF),
             vm((16, 1536), F32), vm((16, 768), F32),
-            dma((6, 16)), dma((6, 16)), dma((8,)), dma((8,)), dma((14,)),
+            dma((8, 16)), dma((8, 16)), dma((28,)), dma((28,)), dma((14,)),
         ],
         compiler_params=pltpu.CompilerParams(collective_id=1, has_side_effects=True, vmem_limit_bytes=VMEM_LIMIT),
     )(*args)
@@ -1355,13 +1405,13 @@
 ):
     winc, win4, winr = windows(segments)
     small = small_share(pool_taps, ln1_gain, ln1_bias, ln2_gain, ln2_bias)
-    wq, wo, wu, wd, taps, gains, h1, q, kv, pe, att, bias = front(
+    wq, wo, wu, wd, taps, gains, h1, q, kv, pe, att, bias, lse = front(
         tokens, winc, win4, winr, w_qkv, w_out, w_up, w_down.T, small
     )
     flat, split = (1024, 768), (2, 512, 768)
     out, _, g_in, g_wq, g_wo, g_wu, g_wd, g_small = back_part(
         tokens.reshape(flat), att.reshape(flat), cotangent.reshape(flat), wo, wu, wd,
-        q, kv, pe, bias, h1, wq, taps, gains, win4,
+        q, kv, pe, bias, h1, wq, taps, gains, win4, lse,
     )
     return (
         out.reshape(split), g_in.reshape(split), g_small[5, :24], g_small[6, :24], g_wq, g_small[0:5, :48], g_wo,

time: 294 us -> 264 us (0.90)
  Pallas kernels: 277 us -> 247 us
    pallas_call x1, Pallas kernels: 172 us -> 147 us  [back_part(): pl.pallas_call(back_kernel, out_shape=[sds((1024, 768), BF), sds((1024, 7...]
    pallas_call x1, Pallas kernels: 105 us -> 99.8 us  [front(): pl.pallas_call(front_kernel, out_shape=[sds(sh, dt) for sh, dt in shapes]...]
where the time goes in v3:
time: 264 us; the launch traced here: 263 us
  Pallas kernels  247 us (94%)
  local copies, waits for them, and re-layouts  13.5 us (5%)
    pallas_call x1, Pallas kernels, back_part(): pl.pallas_call(back_kernel, out_shape=[sds((1024, 768), BF), sds((1024, 7...  147 us
    pallas_call x1, Pallas kernels, front(): pl.pallas_call(front_kernel, out_shape=[sds(sh, dt) for sh, dt in shapes]...  99.8 us
    unnamed x18, local copies, waits for them, and re-layouts  7.09 us

profile of v3, /device:TPU:0, one launch (start us, length us, event | category | flops | bytes accessed | tf_op | source)
XLA Modules:
  0.0 263.3 jit_solution(12980901236255990517)
XLA Ops:
  0.6 0.7 fusion.10
  1.4 1.3 fusion.6.small
  2.6 0.7 pad_dynamic-slice_fusion.winr
  3.3 0.0 copy-start.4
  3.4 0.7 fusion.14
  4.1 1.0 reshape.41.win4
  5.0 1.3 copy.23.winc
  6.4 0.0 copy-done.4
  6.4 99.8 %shard_map.203 = (bf16[768,2304]{1,0:T(8,128)(2,1)}, bf16[768,768]{1,0:T(8,128)(2,1)}, bf16[768,3072]{1,0:T(8,128)(2,1)}, bf16[768,3072]{1,0:T(8,128)(2,1)}, f32...) custom-call(bf16[2,512,768]{2,1,0:T(8,128)(2,1)} %tok.1, ...), custom_call_target="tpu_custom_call" | custom-call | tf_op jit(solution)/shard_map/pallas_call | solution.py:535
  106.2 147.3 %shard_map.204 = (bf16[1024,768]{1,0:T(8,128)(2,1)}, f32[1024,768]{1,0:T(8,128)}, f32[1024,768]{1,0:T(8,128)}, f32[24,2304]{1,0:T(8,128)}, f32[24,768]{1,0:T(8,1...) custom-call(bf16[1024,768]{1,0:T(8,128)(2,1)} %bitcast.21, bf16[1024,768]{1,0:T(8,128)(2,1)} %bitcast.24, ...), custom_call_target="tpu_custom_call" | custom-call | tf_op jit(solution)/shard_map/pallas_call | solution.py:1076
  253.6 0.0 copy-start
  253.6 1.4 slice_bitcast_fusion
  254.9 1.3 slice.17
  256.2 2.7 %copy.30 = bf16[2,512,768]{2,1,0:T(8,128)(2,1)} copy(bf16[2,512,768]{2,1,0:T(8,128)(2,1)} %bitcast.25) | data formatting | bytes 3145728
  258.9 0.0 copy-done
  258.9 0.0 copy-start.3
  258.9 0.0 copy-start.5
  258.9 0.0 copy-start.2
  258.9 0.0 copy-start.1
  258.9 1.7 copy.31
  260.6 0.0 copy-done.3
  260.6 0.7 copy.32
  261.2 0.0 copy-done.5
  261.2 0.6 copy.33
  261.9 0.0 copy-done.2
  261.9 0.7 copy.34
  262.6 0.0 copy-done.1
  262.6 0.7 copy.35
Async XLA Ops:
  3.3 3.0 %copy-start.4 = (s32[2,1024]{1,0:T(2,128)}, s32[2,1024]{1,0:T(2,128)S(1)}, u32[]{:S(2)}) copy-start(s32[2,1024]{1,0:T(2,128)S(1)} %pad_dynamic-slice_fusion.winr) | copy-start | bytes 24580
  253.6 5.3 %copy-start = (f32[1024,768]{1,0:T(8,128)S(1)}, f32[1024,768]{1,0:T(8,128)}, u32[]{:S(2)}) copy-start(f32[1024,768]{1,0:T(8,128)} %get-tuple-element.45) | copy-start | bytes 9437188
  258.9 1.7 copy-start.3
  258.9 2.4 copy-start.5
  258.9 3.0 %copy-start.2 = (f32[24,3072]{1,0:T(8,128)S(1)}, f32[24,3072]{1,0:T(8,128)}, u32[]{:S(2)}) copy-start(f32[24,3072]{1,0:T(8,128)} %get-tuple-element.75) | copy-start | bytes 884740
  258.9 3.7 %copy-start.1 = (f32[24,3072]{1,0:T(8,128)S(1)}, f32[24,3072]{1,0:T(8,128)}, u32[]{:S(2)}) copy-start(f32[24,3072]{1,0:T(8,128)} %get-tuple-element.50) | copy-start | bytes 884740

commit v4 on v3

--- a/solution.py
+++ b/solution.py
@@ -18,7 +18,7 @@
 MESH = pl.DeviceIdType.MESH
 ANY = pl.BlockSpec(memory_space=pl.ANY)
 VM = pl.BlockSpec(memory_space=pltpu.VMEM)
-VMEM_LIMIT = 62 * 2**20
+VMEM_LIMIT = 63 * 2**20
 UNIT = 384
 CLS = 3456
 WIDE = 3584
@@ -51,26 +51,27 @@
     )
 
 
-def greet(me, halo):
+def greet(me):
     bar = pltpu.get_barrier_semaphore()
     who = [me["px"], me["py"], me["pd"]]
     who += [(me["c"], lax.rem(me["z"] + j, 4) * 4 + me["col"]) for j in (1, 2, 3)]
     for dev in who:
         pl.semaphore_signal(bar, inc=1, device_id=dev, device_id_type=MESH)
-    count = 6
-    if halo:
-        last = lax.axis_size("seq") - 1
-
-        @pl.when(me["s"] > 0)
-        def _():
-            pl.semaphore_signal(bar, inc=1, device_id=(me["c"], me["s"] - 1), device_id_type=MESH)
-
-        @pl.when(me["s"] < last)
-        def _():
-            pl.semaphore_signal(bar, inc=1, device_id=(me["c"], me["s"] + 1), device_id_type=MESH)
-
-        count = 6 + (me["s"] > 0).astype(jnp.int32) + (me["s"] < last).astype(jnp.int32)
-    pl.semaphore_wait(bar, count)
+    last = lax.axis_size("seq") - 1
+
+    @pl.when(me["s"] > 0)
+    def _():
+        pl.semaphore_signal(bar, inc=1, device_id=(me["c"], me["s"] - 1), device_id_type=MESH)
+
+    @pl.when(me["s"] < last)
+    def _():
+        pl.semaphore_signal(bar, inc=1, device_id=(me["c"], me["s"] + 1), device_id_type=MESH)
+
+    return 6 + (me["s"] > 0).astype(jnp.int32) + (me["s"] < last).astype(jnp.int32)
+
+
+def all_here(count):
+    pl.semaphore_wait(pltpu.get_barrier_semaphore(), count)
 
 
 def greet_all(me):
@@ -78,7 +79,6 @@
     pl.semaphore_signal(bar, inc=1, device_id=me["pd"], device_id_type=MESH)
     for d in range(1, 16):
         pl.semaphore_signal(bar, inc=1, device_id=(me["c"], lax.rem(me["s"] + d, 16)), device_id_type=MESH)
-    pl.semaphore_wait(bar, 16)
 
 
 def lane_low():
@@ -104,25 +104,39 @@
     return e, 1.0 / total, top + jnp.log(total)
 
 
-def mask_block(winc, win4, winr, r, b):
-    seg_q = winr[r : r + 1, 256 + 128 * b : 384 + 128 * b]
+def fill_window(seg, winr, wcol, has_left, has_right, s):
+    length, block = seg.shape[1], 512
+    left = pl.multiple_of(jnp.maximum(s * block - REACH, 0), REACH)
+    right = pl.multiple_of(jnp.minimum(s * block + block, length - REACH), REACH)
+    before = seg[:, pl.ds(left, REACH)].astype(F32)
+    after = seg[:, pl.ds(right, REACH)].astype(F32)
+    winr[:, 0:REACH] = jnp.where(has_left, before, -1.0)
+    winr[:, REACH : REACH + block] = seg[:, pl.ds(pl.multiple_of(s * block, block), block)].astype(F32)
+    winr[:, REACH + block :] = jnp.where(has_right, after, -1.0)
+    for r in range(2):
+        for t in range(8):
+            row = winr[r : r + 1, t * 128 : t * 128 + 128]
+            wcol[r, t * 128 : t * 128 + 128] = jnp.broadcast_to(row, (128, 128)).T
+
+
+def fill_masks(winr, wcol, bias, same):
     kk = lax.broadcasted_iota(jnp.int32, (256, 128), 0)
     ii = lax.broadcasted_iota(jnp.int32, (256, 128), 1)
-    seg_k = winc[r, 192 + 128 * b : 448 + 128 * b, :]
-    near = (jnp.abs(kk - NEAR - ii) <= NEAR) & (seg_k == seg_q)
     pp = lax.broadcasted_iota(jnp.int32, (160, 128), 0)
     qi = lax.broadcasted_iota(jnp.int32, (160, 128), 1)
-    seg_p = win4[r, 32 * b : 32 * b + 160, 0:1]
-    far = (jnp.abs(4 * pp - REACH - qi) <= REACH) & (seg_p == seg_q)
-    return jnp.where(near, 0.0, -1e30), jnp.where(far, 0.0, -1e30)
-
-
-def fill_masks(winc, win4, winr, bias):
+    close = jnp.abs(kk - NEAR - ii) <= NEAR
+    reach = jnp.abs(4 * pp - REACH - qi) <= REACH
     for r in range(2):
         for b in range(4):
-            near, far = mask_block(winc, win4, winr, r, b)
-            bias[r * 4 + b, 0:256] = near
-            bias[r * 4 + b, 256:416] = far
+            seg_q = winr[r : r + 1, 256 + 128 * b : 384 + 128 * b]
+            near = close & (wcol[r, 192 + 128 * b : 448 + 128 * b] == seg_q)
+            far = reach & (wcol[r, pl.ds(128 * b, 160, stride=4), :] == seg_q)
+            bias[r * 4 + b, 0:256] = jnp.where(near, 0.0, -1e30)
+            bias[r * 4 + b, 256:416] = jnp.where(far, 0.0, -1e30)
+        anchor = wcol[r, pl.ds(REACH, 128, stride=4), :]
+        for t in range(5):
+            hit = wcol[r, pl.ds(REACH - 2 + t, 128, stride=4), :] == anchor
+            same[r, t] = jnp.where(hit, 1.0, 0.0).astype(BF)
 
 
 def head_lanes(h):
@@ -176,6 +190,9 @@
     return cen * rs, rs
 
 
+LAST = 29
+
+
 def pack_own(grab, put):
     for name in ("qkv", "out", "up", "down"):
         half = units(name) // 2
@@ -236,9 +253,9 @@
 
 
 def front_kernel(
-    tok, winc, win4, winr, wq, wo, wu, wd, small,
-    o_wq, o_wo, o_wu, o_wd, o_taps, o_gains, o_h1, o_q, o_kv, o_pe, o_att, o_bias, o_lse,
-    G, Wq, Wo, Wu, Wd, taps, gains, xe, h1, q, kv, pe, att, bias, lse, chunk,
+    tok, seg, wq, wo, wu, wd, small,
+    o_wq, o_wo, o_wu, o_wd, o_taps, o_gains, o_h1, o_q, o_kv, o_pe, o_att, o_bias, o_lse, o_same,
+    G, Wq, Wo, Wu, Wd, taps, gains, xe, h1, q, kv, pe, att, bias, lse, same, chunk, winr, wcol,
     send_x, send_y, send_d, send_z, send_g, recv, hsend, hrecv, local,
 ):
     me = where_am_i()
@@ -359,6 +376,7 @@
         def _():
             make(r, False).wait_recv()
 
+    expected = greet(me)
     load = [pltpu.make_async_copy(tok.at[r], xe.at[r, pl.ds(64, 512)], local.at[r]) for r in range(2)]
     for copy in load:
         copy.start()
@@ -386,13 +404,14 @@
             pe[r, 192:256] = jnp.zeros((64, 1536), BF)
 
     lse[...] = jnp.zeros((12, 8, 256), F32)
-    greet(me, True)
+    all_here(expected)
     own(0)
     for r in range(2):
         both(halo_tok, r, lambda copy, right: copy.start())
     own(1)
     own(2)
-    fill_masks(winc, win4, winr, bias)
+    fill_window(seg, winr, wcol, has_left, has_right, s)
+    fill_masks(winr, wcol, bias, same)
     for j in (1, 2, 3):
         column(0, j)
     for j in range(4):
@@ -417,10 +436,10 @@
         pltpu.make_async_copy(a, b, local.at[2 + i])
         for i, (a, b) in enumerate(
             [(Wq, o_wq), (taps, o_taps), (gains, o_gains), (h1, o_h1), (q, o_q), (kv, o_kv), (pe, o_pe),
-             (att, o_att), (bias, o_bias), (Wo, o_wo), (Wu, o_wu), (Wd, o_wd), (lse, o_lse)]
+             (att, o_att), (bias, o_bias), (Wo, o_wo), (Wu, o_wu), (Wd, o_wd), (lse, o_lse), (same, o_same)]
         )
     ]
-    for i in (0, 1, 2, 8):
+    for i in (0, 1, 2, 8, 13):
         outs[i].start()
     for copy in load:
         copy.wait()
@@ -445,12 +464,6 @@
             return carry
 
         lax.fori_loop(0, 3, queries, 0)
-        anchor = win4[r, 64:192, 0:1]
-        same = [
-            (win4[r, a : a + 128, f : f + 1] == anchor).astype(F32)
-            for a, f in ((63, 2), (63, 3), (64, 0), (64, 1), (64, 2))
-        ]
-
         def keys(j, carry):
             event(r * 6 + j)
             lanes = pl.ds(pl.multiple_of(j * 128, 128), 128)
@@ -464,7 +477,7 @@
                 hl = pl.ds(pl.multiple_of(j * 256 + half * 128, 128), 128)
                 acc = jnp.zeros((128, 128), F32)
                 for t in range(5):
-                    acc = acc + taps[t : t + 1, hl] * chunk[half, pl.ds(62 + t, 128, stride=4), :] * same[t]
+                    acc = acc + taps[t : t + 1, hl] * chunk[half, pl.ds(62 + t, 128, stride=4), :] * same[r, t].astype(F32)
                 pe[r, 64:192, hl] = acc.astype(BF)
             return carry
 
@@ -479,11 +492,11 @@
             attend(q, kv, pe, bias, att, lse, r, h)
             base = 12 + (r * 6 + h) * 2
 
-            @pl.when(base < 33)
+            @pl.when(base < LAST)
             def _():
                 event(base)
 
-            @pl.when(base + 1 < 33)
+            @pl.when(base + 1 < LAST)
             def _():
                 event(base + 1)
 
@@ -493,11 +506,16 @@
     outs[6].start()
     outs[7].start()
     outs[12].start()
-    for k in (1, 2, 3):
+    for k in (1, 2):
         other(k)
-    for i, (name, dst) in enumerate((("out", Wo), ("up", Wu), ("down", Wd))):
-        unpack(name, G, dst)
+    finish = (("out", Wo), ("up", Wu), ("down", Wd))
+    for i in range(2):
+        unpack(finish[i][0], G, finish[i][1])
         outs[9 + i].start()
+    lax.fori_loop(LAST, 33, lambda e, carry: (event(e), carry)[1], 0)
+    other(3)
+    unpack("down", G, Wd)
+    outs[11].start()
     for r in range(2):
         both(halo_tok, r, lambda copy, right: copy.wait_send())
         both(halo_pool, r, lambda copy, right: copy.wait_send())
@@ -517,36 +535,30 @@
         copy.wait()
 
 
-def front(tok, winc, win4, winr, wq, wo, wu, wd, small):
+def front(tok, seg, wq, wo, wu, wd, small):
     sds = jax.ShapeDtypeStruct
     shapes = [
         ((768, 2304), BF), ((768, 768), BF), ((768, 3072), BF), ((768, 3072), BF),
         ((16, 1536), F32), ((16, 768), F32),
         ((2, 640, 768), BF), ((2, 512, 768), BF), ((2, 640, 1536), BF), ((2, 256, 1536), BF),
         ((2, 512, 768), BF), ((8, 416, 128), F32), ((12, 8, 256), F32),
+        ((2, 5, 128, 128), BF),
     ]
     scratch = [pltpu.VMEM((4, 32, 16, WIDE), BF)]
     scratch += [pltpu.VMEM(sh, dt) for sh, dt in shapes[:6]]
     scratch += [pltpu.VMEM((2, 640, 768), BF)]
     scratch += [pltpu.VMEM(sh, dt) for sh, dt in shapes[6:]]
-    scratch += [pltpu.VMEM((2, 640, 128), F32)]
+    scratch += [pltpu.VMEM((2, 640, 128), F32), pltpu.VMEM((2, 1024), F32), pltpu.VMEM((2, 1024, 128), F32)]
     dma = pltpu.SemaphoreType.DMA
-    scratch += [dma((4, 16)), dma((4, 16)), dma((4, 16)), dma((4, 3)), dma((4, 4)), dma((4, 32)), dma((8,)), dma((8,)), dma((15,))]
+    scratch += [dma((4, 16)), dma((4, 16)), dma((4, 16)), dma((4, 3)), dma((4, 4)), dma((4, 32)), dma((8,)), dma((8,)), dma((16,))]
     return pl.pallas_call(
         front_kernel,
         out_shape=[sds(sh, dt) for sh, dt in shapes],
-        in_specs=[ANY] + [VM] * 8,
+        in_specs=[ANY] + [VM] * 6,
         out_specs=[ANY] * len(shapes),
         scratch_shapes=scratch,
         compiler_params=pltpu.CompilerParams(collective_id=0, has_side_effects=True, vmem_limit_bytes=VMEM_LIMIT),
-    )(tok, winc, win4, winr, wq, wo, wu, wd, small)
-
-
-def windows(segments):
-    block = 512
-    padded = jnp.pad(segments, ((0, 0), (REACH, REACH)), constant_values=-1)
-    win = lax.dynamic_slice_in_dim(padded, lax.axis_index("seq") * block, block + 2 * REACH, 1)
-    return win[:, :, None], win.reshape(2, 256, 4), win
+    )(tok, seg, wq, wo, wu, wd, small)
 
 
 def small_share(pool_taps, ln1_gain, ln1_bias, ln2_gain, ln2_bias):
@@ -587,12 +599,13 @@
 
 def back_kernel(
     tok_in, att_in, dy_in, wo_in, wu_in, wd_in,
-    q_in, kv_in, pe_in, bias_in, h1_in, wq_in, taps, gains, win4, lse,
+    q_in, kv_in, pe_in, bias_in, h1_in, wq_in, taps, gains, same, lse,
     o_out, o_gmid, o_in, o_wq, o_wo, o_wu, o_wd, o_small,
     Sf, So, Ss, Rf, Ro, Rq, Rs, gatt, pstage, precv, hstage, hrecv, tg, lg,
     send, recv, psend, prsem, local,
 ):
     me = where_am_i()
+    greet_all(me)
     c, s, z, col = me["c"], me["s"], me["z"], me["col"]
     has_left, has_right = s > 0, s < lax.axis_size("seq") - 1
 
@@ -777,7 +790,6 @@
 
     tg[...] = jnp.zeros((16, 1536), F32)
     lg[...] = jnp.zeros((16, 768), F32)
-    greet_all(me)
 
     def perform(todo):
         for fn, k in todo:
@@ -834,6 +846,8 @@
             5: [(begin, 0)], 7: [(do_g, 0)], 11: [(do_p, 0), (begin, 1)], 13: [(do_g, 1)],
             17: [(do_c, 0), (begin, 2)],
         }
+
+        all_here(16)
 
         def chunk(j, carry):
             lanes = [pl.ds(pl.multiple_of(j * 512 + h * 256, 256), 256) for h in range(2)]
@@ -914,35 +928,42 @@
             Sq[j, i, :, 768:1152] = pack_pair(tail[:, 0:384], tail[:, 384:768])
         begin(4 + j)
 
-    def attention(gext, h1, h1t, Sq, q, kv, pe, bias, dkv, dpe, chunk):
-        loads = [
-            copy(4 + i, a, b)
-            for i, (a, b) in enumerate([(q_in, q), (kv_in, kv), (pe_in, pe), (bias_in, bias), (h1_in, h1)])
-        ]
-        for ld in loads:
-            ld.start()
-        for r in range(2):
-            gext[r * 640 : r * 640 + 64, 0:768] = jnp.zeros((64, 768), BF)
-            gext[r * 640 + 576 : r * 640 + 640, 0:768] = jnp.zeros((64, 768), BF)
-        for ld in loads[:4]:
-            ld.wait()
-        plans = (
-            {0: [(do_c, 1)], 2: [(do_p, 2)], 3: [(do_g, 3)], 5: [(do_p, 3)]},
-            {2: [(do_c, 2)], 3: [(do_c, 3)]},
-        )
-        for r in range(2):
-            def heads(h, carry):
-                attend_back(q, kv, pe, bias, lse, gatt, gext, dkv, dpe, r, h)
-                for part in range(2):
-                    pstage[r, 0, h, part] = dpe[r, part * 6 + h, 0:64].astype(BF)
-                    pstage[r, 1, h, part] = dpe[r, part * 6 + h, 192:256].astype(BF)
-                both(pstage, precv, r, h, lambda cp: cp.start())
-                run(plans[r], h)
-                return carry
-
-            lax.fori_loop(0, 6, heads, 0)
-
-        loads[4].wait()
+    def attention(gext, h1, h1t, Sq, kv, dkv, dpe, chunk):
+        late_load = copy(8, h1_in, h1)
+        late_load.start()
+
+        def scores(q, pe, bias):
+            loads = [
+                copy(4 + i, a, b)
+                for i, (a, b) in enumerate([(q_in, q), (kv_in, kv), (pe_in, pe), (bias_in, bias)])
+            ]
+            for ld in loads:
+                ld.start()
+            for r in range(2):
+                gext[r * 640 : r * 640 + 64, 0:768] = jnp.zeros((64, 768), BF)
+                gext[r * 640 + 576 : r * 640 + 640, 0:768] = jnp.zeros((64, 768), BF)
+            for ld in loads:
+                ld.wait()
+            plans = (
+                {0: [(do_c, 1)], 2: [(do_p, 2)], 3: [(do_g, 3)], 5: [(do_p, 3)]},
+                {2: [(do_c, 2)], 3: [(do_c, 3)]},
+            )
+            for r in range(2):
+                def heads(h, carry):
+                    attend_back(q, kv, pe, bias, lse, gatt, gext, dkv, dpe, r, h)
+                    for part in range(2):
+                        pstage[r, 0, h, part] = dpe[r, part * 6 + h, 0:64].astype(BF)
+                        pstage[r, 1, h, part] = dpe[r, part * 6 + h, 192:256].astype(BF)
+                    both(pstage, precv, r, h, lambda cp: cp.start())
+                    run(plans[r], h)
+                    return carry
+
+                lax.fori_loop(0, 6, heads, 0)
+
+        pl.run_scoped(
+            scores, vm((2, 512, 768), BF), vm((2, 256, 1536), BF), vm((8, 416, 128), F32)
+        )
+        late_load.wait()
         for r in range(2):
             def flip(i, carry):
                 rows = pl.ds(pl.multiple_of(i * 128, 128), 128)
@@ -953,36 +974,30 @@
 
             lax.fori_loop(0, 5, flip, 0)
         weight_grad(gext, h1t, Sq, 0)
-        for r in range(2):
-            anchor = win4[r, 64:192, 0:1]
-            same = [
-                (win4[r, a : a + 128, f : f + 1] == anchor).astype(F32)
-                for a, f in ((63, 2), (63, 3), (64, 0), (64, 1), (64, 2))
-            ]
-
-            def pool_back(t, carry):
-                lanes = pl.ds(pl.multiple_of(t * 128, 128), 128)
-                h, part = lax.rem(t, 6), t // 6
-
-                @pl.when(t < 6)
-                def _():
-                    arrived(pstage, precv, r, h)
-
-                low = dpe[r, t, 64:128] + precv[r, 1, h, part].astype(F32)
-                high = dpe[r, t, 128:192] + precv[r, 0, h, part].astype(F32)
-                gp = jnp.concatenate([low, high], axis=0)
-                chunk[...] = kv[r, :, lanes].astype(F32)
-                for i in range(5):
-                    at = pl.ds(62 + i, 128, stride=4)
-                    gm = gp * same[i]
-                    tg[i : i + 1, lanes] += jnp.sum(gm * chunk[at, :], axis=0, keepdims=True)
-                    dkv[r, t, at, :] += gm * taps[i : i + 1, lanes]
-                out_lanes = pl.ds(pl.multiple_of(768 + t * 128, 128), 128)
-                gext[r * 640 : r * 640 + 640, out_lanes] = dkv[r, t].astype(BF)
-                return carry
-
-            lax.fori_loop(0, 12, pool_back, 0)
-        perform([(do_g, 4)])
+        for part in range(2):
+            for r in range(2):
+                def pool_back(h, carry):
+                    t = part * 6 + h
+                    lanes = pl.ds(pl.multiple_of(t * 128, 128), 128)
+                    if part == 0:
+                        arrived(pstage, precv, r, h)
+
+                    low = dpe[r, t, 64:128] + precv[r, 1, h, part].astype(F32)
+                    high = dpe[r, t, 128:192] + precv[r, 0, h, part].astype(F32)
+                    gp = jnp.concatenate([low, high], axis=0)
+                    chunk[...] = kv[r, :, lanes].astype(F32)
+                    for i in range(5):
+                        at = pl.ds(62 + i, 128, stride=4)
+                        gm = gp * same[r, i].astype(F32)
+                        tg[i : i + 1, lanes] += jnp.sum(gm * chunk[at, :], axis=0, keepdims=True)
+                        dkv[r, t, at, :] += gm * taps[i : i + 1, lanes]
+                    out_lanes = pl.ds(pl.multiple_of(768 + t * 128, 128), 128)
+                    gext[r * 640 : r * 640 + 640, out_lanes] = dkv[r, t].astype(BF)
+                    return carry
+
+                lax.fori_loop(0, 6, pool_back, 0)
+            weight_grad(gext, h1t, Sq, 1 + part)
+            perform([(do_g, 4 + part)])
 
     def projection(gext, h1t, Sq, wq, tok, gmid, gh):
         loads = [
@@ -990,9 +1005,7 @@
         ]
         for ld in loads:
             ld.start()
-        weight_grad(gext, h1t, Sq, 1)
-        weight_grad(gext, h1t, Sq, 2)
-        perform([(do_p, 4), (do_g, 5)])
+        perform([(do_p, 4)])
         for ld in loads:
             ld.wait()
         for r in range(2):
@@ -1053,8 +1066,7 @@
         late.append(Sq)
         pl.run_scoped(
             functools.partial(attention, gext, h1, h1t, Sq),
-            vm((2, 512, 768), BF), vm((2, 640, 1536), BF), vm((2, 256, 1536), BF), vm((8, 416, 128), F32),
-            vm((2, 12, 640, 128), F32), vm((2, 12, 256, 128), F32), vm((640, 128), F32),
+            vm((2, 640, 1536), BF), vm((2, 12, 640, 128), F32), vm((2, 12, 256, 128), F32), vm((640, 128), F32),
         )
         pl.run_scoped(
             functools.partial(projection, gext, h1t, Sq),
@@ -1403,15 +1415,14 @@
 def chained(
     tokens, segments, cotangent, ln1_gain, ln1_bias, w_qkv, pool_taps, w_out, ln2_gain, ln2_bias, w_up, w_down,
 ):
-    winc, win4, winr = windows(segments)
     small = small_share(pool_taps, ln1_gain, ln1_bias, ln2_gain, ln2_bias)
-    wq, wo, wu, wd, taps, gains, h1, q, kv, pe, att, bias, lse = front(
-        tokens, winc, win4, winr, w_qkv, w_out, w_up, w_down.T, small
+    wq, wo, wu, wd, taps, gains, h1, q, kv, pe, att, bias, lse, same = front(
+        tokens, segments, w_qkv, w_out, w_up, w_down.T, small
     )
     flat, split = (1024, 768), (2, 512, 768)
     out, _, g_in, g_wq, g_wo, g_wu, g_wd, g_small = back_part(
         tokens.reshape(flat), att.reshape(flat), cotangent.reshape(flat), wo, wu, wd,
-        q, kv, pe, bias, h1, wq, taps, gains, win4, lse,
+        q, kv, pe, bias, h1, wq, taps, gains, same, lse,
     )
     return (
         out.reshape(split), g_in.reshape(split), g_small[5, :24], g_small[6, :24], g_wq, g_small[0:5, :48], g_wo,

time: 264 us -> 256 us (0.970)
  local copies, waits for them, and re-layouts: 13.5 us -> 9.72 us
  Pallas kernels: 247 us -> 244 us
    unnamed x18 -> x16, local copies, waits for them, and re-layouts: 7.09 us -> 7.08 us
where the time goes in v4:
time: 256 us
  Pallas kernels  244 us (95%)
  local copies, waits for them, and re-layouts  9.72 us (4%)
    pallas_call x1, Pallas kernels, back_part(): pl.pallas_call(back_kernel, out_shape=[sds((1024, 768), BF), sds((1024, 7...  145 us
    pallas_call x1, Pallas kernels, front(): pl.pallas_call(front_kernel, out_shape=[sds(sh, dt) for sh, dt in shapes]...  98.7 us
    unnamed x16, local copies, waits for them, and re-layouts  7.08 us

profile of v4, /device:TPU:0, one launch (start us, length us, event | category | flops | bytes accessed | tf_op | source)
XLA Modules:
  0.0 256.1 jit_solution(8224458115542494328)
XLA Ops:
  0.6 0.7 fusion.10
  1.4 1.3 fusion.6.small
  2.6 98.7 %shard_map.203 = (bf16[768,2304]{1,0:T(8,128)(2,1)}, bf16[768,768]{1,0:T(8,128)(2,1)}, bf16[768,3072]{1,0:T(8,128)(2,1)}, bf16[768,3072]{1,0:T(8,128)(2,1)}, f32...) custom-call(bf16[2,512,768]{2,1,0:T(8,128)(2,1)} %tok.1, ...), custom_call_target="tpu_custom_call" | custom-call | tf_op jit(solution)/shard_map/pallas_call | solution.py:554
  101.4 144.9 %shard_map.204 = (bf16[1024,768]{1,0:T(8,128)(2,1)}, f32[1024,768]{1,0:T(8,128)}, f32[1024,768]{1,0:T(8,128)}, f32[24,2304]{1,0:T(8,128)}, f32[24,768]{1,0:T(8,1...) custom-call(bf16[1024,768]{1,0:T(8,128)(2,1)} %bitcast.19, bf16[1024,768]{1,0:T(8,128)(2,1)} %bitcast.22, ...), custom_call_target="tpu_custom_call" | custom-call | tf_op jit(solution)/shard_map/pallas_call | solution.py:1088
  246.3 0.0 copy-start
  246.3 1.4 slice_bitcast_fusion
  247.7 1.3 slice.17
  249.0 2.7 %copy.29 = bf16[2,512,768]{2,1,0:T(8,128)(2,1)} copy(bf16[2,512,768]{2,1,0:T(8,128)(2,1)} %bitcast.23) | data formatting | bytes 3145728
  251.6 0.0 copy-done
  251.6 0.0 copy-start.3
  251.6 0.0 copy-start.4
  251.6 0.0 copy-start.2
  251.6 0.0 copy-start.1
  251.6 1.7 copy.30
  253.3 0.0 copy-done.3
  253.3 0.7 copy.31
  254.0 0.0 copy-done.4
  254.0 0.6 copy.32
  254.6 0.0 copy-done.2
  254.6 0.7 copy.33
  255.3 0.0 copy-done.1
  255.3 0.7 copy.34
Async XLA Ops:
  246.3 5.3 %copy-start = (f32[1024,768]{1,0:T(8,128)S(1)}, f32[1024,768]{1,0:T(8,128)}, u32[]{:S(2)}) copy-start(f32[1024,768]{1,0:T(8,128)} %get-tuple-element.47) | copy-start | bytes 9437188
  251.6 1.7 copy-start.3
  251.6 2.4 copy-start.4
  251.6 3.0 %copy-start.2 = (f32[24,3072]{1,0:T(8,128)S(1)}, f32[24,3072]{1,0:T(8,128)}, u32[]{:S(2)}) copy-start(f32[24,3072]{1,0:T(8,128)} %get-tuple-element.77) | copy-start | bytes 884740
  251.6 3.7 %copy-start.1 = (f32[24,3072]{1,0:T(8,128)S(1)}, f32[24,3072]{1,0:T(8,128)}, u32[]{:S(2)}) copy-start(f32[24,3072]{1,0:T(8,128)} %get-tuple-element.52) | copy-start | bytes 884740

commit v5 on v4

--- a/solution.py
+++ b/solution.py
@@ -158,7 +158,7 @@
         att[r, i, kl] = pair_out(dg(values, low, TN)).astype(BF)
 
 
-def attend_back(q, kv, pe, bias, lse, g, gext, dkv, dpe, r, h):
+def attend_back(q, kv, pe, bias, lse, delta, g, gext, dkv, dpe, r, h):
     kl, vl = head_lanes(h)
     for part in (h, 6 + h):
         dkv[r, part] = jnp.zeros((640, 128), F32)
@@ -170,8 +170,8 @@
         st = jnp.concatenate([dg(kn, q2, NT), dg(kf, q2, NT)], axis=0) - lse[r * 6 + h, b : b + 1]
         p = jnp.exp(st + jnp.concatenate([bias[r * 4 + b], bias[r * 4 + b]], axis=1))
         dp = jnp.concatenate([dg(vn, g2, NT), dg(vf, g2, NT)], axis=0)
-        delta = jnp.sum(p * dp, axis=0, keepdims=True)
-        ds = (p * (dp - delta)).astype(BF)
+        at = slice(r * 512 + b * 128, r * 512 + b * 128 + 128)
+        ds = (p * (dp - jnp.concatenate([delta[h, 0:1, at], delta[h, 1:2, at]], axis=1))).astype(BF)
         low = p.astype(BF)
         dv, dk = dg(low, g2, NN), dg(ds, q2, NN)
         dkv[r, h, n] += dk[:256]
@@ -601,7 +601,7 @@
     tok_in, att_in, dy_in, wo_in, wu_in, wd_in,
     q_in, kv_in, pe_in, bias_in, h1_in, wq_in, taps, gains, same, lse,
     o_out, o_gmid, o_in, o_wq, o_wo, o_wu, o_wd, o_small,
-    Sf, So, Ss, Rf, Ro, Rq, Rs, gatt, pstage, precv, hstage, hrecv, tg, lg,
+    Sf, So, Ss, Rf, Ro, Rq, Rs, gatt, delta, pstage, precv, hstage, hrecv, tg, lg,
     send, recv, psend, prsem, local,
 ):
     me = where_am_i()
@@ -642,7 +642,7 @@
 
     def step_g(k, zz):
         S, R = cls(k)
-        to = me["px"] if zz % 2 == 0 else me["py"]
+        to = me["px"] if zz == 0 else me["py"]
         return remote(k, S.at[zz * 4 + me["cold"]], R.at[16 + zz], 1 + zz, to)
 
     def step_x(k, zz):
@@ -677,7 +677,7 @@
 
     def do_p(k, zz):
         step_g(k, zz).wait_recv()
-        even = zz % 2 == 0
+        even = zz == 0
         for at, step, has in ((zz * 4 + me["colx"], step_x, not even), (zz * 4 + me["coly"], step_y, even)):
             cls(k)[0][at] = add(k, at, [16 + zz] if has else []).astype(BF)
             step(k, zz).start()
@@ -917,6 +917,21 @@
             So[i, :, 768:1152] = pack_pair(tail[:, 0:384], tail[:, 384:768])
         begin(3)
         perform([(do_g, 2)])
+
+        def products(i, carry):
+            rows = pl.ds(pl.multiple_of(i * 128, 128), 128)
+            v = gatt[rows].astype(F32) * Att[rows].astype(F32)
+            high = v.astype(BF)
+            Dy[rows] = high
+            Att[rows] = (v - high.astype(F32)).astype(BF)
+            return carry
+
+        lax.fori_loop(0, 8, products, 0)
+        head = lax.broadcasted_iota(jnp.int32, (16, 768), 1) // HEAD
+        pick = jnp.where(head == lax.broadcasted_iota(jnp.int32, (16, 768), 0), 1.0, 0.0).astype(BF)
+        sums = dg(pick, Dy[...], NT) + dg(pick, Att[...], NT)
+        for h in range(6):
+            delta[h, 0:2] = sums[2 * h : 2 * h + 2]
         for st in store:
             st.wait()
 
@@ -950,7 +965,7 @@
             )
             for r in range(2):
                 def heads(h, carry):
-                    attend_back(q, kv, pe, bias, lse, gatt, gext, dkv, dpe, r, h)
+                    attend_back(q, kv, pe, bias, lse, delta, gatt, gext, dkv, dpe, r, h)
                     for part in range(2):
                         pstage[r, 0, h, part] = dpe[r, part * 6 + h, 0:64].astype(BF)
                         pstage[r, 1, h, part] = dpe[r, part * 6 + h, 192:256].astype(BF)
@@ -1096,7 +1111,7 @@
         scratch_shapes=[
             vm((3, 32, 16, 3072), BF), vm((32, 16, 1152), BF), vm((32, 16, 128), BF),
             vm((3, 31, 16, 3072), BF), vm((31, 16, 1152), BF), vm((3, 31, 16, 1152), BF), vm((32, 16, 128), BF),
-            vm((1024, 768), BF),
+            vm((1024, 768), BF), vm((6, 8, 1024), F32),
             vm((2, 2, 6, 2, 64, 128), BF), vm((2, 2, 6, 2, 64, 128), BF), vm((2, 2, 64, 768), BF), vm((2, 2, 64, 768), BF),
             vm((16, 1536), F32), vm((16, 768), F32),
             dma((8, 16)), dma((8, 16)), dma((28,)), dma((28,)), dma((14,)),

time: 256 us -> 254 us (level)
  no operation moved by 1% of the time
where the time goes in v5:
time: 254 us
  Pallas kernels  242 us (95%)
  local copies, waits for them, and re-layouts  9.72 us (4%)
    pallas_call x1, Pallas kernels, back_part(): pl.pallas_call(back_kernel, out_shape=[sds((1024, 768), BF), sds((1024, 7...  143 us
    pallas_call x1, Pallas kernels, front(): pl.pallas_call(front_kernel, out_shape=[sds(sh, dt) for sh, dt in shapes]...  98.7 us
    unnamed x16, local copies, waits for them, and re-layouts  7.08 us

profile of v5, /device:TPU:0, one launch (start us, length us, event | category | flops | bytes accessed | tf_op | source)
XLA Modules:
  0.0 253.9 jit_solution(17477234580043249497)
XLA Ops:
  0.6 0.7 fusion.10
  1.4 1.3 fusion.6.small
  2.6 98.7 %shard_map.203 = (bf16[768,2304]{1,0:T(8,128)(2,1)}, bf16[768,768]{1,0:T(8,128)(2,1)}, bf16[768,3072]{1,0:T(8,128)(2,1)}, bf16[768,3072]{1,0:T(8,128)(2,1)}, f32...) custom-call(bf16[2,512,768]{2,1,0:T(8,128)(2,1)} %tok.1, ...), custom_call_target="tpu_custom_call" | custom-call | tf_op jit(solution)/shard_map/pallas_call | solution.py:554
  101.4 142.8 %shard_map.204 = (bf16[1024,768]{1,0:T(8,128)(2,1)}, f32[1024,768]{1,0:T(8,128)}, f32[1024,768]{1,0:T(8,128)}, f32[24,2304]{1,0:T(8,128)}, f32[24,768]{1,0:T(8,1...) custom-call(bf16[1024,768]{1,0:T(8,128)(2,1)} %bitcast.19, bf16[1024,768]{1,0:T(8,128)(2,1)} %bitcast.22, ...), custom_call_target="tpu_custom_call" | custom-call | tf_op jit(solution)/shard_map/pallas_call | solution.py:1103
  244.2 0.0 copy-start
  244.2 1.4 slice_bitcast_fusion
  245.6 1.3 slice.17
  246.8 2.7 %copy.29 = bf16[2,512,768]{2,1,0:T(8,128)(2,1)} copy(bf16[2,512,768]{2,1,0:T(8,128)(2,1)} %bitcast.23) | data formatting | bytes 3145728
  249.5 0.0 copy-done
  249.5 0.0 copy-start.3
  249.5 0.0 copy-start.4
  249.5 0.0 copy-start.2
  249.5 0.0 copy-start.1
  249.5 1.7 copy.30
  251.2 0.0 copy-done.3
  251.2 0.7 copy.31
  251.9 0.0 copy-done.4
  251.9 0.6 copy.32
  252.5 0.0 copy-done.2
  252.5 0.7 copy.33
  253.2 0.0 copy-done.1
  253.2 0.7 copy.34
Async XLA Ops:
  244.2 5.3 %copy-start = (f32[1024,768]{1,0:T(8,128)S(1)}, f32[1024,768]{1,0:T(8,128)}, u32[]{:S(2)}) copy-start(f32[1024,768]{1,0:T(8,128)} %get-tuple-element.47) | copy-start | bytes 9437188
  249.5 1.7 copy-start.3
  249.5 2.4 copy-start.4
  249.5 3.0 %copy-start.2 = (f32[24,3072]{1,0:T(8,128)S(1)}, f32[24,3072]{1,0:T(8,128)}, u32[]{:S(2)}) copy-start(f32[24,3072]{1,0:T(8,128)} %get-tuple-element.77) | copy-start | bytes 884740
  249.5 3.7 %copy-start.1 = (f32[24,3072]{1,0:T(8,128)S(1)}, f32[24,3072]{1,0:T(8,128)}, u32[]{:S(2)}) copy-start(f32[24,3072]{1,0:T(8,128)} %get-tuple-element.52) | copy-start | bytes 884740

commit v6 on v5

--- a/solution.py
+++ b/solution.py
@@ -961,7 +961,7 @@
                 ld.wait()
             plans = (
                 {0: [(do_c, 1)], 2: [(do_p, 2)], 3: [(do_g, 3)], 5: [(do_p, 3)]},
-                {2: [(do_c, 2)], 3: [(do_c, 3)]},
+                {0: [(finish, 0)], 2: [(do_c, 2)], 3: [(do_c, 3)], 4: [(finish, 1)]},
             )
             for r in range(2):
                 def heads(h, carry):
@@ -1062,9 +1062,9 @@
 
         pick_small(tg, lg, put)
         begin(7)
-        perform([(do_c, 5), (finish, 0)])
+        perform([(do_c, 5)])
         small_out()
-        perform([(finish, 1), (finish, 2), (finish, 3), (do_c, 6), (finish, 4), (finish, 5)])
+        perform([(finish, 2), (finish, 3), (do_c, 6), (finish, 4), (finish, 5)])
         small_in()
         perform([(finish, 6)])
         out.wait()

time: 254 us -> 255 us (level)
  no operation moved by 1% of the time
where the time goes in v6:
time: 255 us; the launch traced here: 254 us
  Pallas kernels  242 us (95%)
  local copies, waits for them, and re-layouts  9.72 us (4%)
    pallas_call x1, Pallas kernels, back_part(): pl.pallas_call(back_kernel, out_shape=[sds((1024, 768), BF), sds((1024, 7...  143 us
    pallas_call x1, Pallas kernels, front(): pl.pallas_call(front_kernel, out_shape=[sds(sh, dt) for sh, dt in shapes]...  98.7 us
    unnamed x16, local copies, waits for them, and re-layouts  7.08 us

profile of v6, /device:TPU:0, one launch (start us, length us, event | category | flops | bytes accessed | tf_op | source)
XLA Modules:
  0.0 254.2 jit_solution(8792637339134356676)
XLA Ops:
  0.6 0.7 fusion.10
  1.4 1.3 fusion.6.small
  2.6 98.7 %shard_map.203 = (bf16[768,2304]{1,0:T(8,128)(2,1)}, bf16[768,768]{1,0:T(8,128)(2,1)}, bf16[768,3072]{1,0:T(8,128)(2,1)}, bf16[768,3072]{1,0:T(8,128)(2,1)}, f32...) custom-call(bf16[2,512,768]{2,1,0:T(8,128)(2,1)} %tok.1, ...), custom_call_target="tpu_custom_call" | custom-call | tf_op jit(solution)/shard_map/pallas_call | solution.py:554
  101.4 143.1 %shard_map.204 = (bf16[1024,768]{1,0:T(8,128)(2,1)}, f32[1024,768]{1,0:T(8,128)}, f32[1024,768]{1,0:T(8,128)}, f32[24,2304]{1,0:T(8,128)}, f32[24,768]{1,0:T(8,1...) custom-call(bf16[1024,768]{1,0:T(8,128)(2,1)} %bitcast.19, bf16[1024,768]{1,0:T(8,128)(2,1)} %bitcast.22, ...), custom_call_target="tpu_custom_call" | custom-call | tf_op jit(solution)/shard_map/pallas_call | solution.py:1103
  244.5 0.0 copy-start
  244.5 1.4 slice_bitcast_fusion
  245.9 1.3 slice.17
  247.1 2.7 %copy.29 = bf16[2,512,768]{2,1,0:T(8,128)(2,1)} copy(bf16[2,512,768]{2,1,0:T(8,128)(2,1)} %bitcast.23) | data formatting | bytes 3145728
  249.8 0.0 copy-done
  249.8 0.0 copy-start.3
  249.8 0.0 copy-start.4
  249.8 0.0 copy-start.2
  249.8 0.0 copy-start.1
  249.8 1.7 copy.30
  251.5 0.0 copy-done.3
  251.5 0.7 copy.31
  252.2 0.0 copy-done.4
  252.2 0.6 copy.32
  252.8 0.0 copy-done.2
  252.8 0.7 copy.33
  253.5 0.0 copy-done.1
  253.5 0.7 copy.34
Async XLA Ops:
  244.5 5.3 %copy-start = (f32[1024,768]{1,0:T(8,128)S(1)}, f32[1024,768]{1,0:T(8,128)}, u32[]{:S(2)}) copy-start(f32[1024,768]{1,0:T(8,128)} %get-tuple-element.47) | copy-start | bytes 9437188
  249.8 1.7 copy-start.3
  249.8 2.4 copy-start.4
  249.8 3.0 %copy-start.2 = (f32[24,3072]{1,0:T(8,128)S(1)}, f32[24,3072]{1,0:T(8,128)}, u32[]{:S(2)}) copy-start(f32[24,3072]{1,0:T(8,128)} %get-tuple-element.77) | copy-start | bytes 884740
  249.8 3.7 %copy-start.1 = (f32[24,3072]{1,0:T(8,128)S(1)}, f32[24,3072]{1,0:T(8,128)}, u32[]{:S(2)}) copy-start(f32[24,3072]{1,0:T(8,128)} %get-tuple-element.52) | copy-start | bytes 884740
